TPU v7x, 32 devices: a whole 2x2x4 slice. The times are simulated.
32 devices in a mesh: seq: 8 (over y, x, core), head: 4 (over z).
Axes of the slice: x: 2, y: 2, z: 4, core: 2. Of those that a mesh axis runs over, the one named last changes fastest.
Arguments:
- input_embeddings: bfloat16 [2048, 1024], P('seq'), may hold values from -6 to 6
- loss_adjoint: bfloat16 [2048, 1024], P('seq'), may hold values from -6 to 6
- earliest_tier_content: bfloat16 [2048, 1024], P('seq', 'head'), may hold values from -6 to 6
- opening_memory: float32 [2, 16, 64, 64], P(None, 'head'), may hold values from -4 to 4
- live_extents: int32 [2], replicated, may hold values from 513 to 1024, as said below
- lagged_blend_coeffs: float32 [7, 1024], replicated, may hold values from 0 to 1
- standardize_scales: float32 [2, 1024], replicated, may hold values from 0.25 to 1.75
- standardize_offsets: float32 [2, 1024], replicated, may hold values from -2 to 2
- adapter_narrowing_coeffs: float32 [1024, 288], replicated, may hold values from -0.1875 to 0.1875
- adapter_widening_coeffs: float32 [288, 1024], P(None, 'head'), may hold values from -0.75 to 0.75
- attention_scale_lines: float32 [3, 1024], P(None, 'head'), may hold values from 0.25 to 1.75
- attention_offset_lines: float32 [3, 1024], P(None, 'head'), may hold values from -4 to 4
- present_reward_array: float32 [1024], P('head'), may hold values from -3 to 3
- forgetting_offset: float32 [1024], P('head'), may hold values from -9.5 to 1.25
- readin_maps: float32 [3, 1024, 1024], P(None, None, 'head'), may hold values from -0.1875 to 0.1875
- emission_coeffs: float32 [1024, 1024], P('head'), may hold values from -0.1875 to 0.1875
- feedforward_address_coeffs: float32 [1024, 4096], P(None, 'head'), may hold values from -0.1875 to 0.1875
- feedforward_content_coeffs: float32 [4096, 1024], P('head'), may hold values from -0.09375 to 0.09375
- lagged_blend_velocity: float32 [7, 1024], replicated, may hold values from -12 to 12
- standardize_scale_velocity: float32 [2, 1024], replicated, may hold values from -30 to 30
- standardize_offset_velocity: float32 [2, 1024], replicated, may hold values from -36 to 36
- narrowing_velocity: float32 [1024, 288], replicated, may hold values from -4 to 4
- widening_velocity: float32 [288, 1024], P(None, 'head'), may hold values from -25 to 25
- attention_scale_velocity: float32 [3, 1024], P(None, 'head'), may hold values from -8 to 8
- attention_offset_velocity: float32 [3, 1024], P(None, 'head'), may hold values from -8 to 8
- reward_velocity_array: float32 [1024], P('head'), may hold values from -8 to 8
- forgetting_velocity: float32 [1024], P('head'), may hold values from -4 to 4
- readin_velocity: float32 [3, 1024, 1024], P(None, None, 'head'), may hold values from -15 to 15
- emission_velocity: float32 [1024, 1024], P('head'), may hold values from -15 to 15
- feedforward_address_velocity: float32 [1024, 4096], P(None, 'head'), may hold values from -20 to 20
- feedforward_content_velocity: float32 [4096, 1024], P('head'), may hold values from -20 to 20
Outputs:
- block_output: bfloat16 [2048, 1024], P('seq')
- tokens_grad: float32 [2048, 1024], P('seq')
- first_grad: float32 [2048, 1024], P('seq', 'head')
- state_grad: float32 [2, 16, 64, 64], P(None, 'head')
- next_shift: float32 [7, 1024], replicated
- next_gains: float32 [2, 1024], replicated
- next_biases: float32 [2, 1024], replicated
- next_down: float32 [1024, 288], replicated
- next_up: float32 [288, 1024], P(None, 'head')
- next_headgain: float32 [3, 1024], P(None, 'head')
- next_headbias: float32 [3, 1024], P(None, 'head')
- next_bonus: float32 [1024], P('head')
- next_decay: float32 [1024], P('head')
- next_project: float32 [3, 1024, 1024], P(None, 'seq', 'head')
- next_output: float32 [1024, 1024], P('head', 'seq')
- next_ffnkey: float32 [1024, 4096], P('seq', 'head')
- next_ffnvalue: float32 [4096, 1024], P('head', 'seq')
- momentum_shift: float32 [7, 1024], replicated
- momentum_gains: float32 [2, 1024], replicated
- momentum_biases: float32 [2, 1024], replicated
- momentum_down: float32 [1024, 288], replicated
- momentum_up: float32 [288, 1024], P(None, 'head')
- momentum_headgain: float32 [3, 1024], P(None, 'head')
- momentum_headbias: float32 [3, 1024], P(None, 'head')
- momentum_bonus: float32 [1024], P('head')
- momentum_decay: float32 [1024], P('head')
- momentum_project: float32 [3, 1024, 1024], P(None, None, 'head')
- momentum_output: float32 [1024, 1024], P('head')
- momentum_ffnkey: float32 [1024, 4096], P(None, 'head')
- momentum_ffnvalue: float32 [4096, 1024], P('head')
Inputs may be any that keep to these rules, and one draw needn't show every extreme that they name: `live_extents`: in every draw some sequence has all 1024 slots live.
All inputs are finite; a program needn't handle non-finite values.
Results may differ from a plain program's by a relative error of at most 0.012.
The roundings to bfloat16 on the way count: a program that leaves them out, or rounds other values in their place, can miss the bound.
Values sent between devices are 32-bit elements; how exact they have to be, the bound alone decides.
A program may use at most 256 MiB of HBM per device.

v0:
```python
import math

import jax
import jax.numpy as jnp
from jax import lax
from jax.sharding import PartitionSpec as P

EMBED_SIZE = 1024
HEAD_SIZE = 64
FF = 4096
LOWRANK_DECAY = 64
LOWRANK_RATE = 64
LOWRANK_VALUE = 32
LOWRANK_GATE = 128
BLOCK = 64
NS_STEPS = 5


HIGHEST = lax.Precision.HIGHEST
COEFF_A = 3.4445
COEFF_B = -4.775
COEFF_C = 2.0315
ORTHO_STEP_RATE = 0.5
VECTOR_RATE = 0.75
DECAY_KEEP = 0.5


def passed_along(value, axis, steps):
    count = lax.axis_size(axis)
    first, last = (max(0, -steps), min(count, count - steps))
    return lax.ppermute(value, axis, [(source, source + steps) for source in range(first, last)])


def spread(value, axis, source):
    kept = jnp.where(lax.axis_index(axis) == source, value, 0).astype(value.dtype)
    return lax.psum(kept, axis)


def layer_norm(content_lines, gain, bias):
    centered = content_lines - jnp.mean(content_lines, axis=-1, keepdims=True)
    variance = jnp.mean(centered * centered, axis=-1, keepdims=True)
    return centered * lax.rsqrt(variance + 1e-05) * gain + bias


def attention_split_layout(item):
    return item.reshape(item.shape[0], -1, HEAD_SIZE)


def product(left, right):
    return jnp.dot(left, right, preferred_element_type=jnp.float32)


def inner_rows(left, right):
    return jnp.einsum("ta,tb->ab", left, right, preferred_element_type=jnp.float32)


def outer_back(left, right):
    return jnp.einsum("ta,ba->tb", left, right, preferred_element_type=jnp.float32)


def gram_exact(item):
    return jnp.einsum(
        "ta,ba->tb", item, item, precision=HIGHEST, preferred_element_type=jnp.float32
    )


def apply_map(carried_memory, matrix):
    return jnp.einsum("...hrm,...hmk->...hrk", carried_memory, matrix, precision=HIGHEST)


def neighbour_row(row, offset):
    return passed_along(row, "seq", offset)


def from_before(row, is_first, stride):
    return jnp.where(is_first, 0.0, neighbour_row(row, stride))


def from_after(row, is_first, stride):
    return neighbour_row(jnp.where(is_first, 0.0, row), -stride)


def head_total(term):
    return lax.psum(term, "head")


def from_owner(part, root):
    return spread(part, "seq", root)


def block_form(carried_memory, block):
    acceptance_lines, log_decay, alpha, beta, address_lines, content_lines = block
    length = acceptance_lines.shape[0]
    total = jnp.cumsum(log_decay, axis=0)
    earlier = total - log_decay
    last = total[-1]
    grown_r = acceptance_lines * jnp.exp(total)
    grown_a = alpha * jnp.exp(earlier)
    shrunk_b = beta * jnp.exp(-total)
    shrunk_k = address_lines * jnp.exp(-total)
    row_ids = lax.broadcasted_iota(jnp.int32, (length, length), 0)
    col_ids = lax.broadcasted_iota(jnp.int32, (length, length), 1)
    strict = (row_ids > col_ids).astype(jnp.float32)
    upto = (row_ids >= col_ids).astype(jnp.float32)
    pair_ab = jnp.einsum("thn,ihn->hti", grown_a, shrunk_b, precision=HIGHEST) * strict
    pair_ak = jnp.einsum("thn,ihn->hti", grown_a, shrunk_k, precision=HIGHEST) * strict
    right = jnp.einsum("thn,hrn->htr", grown_a, carried_memory, precision=HIGHEST) + jnp.einsum(
        "hti,ihr->htr", pair_ak, content_lines, precision=HIGHEST
    )
    system = jnp.eye(length, dtype=jnp.float32) - pair_ab
    carried = jax.scipy.linalg.solve_triangular(system, right, lower=True, unit_diagonal=True)
    pair_rb = jnp.einsum("thn,ihn->hti", grown_r, shrunk_b, precision=HIGHEST) * upto
    pair_rk = jnp.einsum("thn,ihn->hti", grown_r, shrunk_k, precision=HIGHEST) * upto
    outputs = (
        jnp.einsum("thn,hrn->thr", grown_r, carried_memory, precision=HIGHEST)
        + jnp.einsum("hti,hir->thr", pair_rb, carried, precision=HIGHEST)
        + jnp.einsum("hti,ihr->thr", pair_rk, content_lines, precision=HIGHEST)
    )
    tail = jnp.exp(last[None] - total)
    new_state = (
        carried_memory * jnp.exp(last)[:, None, :]
        + jnp.einsum("hir,ihn->hrn", carried, beta * tail, precision=HIGHEST)
        + jnp.einsum("ihr,ihn->hrn", content_lines, address_lines * tail, precision=HIGHEST)
    )
    return (new_state, outputs)


def recurrence(carried_memory, residual_streams):
    overall_tally = residual_streams[0].shape[0] // BLOCK
    blocks = tuple(
        (item.reshape((overall_tally, BLOCK) + item.shape[1:]) for item in residual_streams)
    )
    carried_memory, outputs = lax.scan(block_form, carried_memory, blocks)
    return (outputs.reshape((overall_tally * BLOCK,) + outputs.shape[2:]), carried_memory)


def prepare(
    address_lines,
    content_lines,
    up_w,
    up_a,
    up_v,
    earliest_tier_content,
    attention_scale_lines,
    attention_offset_lines,
    forgetting_offset,
):
    log_decay = -jnp.exp(-jax.nn.softplus(-(forgetting_offset + up_w)) - 0.5)
    rate = jax.nn.sigmoid(attention_offset_lines[0] + up_a)
    content_lines = content_lines + (earliest_tier_content - content_lines) * jax.nn.sigmoid(
        attention_offset_lines[1] + up_v
    )
    scaled = attention_split_layout(address_lines * attention_scale_lines[0])
    unit = scaled * lax.rsqrt(jnp.sum(scaled * scaled, axis=-1, keepdims=True) + 1e-05)
    address_lines = address_lines * (1.0 + (rate - 1.0) * attention_scale_lines[1])
    return (
        attention_split_layout(log_decay),
        -unit,
        unit * attention_split_layout(rate),
        attention_split_layout(address_lines),
        attention_split_layout(content_lines),
    )


def finish_index(
    carried_memory,
    acceptance_lines,
    residual_streams,
    valve_amount,
    attention_scale_lines,
    attention_offset_lines,
    present_reward_array,
):
    log_decay, alpha, beta, address_lines, content_lines = residual_streams
    outputs, carried_memory = recurrence(
        carried_memory,
        (
            attention_split_layout(acceptance_lines),
            log_decay,
            alpha,
            beta,
            address_lines,
            content_lines,
        ),
    )
    centered = outputs - jnp.mean(outputs, axis=-1, keepdims=True)
    variance = jnp.mean(centered * centered, axis=-1, keepdims=True)
    overall_tally = outputs.shape[0]
    clustered_lines = (centered * lax.rsqrt(variance + 0.00064)).reshape(
        overall_tally, -1
    ) * attention_scale_lines[2] + attention_offset_lines[2]
    reward_summand = (
        jnp.sum(
            attention_split_layout(acceptance_lines * present_reward_array) * address_lines,
            axis=-1,
            keepdims=True,
        )
        * content_lines
    )
    return (
        (clustered_lines + reward_summand.reshape(overall_tally, -1)) * valve_amount,
        carried_memory,
    )


def vector_step(param, moved_rows):
    blocks = moved_rows.reshape(
        moved_rows.shape[:-1] + (moved_rows.shape[-1] // HEAD_SIZE, HEAD_SIZE)
    )
    scale = jnp.sqrt(jnp.mean(blocks * blocks, axis=-1, keepdims=True)) + 1e-06
    return param - VECTOR_RATE * (blocks / scale).reshape(moved_rows.shape)


def newton_update(current, gram):
    first = jnp.dot(gram, current, precision=HIGHEST, preferred_element_type=jnp.float32)
    second = jnp.dot(gram, first, precision=HIGHEST, preferred_element_type=jnp.float32)
    return COEFF_A * current + COEFF_B * first + COEFF_C * second


def on_device(
    input_embeddings,
    loss_adjoint,
    earliest_tier_content,
    opening_memory,
    live_extents,
    lagged_blend_coeffs,
    standardize_scales,
    standardize_offsets,
    adapter_narrowing_coeffs,
    adapter_widening_coeffs,
    attention_scale_lines,
    attention_offset_lines,
    present_reward_array,
    forgetting_offset,
    readin_maps,
    emission_coeffs,
    feedforward_address_coeffs,
    feedforward_content_coeffs,
    lagged_blend_velocity,
    standardize_scale_velocity,
    standardize_offset_velocity,
    narrowing_velocity,
    widening_velocity,
    attention_scale_velocity,
    attention_offset_velocity,
    reward_velocity_array,
    forgetting_velocity,
    readin_velocity,
    emission_velocity,
    feedforward_address_velocity,
    feedforward_content_velocity,
):
    seq_count = lax.axis_size("seq")
    seq_index = lax.axis_index("seq")
    overall_tally = input_embeddings.shape[0]
    stride = live_extents.shape[0]
    per_sequence = seq_count // stride
    place = seq_index // stride
    sequence_id = seq_index % stride
    is_first = place == 0
    is_last = place == per_sequence - 1
    slot_ids = place * overall_tally + lax.iota(jnp.int32, overall_tally)
    live = (slot_ids < live_extents[sequence_id]).astype(jnp.float32)[:, None]
    sequence_edges = (
        0,
        LOWRANK_DECAY,
        LOWRANK_DECAY + LOWRANK_RATE,
        LOWRANK_DECAY + LOWRANK_RATE + LOWRANK_VALUE,
        LOWRANK_DECAY + LOWRANK_RATE + LOWRANK_VALUE + LOWRANK_GATE,
    )
    sequence_spans = list(zip(sequence_edges[:-1], sequence_edges[1:]))
    sources = (1, 4, 3, 5)
    inputs = input_embeddings.astype(jnp.float32)
    normed, first_pull = jax.vjp(layer_norm, inputs, standardize_scales[0], standardize_offsets[0])
    before = jnp.concatenate([from_before(normed[-1:], is_first, stride), normed[:-1]], axis=0)
    delta = before - normed
    mixes = [
        (normed + delta * lagged_blend_coeffs[index]).astype(jnp.bfloat16) for index in range(6)
    ]
    weights = readin_maps.astype(jnp.bfloat16)
    down_matrix = adapter_narrowing_coeffs.astype(jnp.bfloat16)
    up_matrix = adapter_widening_coeffs.astype(jnp.bfloat16)
    acceptance_lines = product(mixes[0], weights[0])
    address_lines = product(mixes[2], weights[1])
    content_lines = product(mixes[3], weights[2])
    hidden = [
        product(
            mixes[sources[index]],
            down_matrix[:, sequence_spans[index][0] : sequence_spans[index][1]],
        )
        for index in range(4)
    ]
    tanh_w = jnp.tanh(hidden[0])
    gate_sig = jax.nn.sigmoid(hidden[3])
    acts = [
        tanh_w.astype(jnp.bfloat16),
        hidden[1].astype(jnp.bfloat16),
        hidden[2].astype(jnp.bfloat16),
        gate_sig.astype(jnp.bfloat16),
    ]
    widened_lines = [
        product(acts[index], up_matrix[sequence_spans[index][0] : sequence_spans[index][1]])
        for index in range(4)
    ]
    residual_streams, prepare_pull = jax.vjp(
        prepare,
        address_lines,
        content_lines,
        widened_lines[0],
        widened_lines[1],
        widened_lines[2],
        earliest_tier_content.astype(jnp.float32),
        attention_scale_lines,
        attention_offset_lines,
        forgetting_offset,
    )
    local_heads = residual_streams[0].shape[1]
    identity = jnp.broadcast_to(
        jnp.eye(HEAD_SIZE, dtype=jnp.float32), (local_heads, HEAD_SIZE, HEAD_SIZE)
    )
    blank = jnp.zeros_like(identity)
    doubled = jnp.concatenate([identity, blank], axis=1)
    doubled_values = jnp.concatenate(
        [jnp.zeros_like(residual_streams[4]), residual_streams[4]], axis=2
    )
    unused, summary = recurrence(
        doubled,
        (
            attention_split_layout(acceptance_lines),
            residual_streams[0],
            residual_streams[1],
            residual_streams[2],
            residual_streams[3],
            doubled_values,
        ),
    )
    transfer = summary[:, :HEAD_SIZE]
    offset = summary[:, HEAD_SIZE:]
    own_start = lax.dynamic_index_in_dim(opening_memory, sequence_id, 0, keepdims=False)

    def forward_link(step, incoming):
        received = passed_along(apply_map(incoming, transfer) + offset, "seq", stride)
        return jnp.where(is_first, own_start, received)

    incoming_state = lax.fori_loop(
        0, per_sequence - 1, forward_link, jnp.where(is_first, own_start, blank)
    )
    (branch_full, state_out), finish_pull = jax.vjp(
        finish_index,
        incoming_state,
        acceptance_lines,
        residual_streams,
        widened_lines[3],
        attention_scale_lines,
        attention_offset_lines,
        present_reward_array,
    )
    adapter_result = branch_full.astype(jnp.bfloat16)
    out_low = emission_coeffs.astype(jnp.bfloat16)
    attended = inputs + head_total(product(adapter_result, out_low))
    normed_two, second_pull = jax.vjp(
        layer_norm, attended, standardize_scales[1], standardize_offsets[1]
    )
    before_two = jnp.concatenate(
        [from_before(normed_two[-1:], is_first, stride), normed_two[:-1]], axis=0
    )
    delta_two = before_two - normed_two
    key_in = (normed_two + delta_two * lagged_blend_coeffs[6]).astype(jnp.bfloat16)
    keys_low = feedforward_address_coeffs.astype(jnp.bfloat16)
    values_low = feedforward_content_coeffs.astype(jnp.bfloat16)
    hidden_ffn = product(key_in, keys_low)
    activated = jnp.square(jax.nn.relu(hidden_ffn)).astype(jnp.bfloat16)
    result = attended + head_total(product(activated, values_low))
    block_output = (result * live).astype(jnp.bfloat16)
    grad_result = loss_adjoint.astype(jnp.float32) * live
    grad_low = grad_result.astype(jnp.bfloat16)
    grad_ffnvalue = inner_rows(activated, grad_low)
    grad_hidden = (outer_back(grad_low, values_low) * 2.0 * jax.nn.relu(hidden_ffn)).astype(
        jnp.bfloat16
    )
    grad_ffnkey = inner_rows(key_in, grad_hidden)
    grad_keyin = lax.psum(outer_back(grad_hidden, keys_low), "head")
    carry_two = grad_keyin * lagged_blend_coeffs[6]
    grad_normed_two = (
        grad_keyin
        - carry_two
        + jnp.concatenate([carry_two[1:], from_after(carry_two[:1], is_first, stride)], axis=0)
    )
    grad_attended, grad_gain_two, grad_bias_two = second_pull(grad_normed_two)
    grad_attended = grad_attended + grad_result
    grad_attended_low = grad_attended.astype(jnp.bfloat16)
    grad_output = inner_rows(adapter_result, grad_attended_low)
    grad_branch = outer_back(grad_attended_low, out_low)
    local_in = finish_pull((grad_branch, jnp.zeros_like(state_out)))[0]
    flipped = jnp.swapaxes(transfer, 1, 2)

    def backward_link(step, outgoing):
        received = passed_along(local_in + apply_map(outgoing, flipped), "seq", -stride)
        return jnp.where(is_last, blank, received)

    state_grad_out = lax.fori_loop(0, per_sequence - 1, backward_link, blank)
    (
        grad_state_in,
        grad_receptance,
        grad_streams,
        grad_gate,
        gain_part_a,
        bias_part_a,
        reward_loss_slope,
    ) = finish_pull((grad_branch, state_grad_out))
    (
        grad_keys,
        grad_values,
        grad_up_w,
        grad_up_a,
        grad_up_v,
        grad_first,
        gain_part_b,
        bias_part_b,
        grad_decay,
    ) = prepare_pull(grad_streams)
    grad_headgain = gain_part_a + gain_part_b
    grad_headbias = bias_part_a + bias_part_b
    grad_rec_low = grad_receptance.astype(jnp.bfloat16)
    grad_key_low = grad_keys.astype(jnp.bfloat16)
    grad_value_low = grad_values.astype(jnp.bfloat16)
    grad_lift_low = [
        item.astype(jnp.bfloat16) for item in (grad_up_w, grad_up_a, grad_up_v, grad_gate)
    ]
    grad_project = jnp.stack(
        [
            inner_rows(mixes[0], grad_rec_low),
            inner_rows(mixes[2], grad_key_low),
            inner_rows(mixes[3], grad_value_low),
        ]
    )
    grad_up = jnp.concatenate(
        [inner_rows(acts[index], grad_lift_low[index]) for index in range(4)], axis=0
    )
    split_grads = (
        outer_back(grad_rec_low, weights[0]),
        outer_back(grad_key_low, weights[1]),
        outer_back(grad_value_low, weights[2]),
    )
    split_ids = (0, 2, 3)
    norm_part = sum(
        (split_grads[index] * (1.0 - lagged_blend_coeffs[split_ids[index]]) for index in range(3))
    )
    prev_part = sum(
        (split_grads[index] * lagged_blend_coeffs[split_ids[index]] for index in range(3))
    )
    shift_part = jnp.stack([jnp.sum(item * delta, axis=0) for item in split_grads])
    acts_part = jnp.concatenate(
        [
            outer_back(
                grad_lift_low[index], up_matrix[sequence_spans[index][0] : sequence_spans[index][1]]
            )
            for index in range(4)
        ],
        axis=1,
    )
    norm_sum, prev_sum, acts_sum, shift_sum = lax.psum(
        (norm_part, prev_part, acts_part, shift_part), "head"
    )
    act_grads = [acts_sum[:, start_index:stop_index] for start_index, stop_index in sequence_spans]
    grad_hidden_low = [
        (act_grads[0] * (1.0 - tanh_w * tanh_w)).astype(jnp.bfloat16),
        act_grads[1].astype(jnp.bfloat16),
        act_grads[2].astype(jnp.bfloat16),
        (act_grads[3] * gate_sig * (1.0 - gate_sig)).astype(jnp.bfloat16),
    ]
    grad_down = jnp.concatenate(
        [inner_rows(mixes[sources[index]], grad_hidden_low[index]) for index in range(4)], axis=1
    )
    rep_grads = [
        outer_back(
            grad_hidden_low[index],
            down_matrix[:, sequence_spans[index][0] : sequence_spans[index][1]],
        )
        for index in range(4)
    ]
    grad_normed = norm_sum + sum(
        (rep_grads[index] * (1.0 - lagged_blend_coeffs[sources[index]]) for index in range(4))
    )
    grad_prev = prev_sum + sum(
        (rep_grads[index] * lagged_blend_coeffs[sources[index]] for index in range(4))
    )
    grad_normed = grad_normed + jnp.concatenate(
        [grad_prev[1:], from_after(grad_prev[:1], is_first, stride)], axis=0
    )
    grad_inputs, grad_gain_one, grad_bias_one = first_pull(grad_normed)
    tokens_grad = grad_attended + grad_inputs
    rep_shift = [jnp.sum(item * delta, axis=0) for item in rep_grads]
    grad_shift = jnp.stack(
        [
            shift_sum[0],
            rep_shift[0],
            shift_sum[1],
            shift_sum[2] + rep_shift[2],
            rep_shift[1],
            rep_shift[3],
            jnp.sum(grad_keyin * delta_two, axis=0),
        ]
    )
    choose = ((lax.iota(jnp.int32, stride) == sequence_id) & is_first).astype(jnp.float32)
    state_part = choose[:, None, None, None] * grad_state_in[None]
    summed = lax.psum(
        (
            grad_shift,
            jnp.stack([grad_gain_one, grad_gain_two]),
            jnp.stack([grad_bias_one, grad_bias_two]),
            grad_down,
            grad_up,
            grad_headgain,
            grad_headbias,
            reward_loss_slope,
            grad_decay,
            grad_project,
            grad_output,
            grad_ffnkey,
            grad_ffnvalue,
            state_part,
        ),
        "seq",
    )
    learnable_tensors = (
        lagged_blend_coeffs,
        standardize_scales,
        standardize_offsets,
        adapter_narrowing_coeffs,
        adapter_widening_coeffs,
        attention_scale_lines,
        attention_offset_lines,
        present_reward_array,
        forgetting_offset,
        readin_maps,
        emission_coeffs,
        feedforward_address_coeffs,
        feedforward_content_coeffs,
    )
    velocity_collection = (
        lagged_blend_velocity,
        standardize_scale_velocity,
        standardize_offset_velocity,
        narrowing_velocity,
        widening_velocity,
        attention_scale_velocity,
        attention_offset_velocity,
        reward_velocity_array,
        forgetting_velocity,
        readin_velocity,
        emission_velocity,
        feedforward_address_velocity,
        feedforward_content_velocity,
    )
    moved_rows = [
        DECAY_KEEP * velocity + grad for velocity, grad in zip(velocity_collection, summed[:13])
    ]
    next_values = list(learnable_tensors)
    for index in (0, 1, 2, 5, 6, 7, 8):
        next_values[index] = vector_step(learnable_tensors[index], moved_rows[index])
    square_stack = jnp.stack(
        [moved_rows[9][0], moved_rows[9][1], moved_rows[9][2], moved_rows[10].T]
    )
    wide_stack = jnp.stack([moved_rows[11], moved_rows[12].T])
    own_square = lax.dynamic_index_in_dim(square_stack, seq_index % 4, 0, keepdims=False)
    own_wide = lax.dynamic_index_in_dim(wide_stack, seq_index % 2, 0, keepdims=False)
    split_pieces = [own_square, own_wide] + [
        moved_rows[4][start_index:stop_index] for start_index, stop_index in sequence_spans
    ]
    norms = lax.psum(jnp.stack([jnp.sum(item * item) for item in split_pieces]), "head")
    split_pieces = [
        split_pieces[index] / (jnp.sqrt(norms[index]) + 1e-07) for index in range(len(split_pieces))
    ]
    square_width = split_pieces[0].shape[1]
    whole_square = lax.all_gather(split_pieces[0], "head", axis=1, tiled=True)
    summed_parts = split_pieces[1:]
    down_parts = [
        moved_rows[3][:, start_index:stop_index].T for start_index, stop_index in sequence_spans
    ]
    down_parts = [item / (jnp.sqrt(jnp.sum(item * item)) + 1e-07) for item in down_parts]
    for step in range(NS_STEPS):
        partial_value = [gram_exact(item) for item in summed_parts]
        summed_grams = lax.psum(tuple(partial_value), "head")
        summed_parts = [
            newton_update(summed_parts[index], summed_grams[index])
            for index in range(len(summed_parts))
        ]
        whole_square = newton_update(whole_square, gram_exact(whole_square))
        down_parts = [newton_update(item, gram_exact(item)) for item in down_parts]
    head_index = lax.axis_index("head")
    split_pieces = [
        lax.dynamic_slice_in_dim(whole_square, head_index * square_width, square_width, 1)
    ] + summed_parts
    square_done = [from_owner(split_pieces[0], root) for root in range(4)]
    wide_done = [from_owner(split_pieces[1], seq_count - 2 + root) for root in range(2)]
    share = EMBED_SIZE // seq_count
    start_row = seq_index * share
    project_full = readin_maps - ORTHO_STEP_RATE * jnp.stack(square_done[:3])
    output_full = emission_coeffs - ORTHO_STEP_RATE * square_done[3].T
    ffnkey_full = feedforward_address_coeffs - ORTHO_STEP_RATE * wide_done[0]
    ffnvalue_full = (
        feedforward_content_coeffs
        - ORTHO_STEP_RATE * math.sqrt(max(1.0, FF / EMBED_SIZE)) * wide_done[1].T
    )
    next_values[9] = lax.dynamic_slice_in_dim(project_full, start_row, share, 1)
    next_values[10] = lax.dynamic_slice_in_dim(output_full, start_row, share, 1)
    next_values[11] = lax.dynamic_slice_in_dim(ffnkey_full, start_row, share, 0)
    next_values[12] = lax.dynamic_slice_in_dim(ffnvalue_full, start_row, share, 1)
    next_values[4] = adapter_widening_coeffs - ORTHO_STEP_RATE * jnp.concatenate(
        split_pieces[2:], axis=0
    )
    next_values[3] = adapter_narrowing_coeffs - ORTHO_STEP_RATE * jnp.concatenate(
        [
            math.sqrt(max(1.0, EMBED_SIZE / (sequence_spans[index][1] - sequence_spans[index][0])))
            * down_parts[index].T
            for index in range(4)
        ],
        axis=1,
    )
    return (
        block_output,
        tokens_grad,
        grad_first,
        summed[13],
        next_values[0],
        next_values[1],
        next_values[2],
        next_values[3],
        next_values[4],
        next_values[5],
        next_values[6],
        next_values[7],
        next_values[8],
        next_values[9],
        next_values[10],
        next_values[11],
        next_values[12],
        moved_rows[0],
        moved_rows[1],
        moved_rows[2],
        moved_rows[3],
        moved_rows[4],
        moved_rows[5],
        moved_rows[6],
        moved_rows[7],
        moved_rows[8],
        moved_rows[9],
        moved_rows[10],
        moved_rows[11],
        moved_rows[12],
    )


def solution(mesh):
    return jax.shard_map(
        on_device,
        mesh=mesh,
        in_specs=(
            P("seq", None),
            P("seq", None),
            P("seq", "head"),
            P(None, "head", None, None),
            P(),
            P(),
            P(),
            P(),
            P(),
            P(None, "head"),
            P(None, "head"),
            P(None, "head"),
            P("head"),
            P("head"),
            P(None, None, "head"),
            P("head", None),
            P(None, "head"),
            P("head", None),
            P(),
            P(),
            P(),
            P(),
            P(None, "head"),
            P(None, "head"),
            P(None, "head"),
            P("head"),
            P("head"),
            P(None, None, "head"),
            P("head", None),
            P(None, "head"),
            P("head", None),
        ),
        out_specs=(
            P("seq", None),
            P("seq", None),
            P("seq", "head"),
            P(None, "head", None, None),
            P(),
            P(),
            P(),
            P(),
            P(None, "head"),
            P(None, "head"),
            P(None, "head"),
            P("head"),
            P("head"),
            P(None, "seq", "head"),
            P("head", "seq"),
            P("seq", "head"),
            P("head", "seq"),
            P(),
            P(),
            P(),
            P(),
            P(None, "head"),
            P(None, "head"),
            P(None, "head"),
            P("head"),
            P("head"),
            P(None, None, "head"),
            P("head", None),
            P(None, "head"),
            P("head", None),
        ),
        check_vma=False,
    )
```

profile of v0, /device:TPU:0, one launch (start us, length us, event | category | flops | bytes accessed | tf_op | source)
XLA Modules:
  0.0 2675.7 jit_solution(8085037798432491743)
XLA Ops:
  60.3 94.5 %while.129 = (s32[]{:T(128)}, f32[4,128,64]{1,2,0:T(8,128)S(1)}, f32[4,64,4,64]{3,2,1,0:T(4,128)S(1)}, f32[4,64,4,64]{3,2,1,0:T(4,128)}, f32[4,64,4,64]{3,2,1,0:...) while((s32[]{:T(128)}, f32[4,128,64]{1,2,0:T(8,128)S(1)}, ...), condition=%wide.region_5.6_spmd, body=%wide.region_3.5_spmd.sunk | while | flops 152399936 | bytes 3537517 | solution.py:133
  63.4 19.7 custom-call.41
  86.9 19.7 custom-call.41
  110.4 19.7 custom-call.41
  133.9 19.7 custom-call.41
  158.2 20.5 while.130
  181.3 151.7 %while.131 = (s32[]{:T(128)}, f32[4,64,64]{2,1,0:T(8,128)S(1)}, f32[4,64,4,64]{3,1,2,0:T(8,128)}, f32[4,64,4,64]{3,2,1,0:T(4,128)}, f32[4,64,4,64]{3,2,1,0:T(4,1...) while((s32[]{:T(128)}, f32[4,64,64]{2,1,0:T(8,128)S(1)}, ...), condition=%wide.region_10.11_spmd.clone.clone, body=%wide.region_8.10_spmd.clone.clone.sunk | while | flops 152571968 | bytes 8377185 | solution.py:133
  189.8 20.4 custom-call.42
  227.7 20.4 custom-call.42
  265.6 20.4 custom-call.42
  303.6 20.4 custom-call.42
  349.5 54.7 %all-reduce.32.cloned.1.call-done = f32[256,1024]{1,0:T(8,128)} async-done(((f32[256,1024]{1,0:T(8,128)}), f32[256,1024]{1,0:T(8,128)}) %all-reduce.32.cloned.1.call-update) | async-done | bytes 1048592 | tf_op jit(solution)/shard_map/psum | solution.py:84
  423.5 45.9 %all-reduce.34.cloned.1.call-done = f32[256,1024]{1,0:T(8,128)} async-done(((f32[256,1024]{1,0:T(8,128)}), f32[256,1024]{1,0:T(8,128)}) %all-reduce.34.cloned.1.call-update) | async-done | bytes 1048592 | tf_op jit(solution)/shard_map/psum | solution.py:382
  482.2 103.0 %while.133 = (s32[]{:T(128)}, f32[4,64,64]{2,1,0:T(8,128)S(1)}, f32[4,4,1,64]{3,1,2,0:T(4,128)}, f32[4,64,4,64]{1,3,2,0:T(8,128)S(1)}, f32[4,64,4,64]{3,1,2,0:T(...) while((s32[]{:T(128)}, f32[4,64,64]{2,1,0:T(8,128)S(1)}, ...), condition=%wide.region_25.27_spmd.clone, body=%wide.region_24.26_spmd.clone.sunk | while | flops 63057988 | bytes 2014371 | solution.py:133
  487.7 19.7 custom-call.44
  513.4 19.7 custom-call.44
  539.2 19.7 custom-call.44
  564.9 19.7 custom-call.44
  585.3 24.1 while.134
  614.6 279.0 %while.132 = (s32[]{:T(128)}, f32[4,64,64]{2,1,0:T(8,128)S(1)}, f32[4,64,4,64]{1,0,3,2:T(4,128)}, f32[4,64,4,64]{3,1,2,0:T(8,128)}, f32[4,64,4,64]{3,1,2,0:T(8,1...) while((s32[]{:T(128)}, f32[4,64,64]{2,1,0:T(8,128)S(1)}, ...), condition=%wide.region_32.34_spmd.clone.clone, body=%wide.region_28.33_spmd.clone.clone.sunk | while | flops 316551232 | bytes 14697449 | solution.py:133
  618.3 19.7 custom-call.43
  687.9 19.7 custom-call.43
  757.5 19.7 custom-call.43
  827.1 19.7 custom-call.43
  938.1 170.5 %all-reduce.38.cloned.1.call-done = (f32[288,256]{1,0:T(8,128)}, f32[256,1024]{0,1:T(8,128)}, f32[3,1024,256]{2,1,0:T(8,128)}, f32[1024,1024]{1,0:T(8,128)}, f32[1024,1024]{0,1:T(8,128)}) async-done(((f32[288,256]{1,0:T(8,128)}, f32[256,1024]{0,1:T(8,128)}, f32[3,1024,256]{2,1,0:T(8,128)}, f32[1024,1024]{1,0:T(8,128)}, f32[1024,1024]{0,1:T(8,128)}), (f32[288,256]{1,0:T(8,128)}, f32[256,1024]{0,1:T(8,128)}, ...) | async-done | bytes 12877840 | tf_op jit(solution)/shard_map/psum | solution.py:507
  1181.3 139.7 %all-reduce.48.cloned.1.call-done = (f32[1024,1024]{1,0:T(8,128)}, f32[128,128]{1,0:T(8,128)}) async-done(((f32[1024,1024]{1,0:T(8,128)}, f32[128,128]{1,0:T(8,128)}), (f32[1024,1024]{1,0:T(8,128)}, f32[128,128]{1,0:T(8,128)})) %all-reduce.48.cloned.1.call-update) | async-done | bytes 4259856 | tf_op jit(solution)/shard_map/psum | solution.py:584
  1344.1 19.1 fusion.228
  1398.9 21.5 all-reduce.16
  1428.2 22.5 all-reduce.15
  1452.4 19.5 all-reduce.14
  1473.1 70.2 %all-reduce.46.cloned.1.call-done = (f32[1024,1024]{1,0:T(8,128)}, f32[128,128]{1,0:T(8,128)}) async-done(((f32[1024,1024]{1,0:T(8,128)}, f32[128,128]{1,0:T(8,128)}), (f32[1024,1024]{1,0:T(8,128)}, f32[128,128]{1,0:T(8,128)})) %all-reduce.46.cloned.1.call-update) | async-done | bytes 4259856 | tf_op jit(solution)/shard_map/psum | solution.py:584
  1567.6 19.1 multiply_add_fusion.5
  1612.1 19.6 all-reduce.13
  1686.8 98.7 %all-reduce.44.cloned.1.call-done = (f32[1024,1024]{1,0:T(8,128)}, f32[128,128]{1,0:T(8,128)}) async-done(((f32[1024,1024]{1,0:T(8,128)}, f32[128,128]{1,0:T(8,128)}), (f32[1024,1024]{1,0:T(8,128)}, f32[128,128]{1,0:T(8,128)})) %all-reduce.44.cloned.1.call-update) | async-done | bytes 4259856 | tf_op jit(solution)/shard_map/psum | solution.py:584
  1785.4 17.8 fusion.529
  1808.6 19.1 multiply_add_fusion.4
  1844.5 21.5 fusion.234
  1912.9 21.7 multiply_add_fusion.8
  1951.4 49.8 %all-reduce.42.cloned.1.call-done = (f32[1024,1024]{1,0:T(8,128)}, f32[128,128]{1,0:T(8,128)}) async-done(((f32[1024,1024]{1,0:T(8,128)}, f32[128,128]{1,0:T(8,128)}), (f32[1024,1024]{1,0:T(8,128)}, f32[128,128]{1,0:T(8,128)})) %all-reduce.42.cloned.1.call-update) | async-done | bytes 4259856 | tf_op jit(solution)/shard_map/psum | solution.py:584
  2024.3 19.0 multiply_add_fusion.3
  2059.9 18.1 fusion.520
  2093.8 21.5 multiply_add_fusion.7
  2162.3 21.6 multiply_add_fusion.6
  2245.3 83.9 %all-reduce.40.cloned.1.call-done = (f32[256,1024]{1,0:T(8,128)}, f32[256,1024]{1,0:T(8,128)}, f32[256,288]{0,1:T(8,128)}, f32[256,1024]{1,0:T(8,128)}, f32[1024,1024]{1,0:T(8,128)}, /*index=5*/f32[128,128]{1,0:T(8,128)}) async-done(((f32[256,1024]{1,0:T(8,128)}, f32[256,1024]{1,0:T(8,128)}, f32[256,288]{0,1:T(8,128)}, f32[256,1024]{1,0:T(8,128)}, f32[1024,1024]{1,0:T(8,128)}, ...) | async-done | bytes 7700496 | tf_op jit(solution)/shard_map/psum | solution.py:84
  2377.4 18.2 all-reduce.12
  2396.6 19.2 select_bitcast_fusion
  2426.1 27.7 %all-reduce.9 = (f32[7,1024]{1,0:T(8,128)S(1)}, f32[2,1024]{1,0:T(2,128)S(1)}, f32[2,1024]{1,0:T(2,128)S(1)}, f32[3,256]{1,0:T(4,128)S(1)}, f32[3,256]{1,0:T(4,128)S(1)}, /*index=5*/f32[256]{0:T(256)S(1)}, f32[256]{0:T(256)S(1)}) all-reduce(f32[7,1024]{1,0:T(8,128)S(1)} %stack.107, ...), channel_id=1, replica_groups=mesh['seq'=8,'head'=4] {'seq'}, use_global_device_ids=true, to_apply=%region_49.51 | all-reduce | flops 13312 | bytes 106496 | tf_op jit(solution)/shard_map/psum | solution.py:507
  2464.0 144.8 %all-reduce.36.cloned.1.call-done = (f32[2,4,64,64]{3,2,1,0:T(8,128)}, f32[1024,288]{0,1:T(8,128)}, f32[1,1024,256]{2,1,0:T(8,128)}, f32[1,1024,256]{2,1,0:T(8,1...) async-done(((f32[2,4,64,64]{3,2,1,0:T(8,128)}, f32[1024,288]{0,1:T(8,128)}, f32[1,1024,256]{2,1,0:T(8,128)}, ...) | async-done | bytes 13893648 | tf_op jit(solution)/shard_map/psum | solution.py:507
  (1498 shorter events, 1124.3 us)
Async XLA Ops:
  7.2 396.9 %all-reduce.32.cloned.1.call-start = ((), (), s32[]{:S(2)}) async-start(), calls=%async_computation | async-start | bytes 2097152 | tf_op jit(solution)/shard_map/psum | solution.py:84
  9.4 401.6 %copy-start.191 = (f32[1,1024]{1,0:T(1,128)}, f32[1,1024]{1,0:T(1,128)S(1)}, u32[]{:S(2)}) copy-start(f32[1,1024]{1,0:T(1,128)S(1)} %get-tuple-element.2674) | copy-start | bytes 12292
  13.4 16.1 collective-permute-start.2
  58.0 97.5 %copy-start.54 = (f32[256,256]{0,1:T(8,128)}, f32[256,256]{0,1:T(8,128)S(1)}, u32[]{:S(2)}) copy-start(f32[256,256]{0,1:T(8,128)S(1)} %get-tuple-element.2696) | copy-start | bytes 786436
  158.4 5.9 collective-permute-start
  164.6 6.9 collective-permute-start
  171.8 6.9 collective-permute-start
  338.1 67.6 %copy-start.95 = (f32[256,4,64]{0,2,1:T(8,128)}, f32[256,4,64]{0,2,1:T(8,128)S(1)}, u32[]{:S(2)}) copy-start(f32[256,4,64]{0,2,1:T(8,128)S(1)} %fusion.221) | copy-start | bytes 786436
  342.8 62.9 %copy-start.189 = (f32[256,4]{0,1:T(4,128)}, f32[256,4]{0,1:T(4,128)S(1)}, u32[]{:S(2)}) copy-start(f32[256,4]{0,1:T(4,128)S(1)} %div.273) | copy-start | bytes 12292
  344.3 61.7 %copy-start.119 = (f32[256,128]{0,1:T(8,128)}, f32[256,128]{0,1:T(8,128)S(1)}, u32[]{:S(2)}) copy-start(f32[256,128]{0,1:T(8,128)S(1)} %fusion.261) | copy-start | bytes 393220
  346.2 59.8 %copy-start.205 = (f32[1,1024]{1,0:T(1,128)S(1)}, f32[1,1024]{1,0:T(1,128)}, u32[]{:S(2)}) copy-start(f32[1,1024]{1,0:T(1,128)} %get-tuple-element.2676) | copy-start | bytes 12292
  348.2 121.1 %all-reduce.34.cloned.1.call-start = ((), (), s32[]{:S(2)}) async-start(), calls=%async_computation.1 | async-start | bytes 2097152 | tf_op jit(solution)/shard_map/psum | solution.py:382
  405.7 72.3 %copy-start.1 = (f32[256,1024]{1,0:T(8,128)}, f32[256,1024]{1,0:T(8,128)S(1)}, u32[]{:S(2)}) copy-start(f32[256,1024]{1,0:T(8,128)S(1)} %get-tuple-element.2549) | copy-start | bytes 3145732
  406.3 4.7 collective-permute-start.3
  417.2 691.5 %all-reduce.38.cloned.1.call-start = ((), (), s32[]{:S(2)}) async-start(), calls=%async_computation.4 | async-start | bytes 25755648 | tf_op jit(solution)/shard_map/psum | solution.py:507
  470.8 5.6 collective-permute-start.4
  482.2 103.1 %copy-start.62 = (f32[4,64,64]{2,1,0:T(8,128)S(1)}, f32[4,64,64]{2,1,0:T(8,128)}, u32[]{:S(2)}) copy-start(f32[4,64,64]{2,1,0:T(8,128)} %get-tuple-element.3551) | copy-start | bytes 196612
  585.5 7.9 collective-permute-start.1
  593.8 7.5 collective-permute-start.1
  601.6 7.8 collective-permute-start.1
  931.1 389.9 %all-reduce.48.cloned.1.call-start = ((), (), s32[]{:S(2)}) async-start(), calls=%async_computation.9 | async-start | bytes 8519680 | tf_op jit(solution)/shard_map/psum | solution.py:584
  932.6 176.0 %copy-start.170 = (f32[288,256]{1,0:T(8,128)S(1)}, f32[288,256]{1,0:T(8,128)}, u32[]{:S(2)}) copy-start(f32[288,256]{1,0:T(8,128)} %param.67) | copy-start | bytes 884740
  1115.8 304.5 %copy-start.9 = (f32[3,1024,256]{2,1,0:T(8,128)}, f32[3,1024,256]{2,1,0:T(8,128)S(1)}, u32[]{:S(2)}) copy-start(f32[3,1024,256]{2,1,0:T(8,128)S(1)} %multiply_add_fusion.11) | copy-start | bytes 9437188
  1166.1 377.1 %all-reduce.46.cloned.1.call-start = ((), (), s32[]{:S(2)}) async-start(), calls=%async_computation.8 | async-start | bytes 8519680 | tf_op jit(solution)/shard_map/psum | solution.py:584
  1379.9 256.6 %all-gather.3.cloned.1.call-start = ((), (), s32[]{:S(2)}) async-start(), calls=%async_computation.2 | async-start | bytes 5242880 | tf_op jit(solution)/shard_map/all_gather | solution.py:576
  1428.1 357.3 %all-reduce.44.cloned.1.call-start = ((), (), s32[]{:S(2)}) async-start(), calls=%async_computation.7 | async-start | bytes 8519680 | tf_op jit(solution)/shard_map/psum | solution.py:584
  1603.8 397.3 %all-reduce.42.cloned.1.call-start = ((), (), s32[]{:S(2)}) async-start(), calls=%async_computation.6 | async-start | bytes 8519680 | tf_op jit(solution)/shard_map/psum | solution.py:584
  1844.5 484.7 %all-reduce.40.cloned.1.call-start = ((), (), s32[]{:S(2)}) async-start(), calls=%async_computation.5 | async-start | bytes 15400960 | tf_op jit(solution)/shard_map/psum | solution.py:84
  2059.8 549.0 %all-reduce.36.cloned.1.call-start = ((), (), s32[]{:S(2)}) async-start(), calls=%async_computation.3 | async-start | bytes 28049408 | tf_op jit(solution)/shard_map/psum | solution.py:507
  2243.4 89.5 %copy-start.158 = (f32[256,64]{0,1:T(8,128)S(1)}, f32[256,64]{0,1:T(8,128)}, u32[]{:S(2)}) copy-start(f32[256,64]{0,1:T(8,128)} %copy-done.157) | copy-start | bytes 196612
  2243.4 90.5 %copy-start.120 = (f32[256,128]{0,1:T(8,128)S(1)}, f32[256,128]{0,1:T(8,128)}, u32[]{:S(2)}) copy-start(f32[256,128]{0,1:T(8,128)} %copy-done.119) | copy-start | bytes 393220
  2243.4 91.4 %copy-start.25 = (bf16[256,1024]{1,0:T(8,128)(2,1)S(1)}, bf16[256,1024]{1,0:T(8,128)(2,1)}, u32[]{:S(2)}) copy-start(bf16[256,1024]{1,0:T(8,128)(2,1)} %copy-done.23) | copy-start | bytes 1572868
  2243.4 93.7 %copy-start.65 = (bf16[256,1024]{1,0:T(8,128)(2,1)S(1)}, bf16[256,1024]{1,0:T(8,128)(2,1)}, u32[]{:S(2)}) copy-start(bf16[256,1024]{1,0:T(8,128)(2,1)} %copy-done.64) | copy-start | bytes 1572868
  2245.2 93.2 %copy-start.44 = (f32[256,1024]{1,0:T(8,128)S(1)}, f32[256,1024]{1,0:T(8,128)}, u32[]{:S(2)}) copy-start(f32[256,1024]{1,0:T(8,128)} %copy-done.43) | copy-start | bytes 3145732
  2245.2 93.2 %copy-start.46 = (f32[256,1024]{1,0:T(8,128)S(1)}, f32[256,1024]{1,0:T(8,128)}, u32[]{:S(2)}) copy-start(f32[256,1024]{1,0:T(8,128)} %copy-done.45) | copy-start | bytes 3145732
  2245.2 93.2 %copy-start.203 = (f32[1,1024]{1,0:T(1,128)S(1)}, f32[1,1024]{1,0:T(1,128)}, u32[]{:S(2)}) copy-start(f32[1,1024]{1,0:T(1,128)} %copy-done.201) | copy-start | bytes 12292
  2245.2 93.2 %copy-start.211 = (f32[1,1024]{1,0:T(1,128)S(1)}, f32[1,1024]{1,0:T(1,128)}, u32[]{:S(2)}) copy-start(f32[1,1024]{1,0:T(1,128)} %copy-done.210) | copy-start | bytes 12292
  2245.2 93.2 %copy-start.213 = (f32[1,1024]{1,0:T(1,128)S(1)}, f32[1,1024]{1,0:T(1,128)}, u32[]{:S(2)}) copy-start(f32[1,1024]{1,0:T(1,128)} %get-tuple-element.2665) | copy-start | bytes 12292
  2245.2 93.2 %copy-start.215 = (f32[1,1024]{1,0:T(1,128)S(1)}, f32[1,1024]{1,0:T(1,128)}, u32[]{:S(2)}) copy-start(f32[1,1024]{1,0:T(1,128)} %get-tuple-element.2667) | copy-start | bytes 12292
  2342.7 77.1 %collective-permute-start.5 = (f32[1,1024]{1,0:T(1,128)S(1)}, f32[1,1024]{1,0:T(1,128)S(1)}, u32[]{:S(2)}, u32[]{:S(2)}) collective-permute-start(f32[1,1024]{1,0:T(1,128)S(1)} %broadcast_select_fusion.5), channel_id=1, source_target_pairs={{8,0},{12,4},{16,8},{20,12},{24,16},{28,20},{9,1},{13,5},{17,9},{2... | collective-permute-start | bytes 12296 | tf_op jit(solution)/shard_map/ppermute | solution.py:31
  2453.8 156.8 %copy-start.183 = (f32[7,1024]{1,0:T(8,128)}, f32[7,1024]{1,0:T(8,128)S(1)}, u32[]{:S(2)}) copy-start(f32[7,1024]{1,0:T(8,128)S(1)} %get-tuple-element.3694) | copy-start | bytes 86020
  2454.2 156.4 %copy-start.233 = (f32[2,1024]{1,0:T(2,128)}, f32[2,1024]{1,0:T(2,128)S(1)}, u32[]{:S(2)}) copy-start(f32[2,1024]{1,0:T(2,128)S(1)} %get-tuple-element.3695) | copy-start | bytes 24580
  2454.5 156.1 %copy-start.234 = (f32[2,1024]{1,0:T(2,128)}, f32[2,1024]{1,0:T(2,128)S(1)}, u32[]{:S(2)}) copy-start(f32[2,1024]{1,0:T(2,128)S(1)} %get-tuple-element.3696) | copy-start | bytes 24580
  2454.9 155.7 %copy-start.243 = (f32[3,256]{1,0:T(4,128)}, f32[3,256]{1,0:T(4,128)S(1)}, u32[]{:S(2)}) copy-start(f32[3,256]{1,0:T(4,128)S(1)} %get-tuple-element.3699) | copy-start | bytes 9220
  2455.3 155.4 %copy-start.244 = (f32[3,256]{1,0:T(4,128)}, f32[3,256]{1,0:T(4,128)S(1)}, u32[]{:S(2)}) copy-start(f32[3,256]{1,0:T(4,128)S(1)} %get-tuple-element.3700) | copy-start | bytes 9220
  2455.6 155.0 %copy-start.269 = (f32[256]{0:T(256)}, f32[256]{0:T(256)S(1)}, u32[]{:S(2)}) copy-start(f32[256]{0:T(256)S(1)} %get-tuple-element.3701) | copy-start | bytes 3076
  2456.0 154.6 %copy-start.270 = (f32[256]{0:T(256)}, f32[256]{0:T(256)S(1)}, u32[]{:S(2)}) copy-start(f32[256]{0:T(256)S(1)} %get-tuple-element.3702) | copy-start | bytes 3076
  2610.7 55.5 %copy-start.32 = (f32[1024,288]{0,1:T(8,128)}, f32[1024,288]{0,1:T(8,128)S(1)}, u32[]{:S(2)}) copy-start(f32[1024,288]{0,1:T(8,128)S(1)} %multiply_add_fusion.12) | copy-start | bytes 3538948
  (261 other events, 2461.5 us)
Sparse Core Ops, SparseCore 0:
  348.3 55.7 all-reduce.31
  417.3 52.0 all-reduce.33
  931.2 177.3 all-reduce.37
  1166.2 154.6 all-reduce.47
  1380.0 163.1 all-reduce.45
  1544.7 81.5 all-gather.2
  1629.5 155.8 all-reduce.43
  1844.6 156.4 all-reduce.41
  2059.9 269.1 all-reduce.39
  2417.1 191.6 all-reduce.35
where the time goes:
time: 2690 us; the launch traced here: 2680 us
  waiting for transfers between devices  885 us (33%)
  matrix products  776 us (29%)
  other arithmetic  491 us (18%)
  local copies, waits for them, and re-layouts  325 us (12%)
  blocking collectives  141 us (5%)
  starting transfers between devices  27.6 us (1%)
    psum x4, waiting for transfers between devices, on_device(): summed_grams = lax.psum(tuple(partial_value), 'head')  358 us
    another operation x60, other arithmetic, block_form(): jax.scipy.linalg.solve_triangular(system, right, lower=True, unit_diagona...  329 us
    psum x2, waiting for transfers between devices, on_device(): lax.psum((grad_shift, jnp.stack([grad_gain_one, grad_gain_two]), jnp.stac...  315 us
    dot_general x50, matrix products, newton_update(): jnp.dot(gram, first, precision=HIGHEST, preferred_element_type=jnp.float32)  226 us
    dot_general x50, matrix products, newton_update(): jnp.dot(gram, current, precision=HIGHEST, preferred_element_type=jnp.floa...  181 us
    dot_general x50, matrix products, gram_exact(): jnp.einsum('ta,ba->tb', item, item, precision=HIGHEST, preferred_element_...  169 us
    psum x2, waiting for transfers between devices, head_total(): return lax.psum(term, 'head')  139 us
    dynamic_update_slice x60, local copies, waits for them, and re-layouts, recurrence(): carried_memory, outputs = lax.scan(block_form, carried_memory, blocks)  89 us
  transfers between devices with their start and end apart: 20, of which 17 were waited for; matrix products, arithmetic and copies ran while one was open for 20% of the time, Pallas kernels for 0%

commit v1 on v0

v1 whole, which is shorter than its diff:
```python
import functools
import math

import jax
import jax.numpy as jnp
from jax import lax
from jax.experimental import pallas as pl
from jax.experimental.pallas import tpu as pltpu
from jax.sharding import PartitionSpec as P

EMBED_SIZE = 1024
HEAD_SIZE = 64
FF = 4096
LOWRANK_DECAY = 64
LOWRANK_RATE = 64
LOWRANK_VALUE = 32
LOWRANK_GATE = 128
BLOCK = 64
NS_STEPS = 5


HIGHEST = lax.Precision.HIGHEST
COEFF_A = 3.4445
COEFF_B = -4.775
COEFF_C = 2.0315
ORTHO_STEP_RATE = 0.5
VECTOR_RATE = 0.75
DECAY_KEEP = 0.5


def passed_along(value, axis, steps):
    count = lax.axis_size(axis)
    first, last = (max(0, -steps), min(count, count - steps))
    return lax.ppermute(value, axis, [(source, source + steps) for source in range(first, last)])


def layer_norm(content_lines, gain, bias):
    centered = content_lines - jnp.mean(content_lines, axis=-1, keepdims=True)
    variance = jnp.mean(centered * centered, axis=-1, keepdims=True)
    return centered * lax.rsqrt(variance + 1e-05) * gain + bias


def product(left, right):
    return jnp.dot(left, right, preferred_element_type=jnp.float32)


def inner_rows(left, right):
    return jnp.einsum("ta,tb->ab", left, right, preferred_element_type=jnp.float32)


def outer_back(left, right):
    return jnp.einsum("ta,ba->tb", left, right, preferred_element_type=jnp.float32)


def neighbour_row(row, offset):
    return passed_along(row, "seq", offset)


def from_before(row, is_first, stride):
    return jnp.where(is_first, 0.0, neighbour_row(row, stride))


def from_after(row, is_first, stride):
    return neighbour_row(jnp.where(is_first, 0.0, row), -stride)


def head_total(term):
    return lax.psum(term, "head")


def vector_step(param, moved_rows):
    blocks = moved_rows.reshape(
        moved_rows.shape[:-1] + (moved_rows.shape[-1] // HEAD_SIZE, HEAD_SIZE)
    )
    scale = jnp.sqrt(jnp.mean(blocks * blocks, axis=-1, keepdims=True)) + 1e-06
    return param - VECTOR_RATE * (blocks / scale).reshape(moved_rows.shape)


BF = jnp.bfloat16
F32 = jnp.float32
SQUASH = math.exp(-0.5)


def split(x):
    high = x.astype(BF)
    return high, (x - high.astype(F32)).astype(BF)


DIMS = {"nn": ((1,), (0,)), "nt": ((1,), (1,)), "tn": ((0,), (0,))}


def dot_kind(a, b, kind):
    return lax.dot_general(a, b, (DIMS[kind], ((), ())), preferred_element_type=F32)


class Pairing:
    def __init__(self, heads, passes):
        self.heads = heads
        self.passes = passes
        width = heads * HEAD_SIZE
        rows = lax.broadcasted_iota(jnp.int32, (width, width), 0) // HEAD_SIZE
        cols = lax.broadcasted_iota(jnp.int32, (width, width), 1) // HEAD_SIZE
        self.same = rows == cols

    def parts(self, x):
        return split(x) if self.passes == 3 else (x.astype(BF),)

    def spread(self, x):
        zero = jnp.zeros((), BF)
        return tuple(
            jnp.where(self.same, jnp.concatenate([item] * self.heads, axis=0), zero)
            for item in self.parts(x)
        )

    def run(self, left, right, kind):
        total = dot_kind(left[0], right[0], kind)
        if len(left) > 1:
            total = total + (dot_kind(left[0], right[1], kind) + dot_kind(left[1], right[0], kind))
        return total

    def nn(self, a, b_spread):
        return self.run(self.parts(a), b_spread, "nn")

    def nt(self, a, b_spread):
        return self.run(self.parts(a), b_spread, "nt")

    def tn(self, a, b):
        full = jnp.where(self.same, self.run(self.parts(a), self.parts(b), "tn"), 0.0)
        total = full[:HEAD_SIZE]
        for head in range(1, self.heads):
            total = total + full[head * HEAD_SIZE : (head + 1) * HEAD_SIZE]
        return total


def head_sum(x, same):
    ones = same.astype(BF)
    high, low = split(x)
    return dot_kind(high, ones, "nn") + dot_kind(low, ones, "nn")


def exact_left(ones, x):
    high, rest = split(x)
    third = (x - high.astype(F32) - rest.astype(F32)).astype(BF)
    return (
        dot_kind(ones, high, "nn") + dot_kind(ones, rest, "nn") + dot_kind(ones, third, "nn")
    )


def sigmoid(x):
    return 1.0 / (1.0 + jnp.exp(-x))


def side_iotas(width):
    rows = lax.broadcasted_iota(jnp.int32, (HEAD_SIZE, width), 0)
    cols = lax.broadcasted_iota(jnp.int32, (HEAD_SIZE, width), 1) % HEAD_SIZE
    return rows, cols


def prepared(keys, values, up_w, up_a, up_v, first, scale, offset, forget, same):
    sig_w = sigmoid(forget + up_w)
    log_decay = -SQUASH * sig_w
    rate = sigmoid(offset[0:1] + up_a)
    sig_v = sigmoid(offset[1:2] + up_v)
    mixed = values + (first - values) * sig_v
    scaled = keys * scale[0:1]
    inverse = lax.rsqrt(head_sum(scaled * scaled, same) + 1e-05)
    unit = scaled * inverse
    grown = 1.0 + (rate - 1.0) * scale[1:2]
    return sig_w, log_decay, rate, sig_v, mixed, inverse, unit, grown


def decays(log_decay):
    rows = lax.broadcasted_iota(jnp.int32, (BLOCK, BLOCK), 0)
    cols = lax.broadcasted_iota(jnp.int32, (BLOCK, BLOCK), 1)
    total = exact_left((rows >= cols).astype(BF), log_decay)
    last = total[BLOCK - 1 : BLOCK]
    return jnp.exp(total), jnp.exp(total - log_decay), jnp.exp(-total), jnp.exp(last - total), jnp.exp(last)


def forward_local_kernel(
    heads, rec_ref, keys_ref, values_ref, upw_ref, upa_ref, upv_ref, first_ref, scale_ref, offset_ref, forget_ref,
    summary_ref, blocks_ref, read_ref, local_ref, inv_ref, wide_ref, fixed_ref, prb_ref, prk_ref, pak_ref,
):
    width = heads * HEAD_SIZE
    pair = Pairing(heads, 3)
    rows, cols = side_iotas(width)
    strict, upto = rows > cols, rows >= cols
    eye = (rows == cols).astype(F32)
    scale, offset, forget = scale_ref[...], offset_ref[...], forget_ref[...]
    count = rec_ref.shape[0] // BLOCK
    moves = []
    for index in range(count):
        span = slice(index * BLOCK, (index + 1) * BLOCK)
        keys = keys_ref[span]
        sig_w, log_decay, rate, sig_v, mixed, inverse, unit, grown = prepared(
            keys, values_ref[span], upw_ref[span], upa_ref[span], upv_ref[span],
            first_ref[span].astype(F32), scale, offset, forget, pair.same,
        )
        e_total, e_before, e_back, e_tail, e_last = decays(log_decay)
        beta, new_keys = unit * rate, keys * grown
        grown_r, grown_a = rec_ref[span] * e_total, -unit * e_before
        both = jnp.concatenate([grown_a, grown_r], axis=0)
        on_b = pair.nt(both, pair.spread(beta * e_back))
        on_k = pair.nt(both, pair.spread(new_keys * e_back))
        pab = jnp.where(strict, on_b[:BLOCK], 0.0)
        pak = jnp.where(strict, on_k[:BLOCK], 0.0)
        prb = jnp.where(upto, on_b[BLOCK:], 0.0)
        prk = jnp.where(upto, on_k[BLOCK:], 0.0)
        size = 1
        solved = eye
        while size < BLOCK:
            corner = (
                ((rows // size) % 2 == 1) & ((cols // size) % 2 == 0)
                & (rows // (2 * size) == cols // (2 * size))
            )
            piece = jnp.where(corner, pab, 0.0)
            if size > 1:
                piece = pair.nn(pair.nn(solved, pair.spread(piece)), pair.spread(solved))
            solved = solved + piece
            size *= 2
        mixed_spread = pair.spread(mixed)
        on_v = pair.nn(jnp.concatenate([pak, prk], axis=0), mixed_spread)
        wide = pair.nn(solved, pair.spread(grown_a))
        fixed = pair.nn(solved, pair.spread(on_v[:BLOCK]))
        read_ref[span] = grown_r + pair.nn(prb, pair.spread(wide))
        local_ref[span] = on_v[BLOCK:] + pair.nn(prb, pair.spread(fixed))
        tail_b, tail_k = beta * e_tail, new_keys * e_tail
        move = eye * e_last + pair.tn(wide, tail_b)
        add = pair.tn(jnp.concatenate([fixed, mixed], axis=0), jnp.concatenate([tail_b, tail_k], axis=0))
        blocks_ref[index, :BLOCK] = move
        blocks_ref[index, BLOCK:] = add
        inv_ref[span] = solved
        wide_ref[span] = wide
        fixed_ref[span] = fixed
        prb_ref[span] = prb
        prk_ref[span] = prk
        pak_ref[span] = pak
        moves.append((move, add))
    summary = jnp.concatenate(moves[0], axis=0)
    for move, add in moves[1:]:
        summary = pair.nn(summary, pair.spread(move))
        summary = jnp.concatenate([summary[:BLOCK], summary[BLOCK:] + add], axis=0)
    summary_ref[...] = summary


def group_norm(outputs, same):
    mean = head_sum(outputs, same) * (1.0 / HEAD_SIZE)
    centered = outputs - mean
    variance = head_sum(centered * centered, same) * (1.0 / HEAD_SIZE)
    inverse = lax.rsqrt(variance + 0.00064)
    return centered * inverse, inverse


def forward_state_kernel(
    heads, start_ref, others_ref, flags_ref, blocks_ref, read_ref, local_ref, rec_ref, keys_ref, values_ref, upa_ref, upv_ref,
    first_ref, gate_ref, scale_ref, offset_ref, reward_ref, branch_ref, states_ref, outputs_ref,
):
    pair = Pairing(heads, 3)
    count = rec_ref.shape[0] // BLOCK
    state = start_ref[...]
    for index in range(others_ref.shape[0]):
        move = pair.spread(others_ref[index, :BLOCK])
        moved = pair.nn(state, move) + others_ref[index, BLOCK:]
        state = jnp.where(flags_ref[index : index + 1] > 0.0, moved, state)
    scale, offset, reward = scale_ref[...], offset_ref[...], reward_ref[...]
    for index in range(count):
        span = slice(index * BLOCK, (index + 1) * BLOCK)
        states_ref[index] = state
        outputs_ref[span] = pair.nt(read_ref[span], pair.spread(state)) + local_ref[span]
        if index < count - 1:
            state = pair.nn(state, pair.spread(blocks_ref[index, :BLOCK])) + blocks_ref[index, BLOCK:]
    normal, _ = group_norm(outputs_ref[...], pair.same)
    rate = sigmoid(offset[0:1] + upa_ref[...])
    values = values_ref[...]
    mixed = values + (first_ref[...].astype(F32) - values) * sigmoid(offset[1:2] + upv_ref[...])
    new_keys = keys_ref[...] * (1.0 + (rate - 1.0) * scale[1:2])
    bonus = head_sum(rec_ref[...] * new_keys * reward, pair.same)
    branch = (normal * scale[2:3] + offset[2:3] + bonus * mixed) * gate_ref[...]
    branch_ref[...] = branch.astype(BF)


def backward_local_kernel(
    heads, slope_ref, outputs_ref, read_ref, blocks_ref, rec_ref, keys_ref, values_ref, upa_ref, upv_ref, first_ref,
    gate_ref, scale_ref, offset_ref, reward_ref,
    local_ref, steps_ref, slope_out_ref, gate_out_ref, rec_out_ref, keys_out_ref, values_out_ref, sums_ref,
):
    pair = Pairing(heads, 3)
    same = pair.same
    count = rec_ref.shape[0] // BLOCK
    scale, offset, reward = scale_ref[...], offset_ref[...], reward_ref[...]
    normal, inverse = group_norm(outputs_ref[...], same)
    rate = sigmoid(offset[0:1] + upa_ref[...])
    values = values_ref[...]
    mixed = values + (first_ref[...].astype(F32) - values) * sigmoid(offset[1:2] + upv_ref[...])
    new_keys = keys_ref[...] * (1.0 + (rate - 1.0) * scale[1:2])
    rec = rec_ref[...]
    bonus = head_sum(rec * new_keys * reward, same)
    slope = slope_ref[...]
    gate_out_ref[...] = (slope * (normal * scale[2:3] + offset[2:3] + bonus * mixed)).astype(BF)
    inner = slope * gate_ref[...]
    d_bonus = head_sum(inner * mixed, same)
    rec_out_ref[...] = d_bonus * new_keys * reward
    keys_out_ref[...] = d_bonus * rec * reward
    values_out_ref[...] = inner * bonus
    d_normal = inner * scale[2:3]
    mean_a = head_sum(d_normal, same) * (1.0 / HEAD_SIZE)
    mean_b = head_sum(d_normal * normal, same) * (1.0 / HEAD_SIZE)
    slope_out_ref[...] = inverse * (d_normal - mean_a - normal * mean_b)
    sums_ref[0:1] = jnp.sum(inner * normal, axis=0, keepdims=True)
    sums_ref[1:2] = jnp.sum(inner, axis=0, keepdims=True)
    sums_ref[2:3] = jnp.sum(d_bonus * rec * new_keys, axis=0, keepdims=True)
    sums_ref[3:8] = jnp.zeros((5, slope.shape[1]), F32)
    total = None
    for index in range(count - 1, -1, -1):
        span = slice(index * BLOCK, (index + 1) * BLOCK)
        step = pair.tn(slope_out_ref[span], read_ref[span])
        steps_ref[index] = step
        total = step if total is None else pair.nt(total, pair.spread(blocks_ref[index, :BLOCK])) + step
    local_ref[...] = total


def backward_state_kernel(
    heads, moves_ref, locals_ref, flags_ref, states_ref, blocks_ref, steps_ref, inv_ref, wide_ref, fixed_ref, prb_ref, prk_ref,
    pak_ref, slope_ref, rec_extra_ref, keys_extra_ref, values_extra_ref, rec_ref, keys_ref, values_ref, upw_ref, upa_ref, upv_ref,
    first_ref, scale_ref, offset_ref, forget_ref,
    d_state_ref, d_rec_ref, d_keys_ref, d_values_ref, d_upw_ref, d_upa_ref, d_upv_ref, d_first_ref, sums_ref,
):
    pair = Pairing(heads, 3)
    same = pair.same
    width = heads * HEAD_SIZE
    rows, cols = side_iotas(width)
    strict, upto = rows > cols, rows >= cols
    count = rec_ref.shape[0] // BLOCK
    scale, offset, forget = scale_ref[...], offset_ref[...], forget_ref[...]
    outgoing = jnp.zeros((HEAD_SIZE, width), F32)
    for index in range(locals_ref.shape[0] - 1, -1, -1):
        moved = pair.nt(outgoing, pair.spread(moves_ref[index])) + locals_ref[index]
        outgoing = jnp.where(flags_ref[index : index + 1] > 0.0, moved, outgoing)
    row_ids = lax.broadcasted_iota(jnp.int32, (BLOCK, 2 * BLOCK), 0)
    col_ids = lax.broadcasted_iota(jnp.int32, (BLOCK, 2 * BLOCK), 1)
    later = ((col_ids < BLOCK) & (col_ids >= row_ids)) | (col_ids - BLOCK > row_ids)
    later = later.astype(BF)
    sums = [jnp.zeros((1, width), F32) for _ in range(5)]
    for index in range(count - 1, -1, -1):
        span = slice(index * BLOCK, (index + 1) * BLOCK)
        keys, values = keys_ref[span], values_ref[span]
        first = first_ref[span].astype(F32)
        sig_w, log_decay, rate, sig_v, mixed, inverse, unit, grown = prepared(
            keys, values, upw_ref[span], upa_ref[span], upv_ref[span],
            first, scale, offset, forget, same,
        )
        e_total, e_before, e_back, e_tail, e_last = decays(log_decay)
        beta, new_keys = unit * rate, keys * grown
        grown_r, grown_a = rec_ref[span] * e_total, -unit * e_before
        shrunk_b, shrunk_k = beta * e_back, new_keys * e_back
        tail_b, tail_k = beta * e_tail, new_keys * e_tail
        state, slope = states_ref[index], slope_ref[span]
        state_spread, outgoing_spread = pair.spread(state), pair.spread(outgoing)
        carried = pair.nt(wide_ref[span], state_spread) + fixed_ref[span]
        tails = pair.nt(jnp.concatenate([tail_b, tail_k], axis=0), outgoing_spread)
        d_carried = pair.tn(prb_ref[span], slope) + tails[:BLOCK]
        d_right = pair.tn(inv_ref[span], d_carried)
        slopes = jnp.concatenate([d_right, slope], axis=0)
        d_mixed = tails[BLOCK:] + values_extra_ref[span] + pair.tn(
            jnp.concatenate([pak_ref[span], prk_ref[span]], axis=0), slopes
        )
        d_grown = pair.nn(slopes, state_spread)
        on_c = pair.nt(slopes, pair.spread(carried))
        on_v = pair.nt(slopes, pair.spread(mixed))
        d_b = jnp.concatenate([jnp.where(strict, on_c[:BLOCK], 0.0), jnp.where(upto, on_c[BLOCK:], 0.0)], axis=0)
        d_k = jnp.concatenate([jnp.where(strict, on_v[:BLOCK], 0.0), jnp.where(upto, on_v[BLOCK:], 0.0)], axis=0)
        d_grown = d_grown + pair.nn(d_b, pair.spread(shrunk_b)) + pair.nn(d_k, pair.spread(shrunk_k))
        both = jnp.concatenate([grown_a, grown_r], axis=0)
        d_shrunk_b, d_shrunk_k = pair.tn(d_b, both), pair.tn(d_k, both)
        d_tails = pair.nn(jnp.concatenate([carried, mixed], axis=0), outgoing_spread)
        d_tail_b, d_tail_k = d_tails[:BLOCK], d_tails[BLOCK:]
        d_last = jnp.sum(state * outgoing, axis=0, keepdims=True) * e_last + jnp.sum(
            d_tail_b * tail_b + d_tail_k * tail_k, axis=0, keepdims=True
        )
        d_grown_a, d_grown_r = d_grown[:BLOCK], d_grown[BLOCK:]
        d_total = (
            d_grown_r * grown_r - d_shrunk_b * shrunk_b - d_shrunk_k * shrunk_k
            - d_tail_b * tail_b - d_tail_k * tail_k
        )
        d_log = exact_left(later, jnp.concatenate([d_total, d_grown_a * grown_a], axis=0)) + d_last
        d_rec_ref[span] = (d_grown_r * e_total + rec_extra_ref[span]).astype(BF)
        d_alpha = d_grown_a * e_before
        d_beta = d_shrunk_b * e_back + d_tail_b * e_tail
        d_new = d_shrunk_k * e_back + d_tail_k * e_tail + keys_extra_ref[span]
        d_unit = d_beta * rate - d_alpha
        d_rate = d_beta * unit + d_new * keys * scale[1:2]
        d_scaled = inverse * (d_unit - unit * head_sum(d_unit * unit, same))
        d_keys_ref[span] = (d_new * grown + d_scaled * scale[0:1]).astype(BF)
        d_upw = d_log * log_decay * (1.0 - sig_w)
        d_upa = d_rate * rate * (1.0 - rate)
        d_upv = d_mixed * (first - values) * sig_v * (1.0 - sig_v)
        d_upw_ref[span] = d_upw.astype(BF)
        d_upa_ref[span] = d_upa.astype(BF)
        d_upv_ref[span] = d_upv.astype(BF)
        d_values_ref[span] = (d_mixed * (1.0 - sig_v)).astype(BF)
        d_first_ref[span] = d_mixed * sig_v
        terms = (d_scaled * keys, d_new * keys * (rate - 1.0), d_upa, d_upv, d_upw)
        sums = [total + jnp.sum(term, axis=0, keepdims=True) for total, term in zip(sums, terms)]
        outgoing = pair.nt(outgoing, pair.spread(blocks_ref[index, :BLOCK])) + steps_ref[index]
    d_state_ref[...] = outgoing
    for index in range(5):
        sums_ref[index : index + 1] = sums[index]
    sums_ref[5:8] = jnp.zeros((3, width), F32)


def local_call(body, heads, results, operands):
    return pl.pallas_call(
        functools.partial(body, heads),
        out_shape=tuple(jax.ShapeDtypeStruct(shape, dtype) for shape, dtype in results),
        in_specs=[pl.BlockSpec(memory_space=pltpu.VMEM)] * len(operands),
        out_specs=tuple(pl.BlockSpec(memory_space=pltpu.VMEM) for _ in results),
        compiler_params=pltpu.CompilerParams(vmem_limit_bytes=48 * 1024 * 1024),
    )(*operands)


def cheap(left, right):
    return jnp.dot(left.astype(BF), right.astype(BF), preferred_element_type=F32)


def close(left, right):
    return jnp.dot(left, right, precision=lax.Precision.HIGH, preferred_element_type=F32)


def exact(left, right):
    return jnp.matmul(left, right, precision=HIGHEST, preferred_element_type=F32)


def shifted_terms(gram, shift, dot):
    rest = gram - shift * jnp.eye(gram.shape[-1], dtype=F32)
    value = COEFF_A + COEFF_B * shift + COEFF_C * shift * shift
    return value, (COEFF_B + 2.0 * COEFF_C * shift) * rest + COEFF_C * dot(rest, rest), rest


def newton_whole(current):
    for step in range(NS_STEPS):
        dot = cheap if step < 3 else close
        gram = dot(current, current.T)
        shift = jnp.trace(gram) / gram.shape[0]
        value, terms, _ = shifted_terms(gram, shift, dot)
        current = value * current + dot(terms, current)
    return current


def gram_next(gram, shift, value, terms, rest, dot):
    square = 2.0 * value * terms + dot(terms, terms)
    return value * value * gram + shift * square + dot(rest, square)


def newton_grams(current, gram, shift_of, dots, applies):
    for step in range(NS_STEPS):
        shift = shift_of(gram)
        value, terms, rest = shifted_terms(gram, shift, dots[step])
        current = value * current + applies[step](terms, current)
        if step < NS_STEPS - 1:
            gram = gram_next(gram, shift, value, terms, rest, dots[step])
    return current


def on_device(
    input_embeddings,
    loss_adjoint,
    earliest_tier_content,
    opening_memory,
    live_extents,
    lagged_blend_coeffs,
    standardize_scales,
    standardize_offsets,
    adapter_narrowing_coeffs,
    adapter_widening_coeffs,
    attention_scale_lines,
    attention_offset_lines,
    present_reward_array,
    forgetting_offset,
    readin_maps,
    emission_coeffs,
    feedforward_address_coeffs,
    feedforward_content_coeffs,
    lagged_blend_velocity,
    standardize_scale_velocity,
    standardize_offset_velocity,
    narrowing_velocity,
    widening_velocity,
    attention_scale_velocity,
    attention_offset_velocity,
    reward_velocity_array,
    forgetting_velocity,
    readin_velocity,
    emission_velocity,
    feedforward_address_velocity,
    feedforward_content_velocity,
):
    seq_count = lax.axis_size("seq")
    seq_index = lax.axis_index("seq")
    overall_tally = input_embeddings.shape[0]
    stride = live_extents.shape[0]
    per_sequence = seq_count // stride
    place = seq_index // stride
    sequence_id = seq_index % stride
    is_first = place == 0
    is_last = place == per_sequence - 1
    slot_ids = place * overall_tally + lax.iota(jnp.int32, overall_tally)
    live = (slot_ids < live_extents[sequence_id]).astype(jnp.float32)[:, None]
    sequence_edges = (
        0,
        LOWRANK_DECAY,
        LOWRANK_DECAY + LOWRANK_RATE,
        LOWRANK_DECAY + LOWRANK_RATE + LOWRANK_VALUE,
        LOWRANK_DECAY + LOWRANK_RATE + LOWRANK_VALUE + LOWRANK_GATE,
    )
    sequence_spans = list(zip(sequence_edges[:-1], sequence_edges[1:]))
    sources = (1, 4, 3, 5)
    inputs = input_embeddings.astype(jnp.float32)
    normed, first_pull = jax.vjp(layer_norm, inputs, standardize_scales[0], standardize_offsets[0])
    before = jnp.concatenate([from_before(normed[-1:], is_first, stride), normed[:-1]], axis=0)
    delta = before - normed
    mixes = [
        (normed + delta * lagged_blend_coeffs[index]).astype(jnp.bfloat16) for index in range(6)
    ]
    weights = readin_maps.astype(jnp.bfloat16)
    down_matrix = adapter_narrowing_coeffs.astype(jnp.bfloat16)
    up_matrix = adapter_widening_coeffs.astype(jnp.bfloat16)
    acceptance_lines = product(mixes[0], weights[0])
    address_lines = product(mixes[2], weights[1])
    content_lines = product(mixes[3], weights[2])
    hidden = [
        product(
            mixes[sources[index]],
            down_matrix[:, sequence_spans[index][0] : sequence_spans[index][1]],
        )
        for index in range(4)
    ]
    tanh_w = jnp.tanh(hidden[0])
    gate_sig = jax.nn.sigmoid(hidden[3])
    acts = [
        tanh_w.astype(jnp.bfloat16),
        hidden[1].astype(jnp.bfloat16),
        hidden[2].astype(jnp.bfloat16),
        gate_sig.astype(jnp.bfloat16),
    ]
    widened_lines = [
        product(acts[index], up_matrix[sequence_spans[index][0] : sequence_spans[index][1]])
        for index in range(4)
    ]
    width = acceptance_lines.shape[1]
    local_heads = width // HEAD_SIZE
    blocks_count = overall_tally // BLOCK
    lines = ((overall_tally, width), F32)
    low_lines = ((overall_tally, width), BF)
    tiny = ((8, width), F32)
    state_shape = ((HEAD_SIZE, width), F32)
    steps_shape = ((blocks_count, HEAD_SIZE, width), F32)
    pieces_shape = ((blocks_count, 2 * HEAD_SIZE, width), F32)
    reward_row = present_reward_array.reshape(1, width)
    forget_row = forgetting_offset.reshape(1, width)
    raw_lines = (address_lines, content_lines)
    summary, pieces, read, local, solved, wide, fixed, pair_rb, pair_rk, pair_ak = local_call(
        forward_local_kernel,
        local_heads,
        [((2 * HEAD_SIZE, width), F32), pieces_shape] + [lines] * 8,
        (acceptance_lines, *raw_lines, *widened_lines[:3], earliest_tier_content)
        + (attention_scale_lines, attention_offset_lines, forget_row),
    )
    distances = range(1, per_sequence)
    earlier = jnp.stack([passed_along(summary, "seq", far * stride) for far in distances][::-1])
    later_moves = jnp.stack(
        [passed_along(summary[:HEAD_SIZE], "seq", -far * stride) for far in distances]
    )
    earlier_flags = jnp.stack([(place >= far).astype(F32) for far in distances][::-1])
    later_flags = jnp.stack([(place + far < per_sequence).astype(F32) for far in distances])
    earlier_flags = jnp.broadcast_to(earlier_flags[:, None], (per_sequence - 1, width))
    later_flags = jnp.broadcast_to(later_flags[:, None], (per_sequence - 1, width))
    own_start = lax.dynamic_index_in_dim(opening_memory, sequence_id, 0, keepdims=False)
    own_start = jnp.swapaxes(own_start, 0, 1).reshape(HEAD_SIZE, width)
    adapter_result, states, outputs = local_call(
        forward_state_kernel,
        local_heads,
        [low_lines, steps_shape, lines],
        (own_start, earlier, earlier_flags, pieces, read, local, acceptance_lines, *raw_lines)
        + (widened_lines[1], widened_lines[2], earliest_tier_content, widened_lines[3])
        + (attention_scale_lines, attention_offset_lines, reward_row),
    )
    out_low = emission_coeffs.astype(jnp.bfloat16)
    attended = inputs + head_total(product(adapter_result, out_low))
    normed_two, second_pull = jax.vjp(
        layer_norm, attended, standardize_scales[1], standardize_offsets[1]
    )
    before_two = jnp.concatenate(
        [from_before(normed_two[-1:], is_first, stride), normed_two[:-1]], axis=0
    )
    delta_two = before_two - normed_two
    key_in = (normed_two + delta_two * lagged_blend_coeffs[6]).astype(jnp.bfloat16)
    keys_low = feedforward_address_coeffs.astype(jnp.bfloat16)
    values_low = feedforward_content_coeffs.astype(jnp.bfloat16)
    hidden_ffn = product(key_in, keys_low)
    activated = jnp.square(jax.nn.relu(hidden_ffn)).astype(jnp.bfloat16)
    result = attended + head_total(product(activated, values_low))
    block_output = (result * live).astype(jnp.bfloat16)
    grad_result = loss_adjoint.astype(jnp.float32) * live
    grad_low = grad_result.astype(jnp.bfloat16)
    grad_ffnvalue = inner_rows(activated, grad_low)
    grad_hidden = (outer_back(grad_low, values_low) * 2.0 * jax.nn.relu(hidden_ffn)).astype(
        jnp.bfloat16
    )
    grad_ffnkey = inner_rows(key_in, grad_hidden)
    grad_ffnkey, grad_ffnvalue = lax.psum((grad_ffnkey, grad_ffnvalue), "seq")
    grad_keyin = lax.psum(outer_back(grad_hidden, keys_low), "head")
    carry_two = grad_keyin * lagged_blend_coeffs[6]
    grad_normed_two = (
        grad_keyin
        - carry_two
        + jnp.concatenate([carry_two[1:], from_after(carry_two[:1], is_first, stride)], axis=0)
    )
    grad_attended, grad_gain_two, grad_bias_two = second_pull(grad_normed_two)
    grad_attended = grad_attended + grad_result
    grad_attended_low = grad_attended.astype(jnp.bfloat16)
    grad_output = inner_rows(adapter_result, grad_attended_low)
    grad_branch = outer_back(grad_attended_low, out_low)
    (
        state_local,
        steps,
        slope,
        grad_gate,
        acceptance_extra,
        address_extra,
        content_extra,
        sums_a,
    ) = local_call(
        backward_local_kernel,
        local_heads,
        [state_shape, steps_shape, lines, low_lines, lines, lines, lines, tiny],
        (grad_branch, outputs, read, pieces, acceptance_lines, *raw_lines)
        + (widened_lines[1], widened_lines[2], earliest_tier_content, widened_lines[3])
        + (attention_scale_lines, attention_offset_lines, reward_row),
    )
    later_locals = jnp.stack([passed_along(state_local, "seq", -far * stride) for far in distances])
    (
        grad_state_in,
        grad_rec_low,
        grad_key_low,
        grad_value_low,
        grad_up_w,
        grad_up_a,
        grad_up_v,
        grad_first,
        sums_b,
    ) = local_call(
        backward_state_kernel,
        local_heads,
        [state_shape] + [low_lines] * 6 + [lines, tiny],
        (later_moves, later_locals, later_flags, states, pieces, steps, solved, wide, fixed)
        + (pair_rb, pair_rk, pair_ak, slope, acceptance_extra, address_extra, content_extra)
        + (acceptance_lines, *raw_lines, *widened_lines[:3], earliest_tier_content)
        + (attention_scale_lines, attention_offset_lines, forget_row),
    )
    grad_state_in = jnp.swapaxes(grad_state_in.reshape(HEAD_SIZE, local_heads, HEAD_SIZE), 0, 1)
    grad_headgain = jnp.concatenate([sums_b[0:2], sums_a[0:1]], axis=0)
    grad_headbias = jnp.concatenate([sums_b[2:4], sums_a[1:2]], axis=0)
    reward_loss_slope = sums_a[2]
    grad_decay = sums_b[4]
    grad_lift_low = [grad_up_w, grad_up_a, grad_up_v, grad_gate]
    grad_project = jnp.stack(
        [
            inner_rows(mixes[0], grad_rec_low),
            inner_rows(mixes[2], grad_key_low),
            inner_rows(mixes[3], grad_value_low),
        ]
    )
    grad_up = jnp.concatenate(
        [inner_rows(acts[index], grad_lift_low[index]) for index in range(4)], axis=0
    )
    split_grads = (
        outer_back(grad_rec_low, weights[0]),
        outer_back(grad_key_low, weights[1]),
        outer_back(grad_value_low, weights[2]),
    )
    split_ids = (0, 2, 3)
    norm_part = sum(
        (split_grads[index] * (1.0 - lagged_blend_coeffs[split_ids[index]]) for index in range(3))
    )
    prev_part = sum(
        (split_grads[index] * lagged_blend_coeffs[split_ids[index]] for index in range(3))
    )
    shift_part = jnp.stack([jnp.sum(item * delta, axis=0) for item in split_grads])
    acts_part = jnp.concatenate(
        [
            outer_back(
                grad_lift_low[index], up_matrix[sequence_spans[index][0] : sequence_spans[index][1]]
            )
            for index in range(4)
        ],
        axis=1,
    )
    acts_sum, shift_sum = lax.psum((acts_part, shift_part), "head")
    normed_part = norm_part + jnp.concatenate(
        [prev_part[1:], from_after(prev_part[:1], is_first, stride)], axis=0
    )
    norm_sum = lax.psum(normed_part, "head")
    act_grads = [acts_sum[:, start_index:stop_index] for start_index, stop_index in sequence_spans]
    grad_hidden_low = [
        (act_grads[0] * (1.0 - tanh_w * tanh_w)).astype(jnp.bfloat16),
        act_grads[1].astype(jnp.bfloat16),
        act_grads[2].astype(jnp.bfloat16),
        (act_grads[3] * gate_sig * (1.0 - gate_sig)).astype(jnp.bfloat16),
    ]
    grad_down = jnp.concatenate(
        [inner_rows(mixes[sources[index]], grad_hidden_low[index]) for index in range(4)], axis=1
    )
    rep_grads = [
        outer_back(
            grad_hidden_low[index],
            down_matrix[:, sequence_spans[index][0] : sequence_spans[index][1]],
        )
        for index in range(4)
    ]
    grad_normed = norm_sum + sum(
        (rep_grads[index] * (1.0 - lagged_blend_coeffs[sources[index]]) for index in range(4))
    )
    grad_prev = sum(
        (rep_grads[index] * lagged_blend_coeffs[sources[index]] for index in range(4))
    )
    grad_normed = grad_normed + jnp.concatenate(
        [grad_prev[1:], from_after(grad_prev[:1], is_first, stride)], axis=0
    )
    grad_inputs, grad_gain_one, grad_bias_one = first_pull(grad_normed)
    tokens_grad = grad_attended + grad_inputs
    rep_shift = [jnp.sum(item * delta, axis=0) for item in rep_grads]
    grad_shift = jnp.stack(
        [
            shift_sum[0],
            rep_shift[0],
            shift_sum[1],
            shift_sum[2] + rep_shift[2],
            rep_shift[1],
            rep_shift[3],
            jnp.sum(grad_keyin * delta_two, axis=0),
        ]
    )
    choose = ((lax.iota(jnp.int32, stride) == sequence_id) & is_first).astype(jnp.float32)
    state_part = choose[:, None, None, None] * grad_state_in[None]
    summed = lax.psum(
        (
            grad_shift,
            jnp.stack([grad_gain_one, grad_gain_two]),
            jnp.stack([grad_bias_one, grad_bias_two]),
            grad_down,
            grad_up,
            grad_headgain,
            grad_headbias,
            reward_loss_slope,
            grad_decay,
            grad_project,
            grad_output,
            state_part,
        ),
        "seq",
    )
    summed = (*summed[:11], grad_ffnkey, grad_ffnvalue, summed[11])
    learnable_tensors = (
        lagged_blend_coeffs,
        standardize_scales,
        standardize_offsets,
        adapter_narrowing_coeffs,
        adapter_widening_coeffs,
        attention_scale_lines,
        attention_offset_lines,
        present_reward_array,
        forgetting_offset,
        readin_maps,
        emission_coeffs,
        feedforward_address_coeffs,
        feedforward_content_coeffs,
    )
    velocity_collection = (
        lagged_blend_velocity,
        standardize_scale_velocity,
        standardize_offset_velocity,
        narrowing_velocity,
        widening_velocity,
        attention_scale_velocity,
        attention_offset_velocity,
        reward_velocity_array,
        forgetting_velocity,
        readin_velocity,
        emission_velocity,
        feedforward_address_velocity,
        feedforward_content_velocity,
    )
    moved_rows = [
        DECAY_KEEP * velocity + grad for velocity, grad in zip(velocity_collection, summed[:13])
    ]
    next_values = list(learnable_tensors)
    for index in (0, 1, 2, 5, 6, 7, 8):
        next_values[index] = vector_step(learnable_tensors[index], moved_rows[index])
    square_stack = jnp.stack(
        [moved_rows[9][0], moved_rows[9][1], moved_rows[9][2], moved_rows[10].T]
    )
    wide_stack = jnp.stack([moved_rows[11], moved_rows[12].T])
    own_square = lax.dynamic_index_in_dim(square_stack, seq_index % 4, 0, keepdims=False)
    own_wide = lax.dynamic_index_in_dim(wide_stack, seq_index % 2, 0, keepdims=False)
    lift_moved = moved_rows[4]
    sink_moved = moved_rows[3].T
    total_rank = lift_moved.shape[0]
    wide_gram, lift_gram = lax.psum(
        (close(own_wide, own_wide.T), exact(lift_moved, lift_moved.T)), "head"
    )
    whole_square = lax.all_gather(own_square, "head", axis=1, tiled=True)
    square_scale = 1.0 / (jnp.sqrt(jnp.sum(whole_square * whole_square)) + 1e-07)
    whole_square = newton_whole(whole_square * square_scale)
    wide_scale = 1.0 / (jnp.sqrt(jnp.trace(wide_gram)) + 1e-07)
    wide_done = newton_grams(
        own_wide * wide_scale,
        wide_gram * (wide_scale * wide_scale),
        lambda gram: jnp.trace(gram) / gram.shape[0],
        (cheap, cheap, close, close, close),
        (cheap, cheap, cheap, close, close),
    )
    group = jnp.stack(
        [(lax.iota(jnp.int32, total_rank) >= edge).astype(jnp.int32) for edge in sequence_edges[1:4]]
    ).sum(axis=0)
    member = (group[:, None] == group[None, :]).astype(F32)
    sizes = jnp.sum(member, axis=1)
    grams = jnp.stack([lift_gram, exact(sink_moved, sink_moved.T)]) * member
    eye = jnp.eye(total_rank, dtype=F32)
    diagonals = jnp.sum(grams * eye, axis=2)
    scales = 1.0 / (jnp.sqrt(exact(diagonals, member)) + 1e-07)
    grams = grams * (scales * scales)[:, :, None]
    shift_of = lambda gram: (exact(jnp.sum(gram * eye, axis=2), member) / sizes)[:, :, None]
    maps = newton_grams(jnp.broadcast_to(eye, grams.shape), grams, shift_of, [exact] * 5, [exact] * 5)
    maps = maps * scales[:, :, None]
    lift_done = exact(maps[0], lift_moved)
    sink_done = exact(maps[1], sink_moved)
    head_index = lax.axis_index("head")
    square_width = own_square.shape[1]
    square_done = lax.dynamic_slice_in_dim(whole_square, head_index * square_width, square_width, 1)
    share = EMBED_SIZE // seq_count
    start_row = seq_index * share

    def shared_rows(done):
        return lax.all_to_all(
            done.reshape(seq_count, share, done.shape[1]), "seq", 0, 0, tiled=True
        )

    square_rows = shared_rows(square_done)
    wide_rows = shared_rows(wide_done)
    rows_of = lambda item, axis: lax.dynamic_slice_in_dim(item, start_row, share, axis)
    next_values[9] = rows_of(readin_maps, 1) - ORTHO_STEP_RATE * square_rows[:3]
    next_values[10] = rows_of(emission_coeffs, 1) - ORTHO_STEP_RATE * square_rows[3].T
    next_values[11] = rows_of(feedforward_address_coeffs, 0) - ORTHO_STEP_RATE * wide_rows[0]
    next_values[12] = (
        rows_of(feedforward_content_coeffs, 1)
        - ORTHO_STEP_RATE * math.sqrt(max(1.0, FF / EMBED_SIZE)) * wide_rows[1].T
    )
    next_values[4] = adapter_widening_coeffs - ORTHO_STEP_RATE * lift_done
    next_values[3] = adapter_narrowing_coeffs - ORTHO_STEP_RATE * jnp.concatenate(
        [
            math.sqrt(max(1.0, EMBED_SIZE / (stop_index - start_index)))
            * sink_done[start_index:stop_index].T
            for start_index, stop_index in sequence_spans
        ],
        axis=1,
    )
    return (
        block_output,
        tokens_grad,
        grad_first,
        summed[13],
        next_values[0],
        next_values[1],
        next_values[2],
        next_values[3],
        next_values[4],
        next_values[5],
        next_values[6],
        next_values[7],
        next_values[8],
        next_values[9],
        next_values[10],
        next_values[11],
        next_values[12],
        moved_rows[0],
        moved_rows[1],
        moved_rows[2],
        moved_rows[3],
        moved_rows[4],
        moved_rows[5],
        moved_rows[6],
        moved_rows[7],
        moved_rows[8],
        moved_rows[9],
        moved_rows[10],
        moved_rows[11],
        moved_rows[12],
    )


def solution(mesh):
    return jax.shard_map(
        on_device,
        mesh=mesh,
        in_specs=(
            P("seq", None),
            P("seq", None),
            P("seq", "head"),
            P(None, "head", None, None),
            P(),
            P(),
            P(),
            P(),
            P(),
            P(None, "head"),
            P(None, "head"),
            P(None, "head"),
            P("head"),
            P("head"),
            P(None, None, "head"),
            P("head", None),
            P(None, "head"),
            P("head", None),
            P(),
            P(),
            P(),
            P(),
            P(None, "head"),
            P(None, "head"),
            P(None, "head"),
            P("head"),
            P("head"),
            P(None, None, "head"),
            P("head", None),
            P(None, "head"),
            P("head", None),
        ),
        out_specs=(
            P("seq", None),
            P("seq", None),
            P("seq", "head"),
            P(None, "head", None, None),
            P(),
            P(),
            P(),
            P(),
            P(None, "head"),
            P(None, "head"),
            P(None, "head"),
            P("head"),
            P("head"),
            P(None, "seq", "head"),
            P("head", "seq"),
            P("seq", "head"),
            P("head", "seq"),
            P(),
            P(),
            P(),
            P(),
            P(None, "head"),
            P(None, "head"),
            P(None, "head"),
            P("head"),
            P("head"),
            P(None, None, "head"),
            P("head", None),
            P(None, "head"),
            P("head", None),
        ),
        check_vma=False,
    )
```

time: 2690 us -> 1100 us (0.41)
  waiting for transfers between devices: 885 us -> 425 us
  matrix products: 776 us -> 355 us
  other arithmetic: 491 us -> 84.2 us
  local copies, waits for them, and re-layouts: 325 us -> 59.9 us
  blocking collectives: 141 us -> 44.4 us
  Pallas kernels: 0 us -> 28.1 us
    dot_general x332 -> x59, matrix products: 706 us -> 322 us  [the longest x16 162 us: close(): jnp.dot(left, right, precision=lax.Precision.HIGH, preferred_element_type...]
    another operation x88 -> x7, other arithmetic: 334 us -> 2.33 us  [the longest x1 1.14 us: on_device(): jnp.stack([moved_rows[9][0], moved_rows[9][1], moved_rows[9][2], moved_ro...]
    psum x4 -> x1, waiting for transfers between devices: 358 us -> 30.1 us  [on_device(): acts_sum, shift_sum = lax.psum((acts_part, shift_part), 'head')]
    psum x2 -> x1, waiting for transfers between devices: 315 us -> 170 us  [on_device(): lax.psum((grad_shift, jnp.stack([grad_gain_one, grad_gain_two]), jnp.stac...]
    psum x6 -> x1, blocking collectives: 113 us -> 19.6 us  [on_device(): acts_sum, shift_sum = lax.psum((acts_part, shift_part), 'head')]
    dynamic_update_slice x60 -> x0, local copies, waits for them, and re-layouts: 89 us -> none  [recurrence(): carried_memory, outputs = lax.scan(block_form, carried_memory, blocks)]
    dot_general x10 -> x0, local copies, waits for them, and re-layouts: 53.6 us -> none  [newton_update(): jnp.dot(gram, current, precision=HIGHEST, preferred_element_type=jnp.floa...]
    dynamic_slice x43 -> x2, local copies, waits for them, and re-layouts: 36.3 us -> 2.03 us  [on_device(): lax.dynamic_slice_in_dim(item, start_row, share, axis)]
  transfers between devices with their start and end apart: 20 -> 22, of which waited for: 17 -> 16; matrix products, arithmetic and copies ran while one was open for 20% -> 41% of each run, Pallas kernels for 0% -> 0%
where the time goes in v1:
time: 1100 us; the launch traced here: 1090 us
  waiting for transfers between devices  425 us (39%)
  matrix products  355 us (32%)
  other arithmetic  84.2 us (8%)
  local copies, waits for them, and re-layouts  59.9 us (5%)
  between operations  51.9 us (5%)
  blocking collectives  44.4 us (4%)
  starting transfers between devices  37.1 us (3%)
  Pallas kernels  28.1 us (3%)
    psum x1, waiting for transfers between devices, on_device(): lax.psum((grad_shift, jnp.stack([grad_gain_one, grad_gain_two]), jnp.stac...  170 us
    dot_general x16, matrix products, close(): jnp.dot(left, right, precision=lax.Precision.HIGH, preferred_element_type...  162 us
    psum x2, waiting for transfers between devices, head_total(): return lax.psum(term, 'head')  141 us
    dot_general x15, matrix products, cheap(): jnp.dot(left.astype(BF), right.astype(BF), preferred_element_type=F32)  107 us
    dot_general x28, matrix products, exact(): jnp.matmul(left, right, precision=HIGHEST, preferred_element_type=F32)  53.7 us
    psum x1, waiting for transfers between devices, on_device(): grad_keyin = lax.psum(outer_back(grad_hidden, keys_low), 'head')  38.6 us
    unnamed x406, local copies, waits for them, and re-layouts  38.5 us
    psum x1, waiting for transfers between devices, on_device(): acts_sum, shift_sum = lax.psum((acts_part, shift_part), 'head')  30.1 us
  transfers between devices with their start and end apart: 22, of which 16 were waited for; matrix products, arithmetic and copies ran while one was open for 41% of the time, Pallas kernels for 0%

profile of v1, /device:TPU:0, one launch (start us, length us, event | category | flops | bytes accessed | tf_op | source)
XLA Modules:
  0.0 1085.3 jit_solution(13614707899591753277)
XLA Ops:
  13.4 5.0 collective-permute-start
  28.1 13.4 %shard_map.526 = (f32[128,256]{1,0:T(8,128)S(1)}, f32[4,128,256]{2,1,0:T(8,128)S(1)}, f32[256,256]{1,0:T(8,128)S(1)}, f32[256,256]{1,0:T(8,128)S(1)}, f32[256,25...) custom-call(f32[256,256]{1,0:T(8,128)S(1)} %fusion.197.rec_ref, ...), custom_call_target="tpu_custom_call" | custom-call | tf_op jit(solution)/shard_map/pallas_call | solution.py:412
  57.4 53.9 %all-reduce.9.cloned.1.call-done = f32[256,1024]{1,0:T(8,128)} async-done(((f32[256,1024]{1,0:T(8,128)}), f32[256,1024]{1,0:T(8,128)}) %all-reduce.9.cloned.1.call-update) | async-done | bytes 1048592 | tf_op jit(solution)/shard_map/psum | solution.py:68
  138.2 38.6 %all-reduce.11.cloned.1.call-done = f32[256,1024]{1,0:T(8,128)} async-done(((f32[256,1024]{1,0:T(8,128)}), f32[256,1024]{1,0:T(8,128)}) %all-reduce.11.cloned.1.call-update) | async-done | bytes 1048592 | tf_op jit(solution)/shard_map/psum | solution.py:611
  199.0 10.6 shard_map.529
  217.1 30.1 %all-reduce.13.cloned.1.call-done = f32[256,288]{0,1:T(8,128)} async-done(((f32[256,288]{0,1:T(8,128)}), f32[256,288]{0,1:T(8,128)}) %all-reduce.13.cloned.1.call-update) | async-done | bytes 294928 | tf_op jit(solution)/shard_map/psum | solution.py:698
  256.4 5.5 copy.174
  261.9 5.1 broadcast_multiply_fusion
  267.0 5.5 copy.175
  272.5 5.5 copy.176
  278.0 169.7 %all-reduce.15.cloned.1.call-done = (f32[2,4,64,64]{3,2,1,0:T(8,128)}, f32[1024,288]{0,1:T(8,128)}, f32[288,256]{1,0:T(8,128)}, f32[3,1024,256]{2,1,0:T(8,128)},...) async-done(((f32[2,4,64,64]{3,2,1,0:T(8,128)}, f32[1024,288]{0,1:T(8,128)}, f32[288,256]{1,0:T(8,128)}, f32[3,1024,256]{2,1,0:T(8,128)}, ...) | async-done | bytes 14188560 | tf_op jit(solution)/shard_map/psum | solution.py:745
  475.2 19.6 %psum.160 = f32[3,1024]{1,0:T(4,128)S(1)} all-reduce(f32[3,1024]{1,0:T(4,128)S(1)} %pad_maximum_fusion.7), channel_id=1, replica_groups=mesh['seq'=8,'head'=4] {'head'}, use_global_device_ids=true, to_apply=%region_17.18 | all-reduce | flops 3072 | bytes 24576 | tf_op jit(solution)/shard_map/psum | solution.py:698
  500.7 6.9 multiply_add_fusion.13
  507.7 5.4 copy.182
  513.0 4.6 add.766
  523.2 8.8 fusion.227
  532.0 4.5 all-gather.3.cloned.1.call-done
  541.0 9.2 select_reduce_fusion.10
  553.5 13.8 %bitcast_add_fusion = f32[1024,1024]{1,0:T(8,128)} fusion(f32[1,1024,1024]{2,1,0:T(8,128)} %all-gather.3.cloned.1.call-done, f32[]{:T(128)S(6)} %add.741, f32[]{:T(128)S(6)} %div.273, f32[1024,1024]{1,0:T(8,128)} %get-tuple-element.302, f32[]{:T(128)S(6)} %div.274, f32[]{:T(128)S(6)} %add.742), kind=kOutput, calls=%fused_computation.6 | convolution fusion | flops 4311744512 | bytes 12582928 | tf_op jit(solution)/shard_map/dot_general | solution.py:422
  567.2 8.5 select_reduce_fusion.9
  578.9 13.7 %multiply_add_fusion.16 = f32[1024,1024]{1,0:T(8,128)} fusion(f32[1024,1024]{1,0:T(8,128)} %bitcast_add_fusion, f32[]{:T(128)S(6)} %add.746, f32[1024,1024]{1,0:T(8,128)} %get-tuple-element.304, f32[]{:T(128)S(6)} %div.275, f32[]{:T(128)S(6)} %add.747), kind=kOutput, calls=%fused_computation.60 | convolution fusion | flops 4309647360 | bytes 12582924 | tf_op jit(solution)/shard_map/dot_general | solution.py:422
  592.6 8.7 select_reduce_fusion.8
  604.5 13.8 %multiply_add_fusion.15 = f32[1024,1024]{1,0:T(8,128)} fusion(f32[1024,1024]{1,0:T(8,128)} %multiply_add_fusion.16, f32[]{:T(128)S(6)} %add.751, f32[1024,1024]{1,0:T(8,128)} %get-tuple-element.306, f32[]{:T(128)S(6)} %div.276, f32[]{:T(128)S(6)} %add.752), kind=kOutput, calls=%fused_computation.56 | convolution fusion | flops 4309647360 | bytes 12582924 | tf_op jit(solution)/shard_map/dot_general | solution.py:422
  618.3 12.6 %select_reduce_fusion.7 = (f32[]{:T(128)}, f32[1024,1024]{1,0:T(8,128)}) fusion(f32[1024,1024]{1,0:T(8,128)} %multiply_add_fusion.15), kind=kOutput, calls=%fused_computation.53 | convolution fusion | flops 6445596672 | bytes 8388612 | tf_op jit(solution)/shard_map/dot_general | solution.py:426
  634.1 11.0 %fusion.17 = f32[1024,1024]{1,0:T(8,128)S(1)} fusion(f32[1024,1024]{1,0:T(8,128)} %get-tuple-element.308, f32[]{:T(128)S(6)} %div.277), kind=kOutput, calls=%fused_computation.71 | convolution fusion | flops 6445596672 | bytes 8388612 | tf_op jit(solution)/shard_map/dot_general | solution.py:426
  645.1 7.3 multiply_add_fusion.14
  652.4 9.9 select_reduce_fusion.6
  665.6 11.0 %fusion.18 = f32[1024,1024]{1,0:T(8,128)S(1)} fusion(f32[1024,1024]{1,0:T(8,128)} %get-tuple-element.310, f32[]{:T(128)S(6)} %div.278), kind=kOutput, calls=%fused_computation.72 | convolution fusion | flops 6445596672 | bytes 8388612 | tf_op jit(solution)/shard_map/dot_general | solution.py:426
  676.6 7.0 fusion.6
  689.4 87.3 %all-reduce.17.cloned.1.call-done = (f32[256,1024]{1,0:T(8,128)}, f32[256,1024]{1,0:T(8,128)}, f32[1,288,288]{2,1,0:T(8,128)}, f32[1024,1024]{1,0:T(8,128)}) async-done(((f32[256,1024]{1,0:T(8,128)}, f32[256,1024]{1,0:T(8,128)}, f32[1,288,288]{2,1,0:T(8,128)}, f32[1024,1024]{1,0:T(8,128)}), (f32[256,1024]{1,0:T(8,128)}, f32[256,1024]{1,0:T(8,128)}, f32[1,288,288]{2,1,0:T(8,128)}, ...) | async-done | bytes 6623248 | tf_op jit(solution)/shard_map/psum | solution.py:68
  786.5 7.3 multiply_add_fusion.12
  797.5 5.5 select_reduce_fusion.3
  806.2 7.1 multiply_add_fusion.10
  817.1 5.4 select_reduce_fusion.2
  825.7 12.2 %multiply_add_fusion.8 = f32[1024,1024]{1,0:T(8,128)S(1)} fusion(f32[1024,1024]{1,0:T(8,128)} %get-tuple-element.314, f32[]{:T(128)S(6)} %add.785, f32[]{:T(128)S(6)} %div.282), kind=kOutput, calls=%fused_computation.26 | convolution fusion | flops 6451888128 | bytes 8388616 | tf_op jit(solution)/shard_map/dot_general | solution.py:426
  838.0 7.0 fusion.362
  845.0 10.7 select_reduce_fusion.1
  858.9 12.0 %multiply_add_fusion.6 = f32[1024,1024]{1,0:T(8,128)S(1)} fusion(f32[1024,1024]{1,0:T(8,128)} %get-tuple-element.316, f32[]{:T(128)S(6)} %add.792, f32[]{:T(128)S(6)} %div.283), kind=kOutput, calls=%fused_computation.21 | convolution fusion | flops 6451888128 | bytes 8388616 | tf_op jit(solution)/shard_map/dot_general | solution.py:426
  871.0 8.3 fusion.363
  879.3 15.3 %select_reduce_fusion = (f32[]{:T(128)}, f32[1024,1024]{1,0:T(8,128)}) fusion(f32[1024,1024]{1,0:T(8,128)} %fusion.363, f32[1024,1024]{1,0:T(8,128)S(1)} %multiply_add_fusion.6, f32[]{:T(128)S(6)} %mul.1800, f32[1024,1024]{1,0:T(8,128)} %get-tuple-element.316, f32[]{:T(128)S(6)} %div.283, f32[]{:T(128)S(6)} %mul.1796), kind=kOutput, calls=%fused_computation.18 | convolution fusion | flops 6457131008 | bytes 16777232 | tf_op jit(solution)/shard_map/dot_general | solution.py:426
  908.9 24.8 %all-reduce = (f32[7,1024]{1,0:T(8,128)S(1)}, f32[2,1024]{1,0:T(2,128)S(1)}, f32[2,1024]{1,0:T(2,128)S(1)}, f32[3,256]{1,0:T(4,128)S(1)}, f32[3,256]{1,0:T(4,128)S(1)}, /*index=5*/f32[256]{0:T(256)S(1)}, f32[256]{0:T(256)S(1)}) all-reduce(f32[7,1024]{1,0:T(8,128)S(1)} %copy-done.118, ...), channel_id=1, replica_groups=mesh['seq'=8,'head'=4] {'seq'}, use_global_device_ids=true, to_apply=%region_23.24 | all-reduce | flops 13312 | bytes 106496 | tf_op jit(solution)/shard_map/psum | solution.py:745
  972.3 8.3 fusion.364
  980.6 11.4 %fusion.20 = f32[1024,1024]{1,0:T(8,128)S(1)} fusion(f32[1024,1024]{1,0:T(8,128)} %get-tuple-element.318, f32[]{:T(128)S(6)} %div.284), kind=kOutput, calls=%fused_computation.74 | convolution fusion | flops 6445596672 | bytes 8388612 | tf_op jit(solution)/shard_map/dot_general | solution.py:426
  992.0 8.9 multiply_add_fusion
  1000.9 5.4 copy.178
  1014.5 4.8 fusion.105
  1019.2 4.8 all-to-all-start.1
  1043.6 29.6 %all-to-all-done.1 = f32[8,128,1024]{1,2,0:T(8,128)} async-done(((f32[8,128,1024]{1,2,0:T(8,128)}), f32[8,128,1024]{1,2,0:T(8,128)}, u32[]{:S(2)}, u32[]{:S(2)}) %all-to-all-start.1) | async-done | bytes 4194336 | tf_op jit(solution)/shard_map/all_to_all | solution.py:844
  (670 shorter events, 238.5 us)
Async XLA Ops:
  7.2 104.1 %all-reduce.9.cloned.1.call-start = ((), (), s32[]{:S(2)}) async-start(), calls=%async_computation.2 | async-start | bytes 2097152 | tf_op jit(solution)/shard_map/psum | solution.py:68
  11.3 107.0 %copy-start.121 = (f32[1,1024]{1,0:T(1,128)}, f32[1,1024]{1,0:T(1,128)S(1)}, u32[]{:S(2)}) copy-start(f32[1,1024]{1,0:T(1,128)S(1)} %get-tuple-element.273) | copy-start | bytes 12292
  12.1 106.2 %copy-start.127 = (f32[1,1024]{1,0:T(1,128)}, f32[1,1024]{1,0:T(1,128)S(1)}, u32[]{:S(2)}) copy-start(f32[1,1024]{1,0:T(1,128)S(1)} %get-tuple-element.275) | copy-start | bytes 12292
  13.4 10.5 collective-permute-start
  20.2 98.1 %copy-start.125 = (f32[1,1024]{1,0:T(1,128)}, f32[1,1024]{1,0:T(1,128)S(1)}, u32[]{:S(2)}) copy-start(f32[1,1024]{1,0:T(1,128)S(1)} %get-tuple-element.264) | copy-start | bytes 12292
  42.2 145.8 %copy-start.2 = (f32[4,128,256]{2,1,0:T(8,128)}, f32[4,128,256]{2,1,0:T(8,128)S(1)}, u32[]{:S(2)}) copy-start(f32[4,128,256]{2,1,0:T(8,128)S(1)} %get-tuple-element.61.blocks_ref) | copy-start | bytes 1572868
  42.2 7.5 collective-permute-start.3
  45.6 6.2 collective-permute-start.2
  47.6 4.2 collective-permute-start.1
  56.7 120.1 %all-reduce.11.cloned.1.call-start = ((), (), s32[]{:S(2)}) async-start(), calls=%async_computation.3 | async-start | bytes 2097152 | tf_op jit(solution)/shard_map/psum | solution.py:611
  113.5 4.7 collective-permute-start.4
  117.6 68.4 %copy-start.152 = (f32[256]{0:T(256)}, f32[256]{0:T(256)S(1)}, u32[]{:S(2)}) copy-start(f32[256]{0:T(256)S(1)} %compare_convert_fusion.1) | copy-start | bytes 3076
  124.6 122.6 %all-reduce.13.cloned.1.call-start = ((), (), s32[]{:S(2)}) async-start(), calls=%async_computation.4 | async-start | bytes 589824 | tf_op jit(solution)/shard_map/psum | solution.py:698
  125.2 7.1 collective-permute-start.8
  126.5 6.5 collective-permute-start.7
  127.8 6.2 collective-permute-start.6
  134.0 42.8 %copy-start.126 = (f32[1,1024]{1,0:T(1,128)S(1)}, f32[1,1024]{1,0:T(1,128)}, u32[]{:S(2)}) copy-start(f32[1,1024]{1,0:T(1,128)} %copy-done.125) | copy-start | bytes 12292
  178.2 5.8 collective-permute-start.5
  190.1 7.1 collective-permute-start.11
  191.4 6.9 collective-permute-start.10
  192.7 6.2 collective-permute-start.9
  211.4 236.4 %all-reduce.15.cloned.1.call-start = ((), (), s32[]{:S(2)}) async-start(), calls=%async_computation.6 | async-start | bytes 28639232 | tf_op jit(solution)/shard_map/psum | solution.py:745
  213.7 34.5 %copy-start.77 = (bf16[256,1024]{1,0:T(8,128)(2,1)S(1)}, bf16[256,1024]{1,0:T(8,128)(2,1)}, u32[]{:S(2)}) copy-start(bf16[256,1024]{1,0:T(8,128)(2,1)} %copy-done.76) | copy-start | bytes 1572868
  213.7 34.7 %copy-start.44 = (bf16[256,1024]{1,0:T(8,128)(2,1)S(1)}, bf16[256,1024]{1,0:T(8,128)(2,1)}, u32[]{:S(2)}) copy-start(bf16[256,1024]{1,0:T(8,128)(2,1)} %copy-done.43) | copy-start | bytes 1572868
  213.7 35.8 %copy-start.75 = (bf16[256,1024]{1,0:T(8,128)(2,1)S(1)}, bf16[256,1024]{1,0:T(8,128)(2,1)}, u32[]{:S(2)}) copy-start(bf16[256,1024]{1,0:T(8,128)(2,1)} %copy-done.74) | copy-start | bytes 1572868
  213.7 36.0 %copy-start.102 = (f32[256,128]{0,1:T(8,128)S(1)}, f32[256,128]{0,1:T(8,128)}, u32[]{:S(2)}) copy-start(f32[256,128]{0,1:T(8,128)} %copy-done.100) | copy-start | bytes 393220
  213.7 36.9 %copy-start.95 = (bf16[256,1024]{1,0:T(8,128)(2,1)S(1)}, bf16[256,1024]{1,0:T(8,128)(2,1)}, u32[]{:S(2)}) copy-start(bf16[256,1024]{1,0:T(8,128)(2,1)} %copy-done.94) | copy-start | bytes 1572868
  252.0 284.4 %all-gather.3.cloned.1.call-start = ((), (), s32[]{:S(2)}) async-start(), calls=%async_computation.5 | async-start | bytes 5242880 | tf_op jit(solution)/shard_map/all_gather | solution.py:811
  278.0 177.9 %copy-start.129 = (s32[288]{0:T(512)}, s32[288]{0:T(512)S(1)}, u32[]{:S(2)}) copy-start(s32[288]{0:T(512)S(1)} %convert_add_fusion.1) | copy-start | bytes 3460
  455.1 321.6 %all-reduce.17.cloned.1.call-start = ((), (), s32[]{:S(2)}) async-start(), calls=%async_computation.7 | async-start | bytes 13467648 | tf_op jit(solution)/shard_map/psum | solution.py:68
  472.0 23.5 %collective-permute-start.12 = (f32[1,1024]{1,0:T(1,128)S(1)}, f32[1,1024]{1,0:T(1,128)S(1)}, u32[]{:S(2)}, u32[]{:S(2)}) collective-permute-start(f32[1,1024]{1,0:T(1,128)S(1)} %broadcast_select_fusion.1), channel_id=1, source_target_pairs={{8,0},{12,4},{16,8},{20,12},{24,16},{28,20},{9,1},{13,5},{17,9},{2... | collective-permute-start | bytes 12296 | tf_op jit(solution)/shard_map/ppermute | solution.py:34
  473.9 428.5 %collective-permute-start.13 = (f32[1,1024]{1,0:T(1,128)}, f32[1,1024]{1,0:T(1,128)}, u32[]{:S(2)}, u32[]{:S(2)}) collective-permute-start(f32[1,1024]{1,0:T(1,128)} %broadcast_select_fusion), channel_id=1, source_target_pairs={{8,0},{12,4},{16,8},{20,12},{24,16},{28,20},{9,1},{13,5},{17,9},{2... | collective-permute-start | bytes 12296 | tf_op jit(solution)/shard_map/ppermute | solution.py:34
  684.9 334.3 %all-to-all-start = ((f32[8,128,256]{2,1,0:T(8,128)}), f32[8,128,256]{2,1,0:T(8,128)}, u32[]{:S(2)}, u32[]{:S(2)}) async-start(f32[8,128,256]{2,1,0:T(8,128)} %bitcast.70), calls=%async_computation | async-start | bytes 2097152 | tf_op jit(solution)/shard_map/all_to_all | solution.py:844
  905.9 29.7 %copy-start.170 = (f32[2,1024]{1,0:T(2,128)S(1)}, f32[2,1024]{1,0:T(2,128)}, u32[]{:S(2)}) copy-start(f32[2,1024]{1,0:T(2,128)} %param.50) | copy-start | bytes 24580
  905.9 30.1 %copy-start.171 = (f32[2,1024]{1,0:T(2,128)S(1)}, f32[2,1024]{1,0:T(2,128)}, u32[]{:S(2)}) copy-start(f32[2,1024]{1,0:T(2,128)} %param.51) | copy-start | bytes 24580
  905.9 30.4 %copy-start.149 = (f32[7,1024]{1,0:T(8,128)S(1)}, f32[7,1024]{1,0:T(8,128)}, u32[]{:S(2)}) copy-start(f32[7,1024]{1,0:T(8,128)} %param.49) | copy-start | bytes 86020
  905.9 30.8 %copy-start.69 = (f32[1,288,288]{2,1,0:T(8,128)S(1)}, f32[1,288,288]{2,1,0:T(8,128)}, u32[]{:S(2)}) copy-start(f32[1,288,288]{2,1,0:T(8,128)} %get-tuple-element.210) | copy-start | bytes 995332
  933.7 72.5 %copy-start.174 = (f32[256]{0:T(256)}, f32[256]{0:T(256)S(1)}, u32[]{:S(2)}) copy-start(f32[256]{0:T(256)S(1)} %get-tuple-element.349) | copy-start | bytes 3076
  934.1 75.2 %copy-start.175 = (f32[256]{0:T(256)}, f32[256]{0:T(256)S(1)}, u32[]{:S(2)}) copy-start(f32[256]{0:T(256)S(1)} %get-tuple-element.350) | copy-start | bytes 3076
  934.5 72.3 %copy-start.159 = (f32[3,256]{1,0:T(4,128)}, f32[3,256]{1,0:T(4,128)S(1)}, u32[]{:S(2)}) copy-start(f32[3,256]{1,0:T(4,128)S(1)} %get-tuple-element.347) | copy-start | bytes 9220
  934.9 72.6 %copy-start.160 = (f32[3,256]{1,0:T(4,128)}, f32[3,256]{1,0:T(4,128)S(1)}, u32[]{:S(2)}) copy-start(f32[3,256]{1,0:T(4,128)S(1)} %get-tuple-element.348) | copy-start | bytes 9220
  935.6 72.5 %copy-start.150 = (f32[2,1024]{1,0:T(2,128)}, f32[2,1024]{1,0:T(2,128)S(1)}, u32[]{:S(2)}) copy-start(f32[2,1024]{1,0:T(2,128)S(1)} %get-tuple-element.343) | copy-start | bytes 24580
  936.0 72.7 %copy-start.151 = (f32[2,1024]{1,0:T(2,128)}, f32[2,1024]{1,0:T(2,128)S(1)}, u32[]{:S(2)}) copy-start(f32[2,1024]{1,0:T(2,128)S(1)} %get-tuple-element.344) | copy-start | bytes 24580
  936.4 73.5 %copy-start.119 = (f32[7,1024]{1,0:T(8,128)}, f32[7,1024]{1,0:T(8,128)S(1)}, u32[]{:S(2)}) copy-start(f32[7,1024]{1,0:T(8,128)S(1)} %get-tuple-element.342) | copy-start | bytes 86020
  1019.2 53.9 %all-to-all-start.1 = ((f32[8,128,1024]{1,2,0:T(8,128)}), f32[8,128,1024]{1,2,0:T(8,128)}, u32[]{:S(2)}, u32[]{:S(2)}) async-start(f32[8,128,1024]{1,2,0:T(8,128)} %copy.178), calls=%async_computation.1 | async-start | bytes 8388608 | tf_op jit(solution)/shard_map/all_to_all | solution.py:844
  1038.2 35.0 %copy-start.93 = (f32[128,1024]{0,1:T(8,128)S(1)}, f32[128,1024]{0,1:T(8,128)}, u32[]{:S(2)}) copy-start(f32[128,1024]{0,1:T(8,128)} %copy.212) | copy-start | bytes 1572868
  1038.2 39.8 %copy-start.1 = (f32[2,4,64,64]{3,2,1,0:T(8,128)S(1)}, f32[2,4,64,64]{3,2,1,0:T(8,128)}, u32[]{:S(2)}) copy-start(f32[2,4,64,64]{3,2,1,0:T(8,128)} %param.34) | copy-start | bytes 393220
  1039.9 37.4 %copy-start.115 = (f32[2,4,64,64]{3,2,1,0:T(8,128)S(1)}, f32[2,4,64,64]{3,2,1,0:T(8,128)}, u32[]{:S(2)}) copy-start(f32[2,4,64,64]{3,2,1,0:T(8,128)} %get-tuple-element.328) | copy-start | bytes 393220
  (172 other events, 1340.2 us)
Sparse Core Ops, SparseCore 0:
  56.8 54.4 all-reduce.8
  124.8 52.0 all-reduce.10
  211.5 35.6 all-reduce.12
  253.7 193.9 all-reduce.14
  455.2 81.2 all-gather.2
  539.7 236.9 all-reduce.16

commit v2 on v1

--- a/solution.py
+++ b/solution.py
@@ -418,47 +418,737 @@
     )(*operands)
 
 
-def cheap(left, right):
-    return jnp.dot(left.astype(BF), right.astype(BF), preferred_element_type=F32)
+TILE = 256
+
+
+def store_split(refs, span, value):
+    high = value.astype(BF)
+    refs[0][span] = high
+    if len(refs) > 1:
+        refs[1][span] = (value - high.astype(F32)).astype(BF)
+
+
+def over_tiles(rows, body, start=None):
+    tile = min(TILE, rows)
+    carry = jnp.zeros((1, 1), F32) if start is None else start
+    step = lambda index, total: body(pl.ds(pl.multiple_of(index * tile, tile), tile), index * tile, total)
+    return lax.fori_loop(0, rows // tile, step, carry, unroll=math.gcd(2, rows // tile))
+
+
+def tile_dot(left, span, right, kind):
+    total = dot_kind(left[0][span], right[0][...], kind)
+    if len(left) > 1:
+        total = total + dot_kind(left[0][span], right[1][...], kind)
+        total = total + dot_kind(left[1][span], right[0][...], kind)
+    return total
+
+
+def total_of(value):
+    return jnp.sum(jnp.sum(value, axis=0, keepdims=True), axis=1, keepdims=True)
+
+
+def diagonal(shape, first_row):
+    rows = lax.broadcasted_iota(jnp.int32, shape, 0) + first_row
+    return rows == lax.broadcasted_iota(jnp.int32, shape, 1)
+
+
+def expansion(shift):
+    value = COEFF_A + COEFF_B * shift + COEFF_C * shift * shift
+    return value, COEFF_B + 2.0 * COEFF_C * shift
+
+
+def newton_square_kernel(
+    coarse, active_ref, x_ref, out_ref, x_high, x_low, d_high, d_low, b_high, b_low, rest_ref
+):
+    rows = out_ref.shape[0]
+    parts, halves, half_rows, width = x_ref.shape
+
+    def advance(step, norm, fine):
+        now = step % 2
+        xs, fresh_xs = [(x_high.at[index], x_low.at[index]) for index in (now, 1 - now)]
+        ds, bs = (d_high, d_low), (b_high, b_low)
+        if not fine:
+            xs, ds, bs = xs[:1], ds[:1], bs[:1]
+        shift = norm * (1.0 / rows)
+        value, slope = expansion(shift)
+
+        def gram(span, first, total):
+            product = tile_dot(xs, span, xs, "nt")
+            rest = jnp.where(diagonal(product.shape, first), product - shift, product)
+            rest_ref[span] = rest
+            store_split(ds, span, rest)
+            return total
+
+        def terms(span, first, total):
+            store_split(bs, span, slope * rest_ref[span] + COEFF_C * tile_dot(ds, span, ds, "nn"))
+            return total
+
+        def update(span, first, total):
+            fresh = value * out_ref[span] + tile_dot(bs, span, xs, "nn")
+            out_ref[span] = fresh
+            store_split(fresh_xs, span, fresh)
+            return total + total_of(jnp.square(fresh))
+
+        over_tiles(rows, gram)
+        over_tiles(rows, terms)
+        return over_tiles(rows, update)
+
+    def iterate():
+        def begin(span, first, total):
+            for half in range(halves):
+                for part in range(parts):
+                    tile = x_ref[part, half, span]
+                    place = pl.ds(
+                        pl.multiple_of(half * half_rows + first, min(TILE, half_rows)), tile.shape[0]
+                    )
+                    out_ref[place, part * width : (part + 1) * width] = tile
+                    total = total + total_of(jnp.square(tile))
+            return total
+
+        norm = over_tiles(half_rows, begin)
+        scale = 1.0 / (jnp.sqrt(norm) + 1e-07)
+
+        def normalise(span, first, total):
+            fresh = out_ref[span] * scale
+            out_ref[span] = fresh
+            store_split((x_high.at[0], x_low.at[0]), span, fresh)
+            return total
+
+        over_tiles(rows, normalise)
+        norm = norm * scale * scale
+        norm = lax.fori_loop(0, coarse, lambda step, norm: advance(step, norm, False), norm)
+        lax.fori_loop(coarse, NS_STEPS, lambda step, norm: advance(step, norm, True), norm)
+
+    pl.when(active_ref[0] > 0)(iterate)
+
+
+def newton_wide_kernel(
+    coarse, active_ref, gram_ref, key_ref, value_ref, out_ref,
+    x_high, d_high, d_low, b_high, b_low, r_high, r_low, a_ref, terms_ref, square_ref,
+):
+    rows = key_ref.shape[0]
+
+    def trace_of(tile, first):
+        return total_of(jnp.where(diagonal(tile.shape, first), tile, 0.0))
+
+    def without(tile, first, shift):
+        return jnp.where(diagonal(tile.shape, first), tile - shift, tile)
+
+    def advance(step, trace, fine, last=False):
+        now = step % 2
+        xs, fresh_xs = (x_high.at[now],), (x_high.at[1 - now],)
+        ds, bs, rs = (d_high, d_low), (b_high, b_low), (r_high, r_low)
+        if not fine:
+            ds, bs, rs = ds[:1], bs[:1], rs[:1]
+        shift = trace * (1.0 / rows)
+        value, slope = expansion(shift)
+
+        def terms(span, first, total):
+            fresh = slope * without(a_ref[span], first, shift)
+            fresh = fresh + COEFF_C * tile_dot(ds, span, ds, "nn")
+            terms_ref[span] = fresh
+            store_split(bs, span, fresh)
+            return total
+
+        def update(span, first, total):
+            fresh = value * out_ref[span] + tile_dot(bs[:1], span, xs, "nn")
+            out_ref[span] = fresh
+            if not last:
+                store_split(fresh_xs, span, fresh)
+            return total
+
+        def square(span, first, total):
+            fresh = 2.0 * value * terms_ref[span] + tile_dot(bs, span, bs, "nn")
+            square_ref[span] = fresh
+            store_split(rs, span, fresh)
+            return total + total_of(fresh * a_ref[span])
+
+        over_tiles(rows, terms)
+        over_tiles(rows, update)
+        if last:
+            return trace
+        fresh_trace = value * value * trace + over_tiles(rows, square)
+        fresh_shift = fresh_trace * (1.0 / rows)
+
+        def move(span, first, total):
+            fresh = value * value * a_ref[span] + shift * square_ref[span]
+            fresh = fresh + tile_dot(ds, span, rs, "nn")
+            a_ref[span] = fresh
+            store_split((d_high, d_low), span, without(fresh, first, fresh_shift))
+            return total
+
+        over_tiles(rows, move)
+        return fresh_trace
+
+    def iterate():
+        trace = over_tiles(rows, lambda span, first, total: total + trace_of(gram_ref[span], first))
+        scale = 1.0 / (jnp.sqrt(trace) + 1e-07)
+        trace = trace * scale * scale
+        first_shift = trace * (1.0 / rows)
+
+        def begin(span, first, total):
+            @pl.when(active_ref[0] == 1)
+            def _():
+                out_ref[span] = key_ref[span]
+
+            @pl.when(active_ref[0] == 2)
+            def _():
+                out_ref[span] = value_ref[:, span].T
+
+            fresh = out_ref[span] * scale
+            out_ref[span] = fresh
+            store_split((x_high.at[0],), span, fresh)
+            tile = gram_ref[span] * (scale * scale)
+            a_ref[span] = tile
+            store_split((d_high, d_low), span, without(tile, first, first_shift))
+            return total
+
+        over_tiles(rows, begin)
+        trace = lax.fori_loop(0, coarse, lambda step, trace: advance(step, trace, False), trace)
+        trace = lax.fori_loop(
+            coarse, NS_STEPS - 1, lambda step, trace: advance(step, trace, True), trace
+        )
+        advance(NS_STEPS - 1, trace, False, True)
+
+    pl.when(active_ref[0] > 0)(iterate)
+
+
+def newton_call(body, active, operands, result_shape, scratch):
+    return pl.pallas_call(
+        body,
+        out_shape=jax.ShapeDtypeStruct(result_shape, F32),
+        in_specs=[pl.BlockSpec(memory_space=pltpu.SMEM)]
+        + [pl.BlockSpec(memory_space=pltpu.VMEM)] * len(operands),
+        out_specs=pl.BlockSpec(memory_space=pltpu.VMEM),
+        scratch_shapes=[pltpu.VMEM(shape, dtype) for shape, dtype in scratch],
+        cost_estimate=pl.CostEstimate(
+            flops=2 * 30 * result_shape[0] ** 2 * result_shape[1],
+            bytes_accessed=8 * result_shape[0] * result_shape[1],
+            transcendentals=0,
+        ),
+        compiler_params=pltpu.CompilerParams(vmem_limit_bytes=58 * 1024 * 1024),
+    )(active.astype(jnp.int32).reshape(1), *operands)
+
+
+def newton_square(active, whole):
+    shape = (whole.shape[1] * whole.shape[2], whole.shape[0] * whole.shape[3])
+    scratch = [((2, *shape), BF)] * 2 + [(shape, BF)] * 4 + [(shape, F32)]
+    return newton_call(
+        functools.partial(newton_square_kernel, 3), active, (whole,), shape, scratch
+    )
+
+
+def newton_wide(active, gram, key, value):
+    part = key
+    scratch = [((2, *part.shape), BF)] + [(gram.shape, BF)] * 6 + [(gram.shape, F32)] * 3
+    return newton_call(
+        functools.partial(newton_wide_kernel, 2), active, (gram, key, value), part.shape, scratch
+    )
+
+
+LOWRANK_PASSES = (1, 3, 3, 3, 3)
+
+
+def newton_small_kernel(active_ref, gram_ref, member_ref, out_ref):
+    def iterate():
+        member = member_ref[...]
+        rows = lax.broadcasted_iota(jnp.int32, member.shape, 0)
+        eye = (rows == lax.broadcasted_iota(jnp.int32, member.shape, 1)).astype(F32)
+        sizes = jnp.maximum(jnp.sum(member, axis=1, keepdims=True), 1.0)
+
+        def block_total(gram):
+            return jnp.sum(jnp.sum(gram * eye, axis=0, keepdims=True) * member, axis=1, keepdims=True)
+
+        def dot(a, b, fine):
+            a_high, a_low = split(a)
+            b_high, b_low = split(b)
+            total = dot_kind(a_high, b_high, "nn")
+            if fine:
+                total = total + (dot_kind(a_high, b_low, "nn") + dot_kind(a_low, b_high, "nn"))
+            return total
+
+        grams, currents = [], []
+        for index in range(gram_ref.shape[0]):
+            gram = gram_ref[index] * member
+            scale = 1.0 / (jnp.sqrt(block_total(gram)) + 1e-07)
+            grams.append(gram * (scale * scale))
+            currents.append(eye * scale)
+        for step in range(NS_STEPS):
+            fine = LOWRANK_PASSES[step] > 1
+            for index, gram in enumerate(grams):
+                shift = block_total(gram) / sizes
+                value, slope = expansion(shift)
+                rest = gram - shift * eye
+                terms = slope * rest + COEFF_C * dot(rest, rest, fine)
+                currents[index] = value * currents[index] + dot(terms, currents[index], fine)
+                if step < NS_STEPS - 1:
+                    square = 2.0 * value * terms + dot(terms, terms, fine)
+                    grams[index] = value * value * gram + shift * square + dot(rest, square, fine)
+        for index, current in enumerate(currents):
+            out_ref[index] = current
+
+    pl.when(active_ref[0] > 0)(iterate)
+
+
+def newton_small(active, gram, member):
+    return pl.pallas_call(
+        newton_small_kernel,
+        out_shape=jax.ShapeDtypeStruct(gram.shape, F32),
+        in_specs=[pl.BlockSpec(memory_space=pltpu.SMEM)]
+        + [pl.BlockSpec(memory_space=pltpu.VMEM)] * 2,
+        out_specs=pl.BlockSpec(memory_space=pltpu.VMEM),
+        cost_estimate=pl.CostEstimate(
+            flops=2 * 100 * gram.shape[1] ** 3, bytes_accessed=0, transcendentals=0
+        ),
+        compiler_params=pltpu.CompilerParams(vmem_limit_bytes=48 * 1024 * 1024),
+    )(active.astype(jnp.int32).reshape(1), gram, member)
+
+
+MESH = pl.DeviceIdType.MESH
+
+
+def greet(neighbours):
+    barrier = pltpu.get_barrier_semaphore()
+    for there, device in neighbours:
+        @pl.when(there)
+        def _():
+            pl.semaphore_signal(barrier, inc=1, device_id=device, device_id_type=MESH)
+
+    pl.semaphore_wait(barrier, sum(jnp.where(there, 1, 0) for there, _ in neighbours))
+
+
+def line_sum_kernel(count, pieces, *refs):
+    me = lax.axis_index("head")
+    greet([(me > 0, {"head": me - 1}), (me < count - 1, {"head": me + 1})])
+    line_sum_body(count, pieces, *refs)
+
+
+def line_sum_body(
+    count, pieces, x_ref, out_ref, right_in, left_in, right_out, left_out,
+    right_send, right_recv, left_send, left_recv, on_send, on_recv, back_send, back_recv,
+):
+    me = lax.axis_index("head")
+    rows = x_ref.shape[0] // (count * pieces)
+    right, left = {"head": me + 1}, {"head": me - 1}
+
+    def span(slot):
+        return pl.ds(pl.multiple_of(slot * rows, rows), rows)
+
+    def reduce_copy(slot, to_right, source):
+        arrive, send, recv, device = (
+            (right_in, right_send, right_recv, right)
+            if to_right
+            else (left_in, left_send, left_recv, left)
+        )
+        return pltpu.make_async_remote_copy(
+            src_ref=source, dst_ref=arrive.at[slot], send_sem=send.at[slot],
+            recv_sem=recv.at[slot], device_id=device, device_id_type=MESH,
+        )
+
+    def share_copy(slot, to_right):
+        send, recv, device = (on_send, on_recv, right) if to_right else (back_send, back_recv, left)
+        return pltpu.make_async_remote_copy(
+            src_ref=out_ref.at[span(slot)], dst_ref=out_ref.at[span(slot)], send_sem=send.at[slot],
+            recv_sem=recv.at[slot], device_id=device, device_id_type=MESH,
+        )
+
+    def pass_on(slot, to_right, first):
+        arrive, leave = (right_in, right_out) if to_right else (left_in, left_out)
+
+        @pl.when(first)
+        def _():
+            reduce_copy(slot, to_right, x_ref.at[span(slot)]).start()
+
+        @pl.when(jnp.logical_not(first))
+        def _():
+            reduce_copy(slot, to_right, x_ref.at[span(slot)]).wait_recv()
+            leave[slot] = x_ref[span(slot)] + arrive[slot]
+            reduce_copy(slot, to_right, leave.at[slot]).start()
+
+    for far in range(count - 1):
+        for piece in range(pieces):
+            owner = count - 1 - far
+
+            @pl.when(me < owner)
+            def _():
+                pass_on(owner * pieces + piece, True, me == 0)
+
+            @pl.when(me > far)
+            def _():
+                pass_on(far * pieces + piece, False, me == count - 1)
+
+    for piece in range(pieces):
+        slot = me * pieces + piece
+        out_ref[span(slot)] = x_ref[span(slot)]
+
+        @pl.when(me > 0)
+        def _():
+            reduce_copy(slot, True, x_ref.at[span(slot)]).wait_recv()
+            out_ref[span(slot)] += right_in[slot]
+
+        @pl.when(me < count - 1)
+        def _():
+            reduce_copy(slot, False, x_ref.at[span(slot)]).wait_recv()
+            out_ref[span(slot)] += left_in[slot]
+            share_copy(slot, True).start()
+
+        @pl.when(me > 0)
+        def _():
+            share_copy(slot, False).start()
+
+    for far in range(1, count):
+        for piece in range(pieces):
+            @pl.when(me >= far)
+            def _():
+                copy = share_copy((me - far) * pieces + piece, True)
+                copy.wait_recv()
+                pl.when(me < count - 1)(copy.start)
+
+            @pl.when(me + far < count)
+            def _():
+                copy = share_copy((me + far) * pieces + piece, False)
+                copy.wait_recv()
+                pl.when(me > 0)(copy.start)
+
+    for slot in range(count * pieces):
+        owner = slot // pieces
+        pl.when(me < owner)(lambda: reduce_copy(slot, True, x_ref.at[span(slot)]).wait_send())
+        pl.when(me > owner)(lambda: reduce_copy(slot, False, x_ref.at[span(slot)]).wait_send())
+        pl.when((owner <= me) & (me < count - 1))(lambda: share_copy(slot, True).wait_send())
+        pl.when((owner >= me) & (me > 0))(lambda: share_copy(slot, False).wait_send())
+
+
+def line_sum(value, collective_id, pieces=2):
+    count = lax.axis_size("head")
+    slots = count * pieces
+    buffer = pltpu.VMEM((slots, value.shape[0] // slots, value.shape[1]), F32)
+    return pl.pallas_call(
+        functools.partial(line_sum_kernel, count, pieces),
+        out_shape=jax.ShapeDtypeStruct(value.shape, F32),
+        in_specs=[pl.BlockSpec(memory_space=pltpu.VMEM)],
+        out_specs=pl.BlockSpec(memory_space=pltpu.VMEM),
+        scratch_shapes=[buffer] * 4 + [pltpu.SemaphoreType.DMA((slots,))] * 8,
+        compiler_params=pltpu.CompilerParams(collective_id=collective_id, has_side_effects=True),
+    )(value)
+
+
+def plane_places():
+    me = lax.axis_index("seq")
+    core = me % 2
+    return me // 2, core, {"seq": me + 1 - 2 * core}, lambda pair: {"seq": 2 * pair + core}
+
+
+def plane_reduce_steps(pairs, x_ref, out_ref, near_in, total_ref, far_in, near_send, near_recv, far_send, far_recv):
+    pair, core, partner, like = plane_places()
+    order = [(pair + step) % pairs for step in range(1, pairs)]
+
+    def near(part):
+        return pltpu.make_async_remote_copy(
+            src_ref=x_ref.at[part, 1 - core], dst_ref=near_in.at[part], send_sem=near_send.at[part],
+            recv_sem=near_recv.at[part], device_id=partner, device_id_type=MESH,
+        )
+
+    def far(part, source):
+        return pltpu.make_async_remote_copy(
+            src_ref=total_ref.at[part], dst_ref=far_in.at[source], send_sem=far_send.at[part],
+            recv_sem=far_recv.at[source], device_id=like(part), device_id_type=MESH,
+        )
+
+    def begin():
+        for part in order + [pair]:
+            near(part).start()
+        for part in order:
+            near(part).wait_recv()
+            total_ref[part] = x_ref[part, core] + near_in[part]
+            far(part, pair).start()
+        near(pair).wait_recv()
+        out_ref[...] = x_ref[pair, core] + near_in[pair]
+
+    def finish():
+        for source in order:
+            far(source, source).wait_recv()
+            out_ref[...] += far_in[source]
+        for part in order + [pair]:
+            near(part).wait_send()
+        for part in order:
+            far(part, pair).wait_send()
+
+    return begin, finish
+
+
+def greet_all(pairs, neighbours):
+    pair, core, partner, like = plane_places()
+    always = pair >= 0
+    plane = [(always, partner)]
+    plane += [(always, like((pair + far) % pairs)) for far in range(1, pairs)]
+    greet(plane + neighbours)
+
+
+def reduce_and_sum_kernel(pairs, count, pieces, parts_ref, line_ref, own_ref, sum_ref, *scratch):
+    line = lax.axis_index("head")
+    greet_all(
+        pairs, [(line > 0, {"head": line - 1}), (line < count - 1, {"head": line + 1})]
+    )
+    begin, finish = plane_reduce_steps(pairs, parts_ref, own_ref, *scratch[:7])
+    begin()
+    line_sum_body(count, pieces, line_ref, sum_ref, *scratch[7:])
+    finish()
+
+
+def reduce_and_sum(parts, line_value, collective_id, pieces=2):
+    pairs, shape = parts.shape[0], parts.shape[2:]
+    count = lax.axis_size("head")
+    slots = count * pieces
+    rows, columns = line_value.shape
+    return pl.pallas_call(
+        functools.partial(reduce_and_sum_kernel, pairs, count, pieces),
+        out_shape=(
+            jax.ShapeDtypeStruct(shape, F32),
+            jax.ShapeDtypeStruct(line_value.shape, F32),
+        ),
+        in_specs=[pl.BlockSpec(memory_space=pltpu.VMEM)] * 2,
+        out_specs=(pl.BlockSpec(memory_space=pltpu.VMEM), pl.BlockSpec(memory_space=pltpu.VMEM)),
+        scratch_shapes=[pltpu.VMEM((pairs, *shape), F32)] * 3
+        + [pltpu.SemaphoreType.DMA((pairs,))] * 4
+        + [pltpu.VMEM((slots, rows // slots, columns), F32)] * 4
+        + [pltpu.SemaphoreType.DMA((slots,))] * 8,
+        compiler_params=pltpu.CompilerParams(
+            collective_id=collective_id, has_side_effects=True, vmem_limit_bytes=48 * 1024 * 1024
+        ),
+    )(parts, line_value)
+
+
+def share_gather_kernel(
+    pairs, count, pieces, square_ref, small_ref, gram_ref, shared_ref, whole_ref, full_ref,
+    out_send, in_recv, back_send, back_recv, half_send, half_recv, gram_send, gram_recv,
+    right_send, right_recv, left_send, left_recv, local_sem,
+):
+    pair, core, partner, like = plane_places()
+    line = lax.axis_index("head")
+    right, left = {"head": line + 1}, {"head": line - 1}
+    half_rows = square_ref.shape[0]
+    rows = half_rows // pieces
+    gathers = core == 0
+    owners = min(pairs, 4)
+    kind = pair % 2
+    slot = (pair // 2) * 2 + core
+    takes = (core == 1) & (pair < owners)
+
+    def odd(other):
+        return {"seq": 2 * other + 1}
+
+    def even(other):
+        return {"seq": 2 * other}
+
+    neighbours = [(gathers & (line > 0), left), (gathers & (line < count - 1), right)]
+    for step in range(owners // 2):
+        target = kind + 2 * step
+        neighbours.append(((core == 0) & (target != pair), odd(target)))
+    for step in range(pairs // 2):
+        source = kind + 2 * step
+        neighbours.append((takes & (source != pair), even(source)))
+    greet_all(pairs, neighbours)
+
+    def gram_copy(source_slot, target):
+        return pltpu.make_async_remote_copy(
+            src_ref=gram_ref, dst_ref=full_ref.at[source_slot], send_sem=gram_send.at[target // 2],
+            recv_sem=gram_recv.at[source_slot], device_id=odd(target), device_id_type=MESH,
+        )
+
+    def half_copy():
+        return pltpu.make_async_remote_copy(
+            src_ref=square_ref, dst_ref=whole_ref.at[line, 1], send_sem=half_send.at[0],
+            recv_sem=half_recv.at[0], device_id=partner, device_id_type=MESH,
+        )
+
+    def out_copy(part):
+        return pltpu.make_async_remote_copy(
+            src_ref=small_ref, dst_ref=shared_ref.at[pair, core], send_sem=out_send.at[part],
+            recv_sem=in_recv.at[pair], device_id=like(part), device_id_type=MESH,
+        )
+
+    def in_copy(source):
+        return pltpu.make_async_remote_copy(
+            src_ref=small_ref, dst_ref=shared_ref.at[source, core], send_sem=out_send.at[source],
+            recv_sem=in_recv.at[source], device_id=like(source), device_id_type=MESH,
+        )
+
+    def partner_copy(source, side, source_ref):
+        return pltpu.make_async_remote_copy(
+            src_ref=source_ref, dst_ref=shared_ref.at[source, side], send_sem=back_send.at[source],
+            recv_sem=back_recv.at[source], device_id=partner, device_id_type=MESH,
+        )
+
+    def span(piece):
+        return pl.ds(piece * rows, rows)
+
+    def line_copy(owner, half, piece, to_right, source):
+        send, recv, device = (
+            (right_send, right_recv, right) if to_right else (left_send, left_recv, left)
+        )
+        return pltpu.make_async_remote_copy(
+            src_ref=source, dst_ref=whole_ref.at[owner, half, span(piece)],
+            send_sem=send.at[owner, half, piece], recv_sem=recv.at[owner, half, piece],
+            device_id=device, device_id_type=MESH,
+        )
+
+    order = [(pair + step) % pairs for step in range(1, pairs)]
+    pl.when(core == 1)(lambda: half_copy().start())
+    for step in range(owners // 2):
+        target = kind + 2 * step
+        pl.when((core == 0) | (target != pair))(lambda: gram_copy(slot, target).start())
+    for part in order:
+        out_copy(part).start()
+    partner_copy(pair, core, small_ref).start()
+    shared_ref[pair, core] = small_ref[...]
+    own_gram = pltpu.make_async_copy(gram_ref, full_ref.at[slot], local_sem)
+    pl.when(takes)(own_gram.start)
+
+    def gather():
+        whole_ref[line, 0] = square_ref[...]
+        half_copy().wait_recv()
+        for half in range(2):
+            for piece in range(pieces):
+                own = whole_ref.at[line, half, span(piece)]
+                pl.when(line < count - 1)(lambda: line_copy(line, half, piece, True, own).start())
+                pl.when(line > 0)(lambda: line_copy(line, half, piece, False, own).start())
+        for far in range(1, count):
+            for half in range(2):
+                for piece in range(pieces):
+                    for there, end, owner, to_right in (
+                        (line >= far, line == count - 1, line - far, True),
+                        (line + far < count, line == 0, line + far, False),
+                    ):
+                        @pl.when(there)
+                        def _():
+                            copy = line_copy(
+                                owner, half, piece, to_right, whole_ref.at[owner, half, span(piece)]
+                            )
+                            copy.wait_recv()
+                            pl.when(jnp.logical_not(end))(copy.start)
+
+        for owner in range(count):
+            for half in range(2):
+                for piece in range(pieces):
+                    sent = whole_ref.at[owner, half, span(piece)]
+                    pl.when((owner <= line) & (line < count - 1))(
+                        lambda: line_copy(owner, half, piece, True, sent).wait_send()
+                    )
+                    pl.when((owner >= line) & (line > 0))(
+                        lambda: line_copy(owner, half, piece, False, sent).wait_send()
+                    )
+
+    pl.when(gathers)(gather)
+    for source in order:
+        in_copy(source).wait_recv()
+        partner_copy(source, core, shared_ref.at[source, core]).start()
+
+    def take():
+        own_gram.wait()
+        for step in range(pairs // 2):
+            for side in range(2):
+                source = kind + 2 * step
+                pl.when((side == 0) | (source != pair))(
+                    lambda: gram_copy(2 * step + side, pair).wait_recv()
+                )
+
+    pl.when(takes)(take)
+    for source in order + [pair]:
+        partner_copy(source, 1 - core, small_ref).wait_recv()
+    for source in order + [pair]:
+        partner_copy(source, core, small_ref).wait_send()
+    for part in order:
+        out_copy(part).wait_send()
+    pl.when(core == 1)(lambda: half_copy().wait_send())
+    for step in range(owners // 2):
+        target = kind + 2 * step
+        pl.when((core == 0) | (target != pair))(lambda: gram_copy(slot, target).wait_send())
+
+
+def share_gather(square, small, gram, collective_id, pieces=2):
+    pairs, count = lax.axis_size("seq") // 2, lax.axis_size("head")
+    slots = (count, 2, pieces)
+    results = ((pairs, 2, *small.shape), (count, 2, *square.shape), (pairs, *gram.shape))
+    dma = pltpu.SemaphoreType.DMA
+    return pl.pallas_call(
+        functools.partial(share_gather_kernel, pairs, count, pieces),
+        out_shape=tuple(jax.ShapeDtypeStruct(shape, F32) for shape in results),
+        in_specs=[pl.BlockSpec(memory_space=pltpu.VMEM)] * 3,
+        out_specs=tuple(pl.BlockSpec(memory_space=pltpu.VMEM) for _ in results),
+        scratch_shapes=[dma((pairs,))] * 4 + [dma((1,))] * 2 + [dma((2,)), dma((pairs,))]
+        + [dma(slots)] * 4 + [dma],
+        compiler_params=pltpu.CompilerParams(
+            collective_id=collective_id, has_side_effects=True, vmem_limit_bytes=48 * 1024 * 1024
+        ),
+    )(square, small, gram)
+
+
+def gram_part_kernel(which_ref, key_ref, value_ref, out_ref):
+    rows = out_ref.shape[0]
+    start = pl.multiple_of(which_ref[1] * rows, rows)
+
+    def three(left, right, kind):
+        left, right = split(left), split(right)
+        total = dot_kind(left[0], right[0], kind)
+        return total + (dot_kind(left[0], right[1], kind) + dot_kind(left[1], right[0], kind))
+
+    @pl.when(which_ref[0] == 0)
+    def _():
+        out_ref[...] = three(key_ref[pl.ds(start, rows)], key_ref[...], "nt")
+
+    @pl.when(which_ref[0] == 1)
+    def _():
+        out_ref[...] = three(value_ref[:, pl.ds(start, rows)], value_ref[...], "tn")
+
+
+def gram_rows(kind, part, parts, key, value):
+    return pl.pallas_call(
+        gram_part_kernel,
+        out_shape=jax.ShapeDtypeStruct((key.shape[0] // parts, key.shape[0]), F32),
+        in_specs=[pl.BlockSpec(memory_space=pltpu.SMEM)]
+        + [pl.BlockSpec(memory_space=pltpu.VMEM)] * 2,
+        out_specs=pl.BlockSpec(memory_space=pltpu.VMEM),
+        compiler_params=pltpu.CompilerParams(vmem_limit_bytes=48 * 1024 * 1024),
+    )(jnp.stack([kind, part]).astype(jnp.int32), key, value)
+
+
+def exact(left, right):
+    return jnp.matmul(left, right, precision=HIGHEST, preferred_element_type=F32)
 
 
 def close(left, right):
     return jnp.dot(left, right, precision=lax.Precision.HIGH, preferred_element_type=F32)
 
 
-def exact(left, right):
-    return jnp.matmul(left, right, precision=HIGHEST, preferred_element_type=F32)
-
-
-def shifted_terms(gram, shift, dot):
-    rest = gram - shift * jnp.eye(gram.shape[-1], dtype=F32)
-    value = COEFF_A + COEFF_B * shift + COEFF_C * shift * shift
-    return value, (COEFF_B + 2.0 * COEFF_C * shift) * rest + COEFF_C * dot(rest, rest), rest
-
-
-def newton_whole(current):
-    for step in range(NS_STEPS):
-        dot = cheap if step < 3 else close
-        gram = dot(current, current.T)
-        shift = jnp.trace(gram) / gram.shape[0]
-        value, terms, _ = shifted_terms(gram, shift, dot)
-        current = value * current + dot(terms, current)
-    return current
-
-
-def gram_next(gram, shift, value, terms, rest, dot):
-    square = 2.0 * value * terms + dot(terms, terms)
-    return value * value * gram + shift * square + dot(rest, square)
-
-
-def newton_grams(current, gram, shift_of, dots, applies):
-    for step in range(NS_STEPS):
-        shift = shift_of(gram)
-        value, terms, rest = shifted_terms(gram, shift, dots[step])
-        current = value * current + applies[step](terms, current)
-        if step < NS_STEPS - 1:
-            gram = gram_next(gram, shift, value, terms, rest, dots[step])
-    return current
+def after(value, *others):
+    return lax.optimization_barrier((value, *others))[0]
+
+
+def pair_swap(value):
+    count = lax.axis_size("seq")
+    return lax.ppermute(value, "seq", [(index, index ^ 1) for index in range(count)])
+
+
+def pair_halves(value, core):
+    mine = lax.dynamic_index_in_dim(value, core, 0, keepdims=False)
+    other = lax.dynamic_index_in_dim(value, 1 - core, 0, keepdims=False)
+    return mine + pair_swap(other)
+
+
+def pair_whole(mine, core):
+    other = pair_swap(mine)
+    first = core == 0
+    return jnp.stack([jnp.where(first, mine, other), jnp.where(first, other, mine)])
+
+
+def across_pairs(value):
+    count = lax.axis_size("seq")
+    groups = [list(range(core, count, 2)) for core in range(2)]
+    return lax.all_to_all(value, "seq", 0, 0, tiled=True, axis_index_groups=groups)
+
+
+def to_all_pairs(value, pairs):
+    return across_pairs(jnp.broadcast_to(value[None], (pairs, *value.shape)))
 
 
 def on_device(
@@ -585,7 +1275,7 @@
         + (attention_scale_lines, attention_offset_lines, reward_row),
     )
     out_low = emission_coeffs.astype(jnp.bfloat16)
-    attended = inputs + head_total(product(adapter_result, out_low))
+    attended = inputs + line_sum(product(adapter_result, out_low), 1)
     normed_two, second_pull = jax.vjp(
         layer_norm, attended, standardize_scales[1], standardize_offsets[1]
     )
@@ -598,8 +1288,6 @@
     values_low = feedforward_content_coeffs.astype(jnp.bfloat16)
     hidden_ffn = product(key_in, keys_low)
     activated = jnp.square(jax.nn.relu(hidden_ffn)).astype(jnp.bfloat16)
-    result = attended + head_total(product(activated, values_low))
-    block_output = (result * live).astype(jnp.bfloat16)
     grad_result = loss_adjoint.astype(jnp.float32) * live
     grad_low = grad_result.astype(jnp.bfloat16)
     grad_ffnvalue = inner_rows(activated, grad_low)
@@ -607,8 +1295,11 @@
         jnp.bfloat16
     )
     grad_ffnkey = inner_rows(key_in, grad_hidden)
+    pairs, core, pair = seq_count // 2, seq_index % 2, seq_index // 2
+    hidden_units = grad_ffnkey.shape[1]
+    keyin_part = after(outer_back(grad_hidden, keys_low), grad_ffnkey, grad_ffnvalue)
     grad_ffnkey, grad_ffnvalue = lax.psum((grad_ffnkey, grad_ffnvalue), "seq")
-    grad_keyin = lax.psum(outer_back(grad_hidden, keys_low), "head")
+    grad_keyin = line_sum(keyin_part, 1)
     carry_two = grad_keyin * lagged_blend_coeffs[6]
     grad_normed_two = (
         grad_keyin
@@ -618,7 +1309,6 @@
     grad_attended, grad_gain_two, grad_bias_two = second_pull(grad_normed_two)
     grad_attended = grad_attended + grad_result
     grad_attended_low = grad_attended.astype(jnp.bfloat16)
-    grad_output = inner_rows(adapter_result, grad_attended_low)
     grad_branch = outer_back(grad_attended_low, out_low)
     (
         state_local,
@@ -663,11 +1353,12 @@
     reward_loss_slope = sums_a[2]
     grad_decay = sums_b[4]
     grad_lift_low = [grad_up_w, grad_up_a, grad_up_v, grad_gate]
-    grad_project = jnp.stack(
+    square_grads = jnp.stack(
         [
             inner_rows(mixes[0], grad_rec_low),
             inner_rows(mixes[2], grad_key_low),
             inner_rows(mixes[3], grad_value_low),
+            inner_rows(grad_attended_low, adapter_result),
         ]
     )
     grad_up = jnp.concatenate(
@@ -695,11 +1386,24 @@
         ],
         axis=1,
     )
-    acts_sum, shift_sum = lax.psum((acts_part, shift_part), "head")
+    spare = (-acts_part.shape[1]) % 128
+    shift_columns = shift_part.size // overall_tally
+    acts_packed = jnp.concatenate(
+        [
+            acts_part,
+            shift_part.reshape(overall_tally, shift_columns),
+            jnp.zeros((overall_tally, spare - shift_columns), F32),
+        ],
+        axis=1,
+    )
     normed_part = norm_part + jnp.concatenate(
         [prev_part[1:], from_after(prev_part[:1], is_first, stride)], axis=0
     )
-    norm_sum = lax.psum(normed_part, "head")
+    acts_packed = line_sum(jnp.concatenate([acts_packed, normed_part], axis=1), 2)
+    norm_sum = acts_packed[:, -EMBED_SIZE:]
+    acts_sum = acts_packed[:, : acts_part.shape[1]]
+    shift_sum = acts_packed[:, acts_part.shape[1] : acts_part.shape[1] + shift_columns]
+    shift_sum = shift_sum.reshape(shift_part.shape)
     act_grads = [acts_sum[:, start_index:stop_index] for start_index, stop_index in sequence_spans]
     grad_hidden_low = [
         (act_grads[0] * (1.0 - tanh_w * tanh_w)).astype(jnp.bfloat16),
@@ -708,7 +1412,7 @@
         (act_grads[3] * gate_sig * (1.0 - gate_sig)).astype(jnp.bfloat16),
     ]
     grad_down = jnp.concatenate(
-        [inner_rows(mixes[sources[index]], grad_hidden_low[index]) for index in range(4)], axis=1
+        [inner_rows(grad_hidden_low[index], mixes[sources[index]]) for index in range(4)], axis=0
     )
     rep_grads = [
         outer_back(
@@ -742,24 +1446,47 @@
     )
     choose = ((lax.iota(jnp.int32, stride) == sequence_id) & is_first).astype(jnp.float32)
     state_part = choose[:, None, None, None] * grad_state_in[None]
-    summed = lax.psum(
-        (
-            grad_shift,
-            jnp.stack([grad_gain_one, grad_gain_two]),
-            jnp.stack([grad_bias_one, grad_bias_two]),
-            grad_down,
-            grad_up,
-            grad_headgain,
-            grad_headbias,
-            reward_loss_slope,
-            grad_decay,
-            grad_project,
-            grad_output,
-            state_part,
-        ),
-        "seq",
-    )
-    summed = (*summed[:11], grad_ffnkey, grad_ffnvalue, summed[11])
+    small = (
+        grad_shift,
+        grad_down,
+        grad_up,
+        grad_headgain,
+        grad_headbias,
+        reward_loss_slope,
+        grad_decay,
+        state_part,
+        jnp.stack([grad_gain_one, grad_gain_two, grad_bias_one, grad_bias_two]),
+    )
+    half_rows = EMBED_SIZE // 2
+    square_parts = square_grads.reshape(4, 2, half_rows, width)
+    square_parts = jnp.pad(square_parts, ((0, pairs - 4), (0, 0), (0, 0), (0, 0)))
+    total_size = sum(item.size for item in small)
+    padding = -total_size % (16 * pairs * width)
+    packed = jnp.concatenate([item.reshape(-1) for item in small] + [jnp.zeros((padding,), F32)])
+    packed = packed.reshape(pairs, 2, -1, width)
+    moved_ffnkey = DECAY_KEEP * feedforward_address_velocity + grad_ffnkey
+    moved_ffnvalue = DECAY_KEEP * feedforward_content_velocity + grad_ffnvalue
+    which_wide = pair % 2
+    part_index = (pair // 2) * 2 + core
+    gram_part = gram_rows(which_wide, part_index, pairs, moved_ffnkey, moved_ffnvalue)
+    own_part, gram_part = reduce_and_sum(
+        jnp.concatenate([square_parts, packed], axis=2), gram_part, 3
+    )
+    own_velocity = jnp.concatenate([readin_velocity, emission_velocity.T[None]], axis=0)
+    own_velocity = lax.dynamic_slice(
+        own_velocity, (jnp.minimum(pair, 3), core * half_rows, 0), (1, half_rows, width)
+    )
+    own_square = own_part[:half_rows] + DECAY_KEEP * own_velocity[0]
+    packed, whole_square, wide_gram = share_gather(own_square, own_part[half_rows:], gram_part, 5)
+    wide_gram = wide_gram.reshape(EMBED_SIZE, EMBED_SIZE)
+    moved_squares = to_all_pairs(after(own_square, whole_square), pairs)[:4]
+    moved_squares = pair_whole(moved_squares, core).swapaxes(0, 1).reshape(4, EMBED_SIZE, width)
+    packed = packed.reshape(-1)
+    unpacked, place_in = [], 0
+    for item in small:
+        unpacked.append(packed[place_in : place_in + item.size].reshape(item.shape))
+        place_in += item.size
+    state_total, norm_gains = unpacked[7:]
     learnable_tensors = (
         lagged_blend_coeffs,
         standardize_scales,
@@ -790,63 +1517,68 @@
         feedforward_address_velocity,
         feedforward_content_velocity,
     )
+    sink_moved = DECAY_KEEP * narrowing_velocity.T + unpacked[1]
     moved_rows = [
-        DECAY_KEEP * velocity + grad for velocity, grad in zip(velocity_collection, summed[:13])
+        DECAY_KEEP * lagged_blend_velocity + unpacked[0],
+        DECAY_KEEP * standardize_scale_velocity + norm_gains[:2],
+        DECAY_KEEP * standardize_offset_velocity + norm_gains[2:],
+        sink_moved.T,
     ]
+    moved_rows += [
+        DECAY_KEEP * velocity + grad for velocity, grad in zip(velocity_collection[4:9], unpacked[2:7])
+    ]
+    moved_rows += [moved_squares[:3], moved_squares[3].T, moved_ffnkey, moved_ffnvalue]
     next_values = list(learnable_tensors)
     for index in (0, 1, 2, 5, 6, 7, 8):
         next_values[index] = vector_step(learnable_tensors[index], moved_rows[index])
-    square_stack = jnp.stack(
-        [moved_rows[9][0], moved_rows[9][1], moved_rows[9][2], moved_rows[10].T]
-    )
-    wide_stack = jnp.stack([moved_rows[11], moved_rows[12].T])
-    own_square = lax.dynamic_index_in_dim(square_stack, seq_index % 4, 0, keepdims=False)
-    own_wide = lax.dynamic_index_in_dim(wide_stack, seq_index % 2, 0, keepdims=False)
     lift_moved = moved_rows[4]
-    sink_moved = moved_rows[3].T
     total_rank = lift_moved.shape[0]
-    wide_gram, lift_gram = lax.psum(
-        (close(own_wide, own_wide.T), exact(lift_moved, lift_moved.T)), "head"
-    )
-    whole_square = lax.all_gather(own_square, "head", axis=1, tiled=True)
-    square_scale = 1.0 / (jnp.sqrt(jnp.sum(whole_square * whole_square)) + 1e-07)
-    whole_square = newton_whole(whole_square * square_scale)
-    wide_scale = 1.0 / (jnp.sqrt(jnp.trace(wide_gram)) + 1e-07)
-    wide_done = newton_grams(
-        own_wide * wide_scale,
-        wide_gram * (wide_scale * wide_scale),
-        lambda gram: jnp.trace(gram) / gram.shape[0],
-        (cheap, cheap, close, close, close),
-        (cheap, cheap, cheap, close, close),
-    )
+    rank_pad = -total_rank % 128
     group = jnp.stack(
         [(lax.iota(jnp.int32, total_rank) >= edge).astype(jnp.int32) for edge in sequence_edges[1:4]]
     ).sum(axis=0)
-    member = (group[:, None] == group[None, :]).astype(F32)
-    sizes = jnp.sum(member, axis=1)
-    grams = jnp.stack([lift_gram, exact(sink_moved, sink_moved.T)]) * member
-    eye = jnp.eye(total_rank, dtype=F32)
-    diagonals = jnp.sum(grams * eye, axis=2)
-    scales = 1.0 / (jnp.sqrt(exact(diagonals, member)) + 1e-07)
-    grams = grams * (scales * scales)[:, :, None]
-    shift_of = lambda gram: (exact(jnp.sum(gram * eye, axis=2), member) / sizes)[:, :, None]
-    maps = newton_grams(jnp.broadcast_to(eye, grams.shape), grams, shift_of, [exact] * 5, [exact] * 5)
-    maps = maps * scales[:, :, None]
-    lift_done = exact(maps[0], lift_moved)
-    sink_done = exact(maps[1], sink_moved)
+    member = jnp.pad((group[:, None] == group[None, :]).astype(F32), ((0, rank_pad), (0, rank_pad)))
+    rank_gram = jnp.pad(exact(lift_moved, lift_moved.T), ((0, rank_pad), (0, rank_pad)))
+    lift_gram = lax.psum(rank_gram, "head")
+    result_sum = lax.psum(after(product(activated, values_low), lift_gram), "head")
+    block_output = ((attended + result_sum) * live).astype(jnp.bfloat16)
+    sink_gram = jnp.pad(exact(sink_moved, sink_moved.T), ((0, rank_pad), (0, rank_pad)))
+    rank_gram = jnp.where(core == 0, lift_gram, sink_gram)[None]
+    wide_role = jnp.where((core == 1) & (pair < 4), 1 + which_wide, 0)
+    wide_done = newton_wide(wide_role, wide_gram, moved_ffnkey, moved_ffnvalue)
+    square_done = newton_square((core == 0) & (pair < 4), after(whole_square, wide_done))
+    maps = newton_small(core >= 0, after(rank_gram, square_done, moved_squares, result_sum), member)
+    square_done, maps, wide_done = lax.optimization_barrier((square_done, maps, wide_done))
+    maps = pair_whole(maps[0], core)[:, :total_rank, :total_rank]
+    lift_done = close(maps[0], lift_moved)
+    sink_done = close(maps[1], sink_moved)
     head_index = lax.axis_index("head")
-    square_width = own_square.shape[1]
-    square_done = lax.dynamic_slice_in_dim(whole_square, head_index * square_width, square_width, 1)
+    square_done = lax.dynamic_slice_in_dim(square_done, head_index * width, width, 1)
     share = EMBED_SIZE // seq_count
     start_row = seq_index * share
-
-    def shared_rows(done):
-        return lax.all_to_all(
-            done.reshape(seq_count, share, done.shape[1]), "seq", 0, 0, tiled=True
-        )
-
-    square_rows = shared_rows(square_done)
-    wide_rows = shared_rows(wide_done)
+    square_rows = lax.all_to_all(
+        square_done.reshape(seq_count, share, width), "seq", 0, 0, tiled=True
+    )[0:8:2]
+    group_size = seq_count // 2
+    wide_shares = wide_done.reshape(seq_count, share, hidden_units)
+    rounds = []
+    for step in range(group_size):
+        chosen = jnp.where(pair % 2 == 0, step, (step + group_size // 2) % group_size)
+        sent = lax.dynamic_index_in_dim(
+            wide_shares, (pair // 2) * group_size + chosen, 0, keepdims=False
+        )
+        routes = []
+        for half in range(2):
+            origin = (1, 3) if half == 0 else (5, 7)
+            routes.append((origin[0], half * group_size + step))
+            routes.append((origin[1], half * group_size + (step + group_size // 2) % group_size))
+        rounds.append(lax.ppermute(sent, "seq", routes))
+    rounds = jnp.stack(rounds)
+    in_group = seq_index % group_size
+    wide_rows = [
+        lax.dynamic_index_in_dim(rounds, in_group, 0, keepdims=False),
+        lax.dynamic_index_in_dim(rounds, (in_group + group_size // 2) % group_size, 0, keepdims=False),
+    ]
     rows_of = lambda item, axis: lax.dynamic_slice_in_dim(item, start_row, share, axis)
     next_values[9] = rows_of(readin_maps, 1) - ORTHO_STEP_RATE * square_rows[:3]
     next_values[10] = rows_of(emission_coeffs, 1) - ORTHO_STEP_RATE * square_rows[3].T
@@ -868,7 +1600,7 @@
         block_output,
         tokens_grad,
         grad_first,
-        summed[13],
+        state_total,
         next_values[0],
         next_values[1],
         next_values[2],

time: 1100 us -> 725 us (0.66)
  waiting for transfers between devices: 425 us -> 53 us
  Pallas kernels: 28.1 us -> 371 us
  matrix products: 355 us -> 41.8 us
  blocking collectives: 44.4 us -> 0 us
  between operations: 51.9 us -> 17.1 us
  starting transfers between devices: 37.1 us -> 65.5 us
  local copies, waits for them, and re-layouts: 59.9 us -> 80.6 us
    pallas_call x0 -> x9, Pallas kernels: none -> 343 us  [the longest x3 137 us: line_sum(): pl.pallas_call(functools.partial(line_sum_kernel, count, pieces), out_sha...]
    psum x5 -> x3, waiting for transfers between devices: 380 us -> 47.4 us  [the longest x1 47.4 us: on_device(): lax.psum(after(product(activated, values_low), lift_gram), 'head')]
    dot_general x16 -> x2, matrix products: 162 us -> 2.28 us  [close(): jnp.dot(left, right, precision=lax.Precision.HIGH, preferred_element_type...]
    dot_general x15 -> x0, matrix products: 107 us -> none  [cheap(): jnp.dot(left.astype(BF), right.astype(BF), preferred_element_type=F32)]
    dot_general x28 -> x2, matrix products: 53.7 us -> 2.69 us  [exact(): jnp.matmul(left, right, precision=HIGHEST, preferred_element_type=F32)]
    psum x2 -> x0, blocking collectives: 44.4 us -> none  [the longest x1 24.8 us: on_device(): lax.psum((grad_shift, jnp.stack([grad_gain_one, grad_gain_two]), jnp.stac...]
    all_to_all x2, waiting for transfers between devices: 29.6 us -> 0.01 us  [the longest x1 0.01 us: across_pairs(): lax.all_to_all(value, 'seq', 0, 0, tiled=True, axis_index_groups=groups)]
    ppermute x0 -> x6, starting transfers between devices: none -> 21.6 us  [the longest x2 15.9 us: pair_swap(): lax.ppermute(value, 'seq', [(index, index ^ 1) for index in range(count)])]
  transfers between devices with their start and end apart: 22 -> 25, of which waited for: 16 -> 5; matrix products, arithmetic and copies ran while one was open for 41% -> 20% of each run, Pallas kernels for 0% -> 29%
where the time goes in v2:
time: 725 us; the launch traced here: 713 us
  Pallas kernels  371 us (51%)
  other arithmetic  84.3 us (12%)
  local copies, waits for them, and re-layouts  80.6 us (11%)
  starting transfers between devices  65.5 us (9%)
  waiting for transfers between devices  53 us (7%)
  matrix products  41.8 us (6%)
  between operations  17.1 us (2%)
    pallas_call x3, Pallas kernels, line_sum(): pl.pallas_call(functools.partial(line_sum_kernel, count, pieces), out_sha...  137 us
    pallas_call x2, Pallas kernels, newton_call(): pl.pallas_call(body, out_shape=jax.ShapeDtypeStruct(result_shape, F32), i...  85.7 us
    pallas_call x1, Pallas kernels, share_gather(): pl.pallas_call(functools.partial(share_gather_kernel, pairs, count, piece...  52.2 us
    pallas_call x1, Pallas kernels, reduce_and_sum(): pl.pallas_call(functools.partial(reduce_and_sum_kernel, pairs, count, pie...  50.4 us
    psum x1, waiting for transfers between devices, on_device(): lax.psum(after(product(activated, values_low), lift_gram), 'head')  47.4 us
    unnamed x372, local copies, waits for them, and re-layouts  31.6 us
    ppermute x14, starting transfers between devices, passed_along(): lax.ppermute(value, axis, [(source, source + steps) for source in range(f...  28.9 us
    pallas_call x4, Pallas kernels, local_call(): pl.pallas_call(functools.partial(body, heads), out_shape=tuple((jax.Shape...  28.1 us
  transfers between devices with their start and end apart: 25, of which 5 were waited for; matrix products, arithmetic and copies ran while one was open for 20% of the time, Pallas kernels for 29%

profile of v2, /device:TPU:0, one launch (start us, length us, event | category | flops | bytes accessed | tf_op | source)
XLA Modules:
  0.0 713.1 jit_solution(5280839325791362488)
XLA Ops:
  12.8 4.8 collective-permute-start
  23.3 3.3 convert_element_type.148
  28.2 2.5 copy.95
  36.6 13.4 %shard_map.526 = (f32[128,256]{1,0:T(8,128)S(1)}, f32[4,128,256]{2,1,0:T(8,128)S(1)}, f32[256,256]{1,0:T(8,128)S(1)}, f32[256,256]{1,0:T(8,128)S(1)}, f32[256,25...) custom-call(f32[256,256]{1,0:T(8,128)S(1)} %fusion.31.rec_ref, ...), custom_call_target="tpu_custom_call" | custom-call | tf_op jit(solution)/shard_map/pallas_call | solution.py:412
  50.8 3.5 collective-permute-start.3
  54.4 1.9 collective-permute-start.2
  62.6 2.0 shard_map.527
  68.0 44.3 %shard_map.528 = f32[256,1024]{1,0:T(8,128)} custom-call(f32[256,1024]{1,0:T(8,128)} %fusion.42.refs_0_), custom_call_target="tpu_custom_call" | custom-call | tf_op jit(solution)/shard_map/pallas_call | solution.py:825
  114.5 4.9 collective-permute-start.4
  126.7 2.8 fusion.110
  129.5 2.9 fusion.47
  132.3 43.3 %shard_map.529 = f32[256,1024]{1,0:T(8,128)} custom-call(f32[256,1024]{1,0:T(8,128)} %fusion.21.refs_0_), custom_call_target="tpu_custom_call" | custom-call | tf_op jit(solution)/shard_map/pallas_call | solution.py:825
  180.0 3.9 fusion.19
  183.9 2.3 slice.364
  186.4 3.8 multiply_reduce_fusion
  192.8 2.0 shard_map.530
  202.9 4.5 collective-permute-done.11
  207.6 10.6 %shard_map.531 = (f32[64,256]{1,0:T(8,128)S(1)}, bf16[256,256]{1,0:T(8,128)(2,1)S(1)}, bf16[256,256]{1,0:T(8,128)(2,1)S(1)}, bf16[256,256]{1,0:T(8,128)(2,1)S(1)...) custom-call(f32[3,64,256]{2,1,0:T(8,128)S(1)} %pad_maximum_fusion.3., ...), custom_call_target="tpu_custom_call" | custom-call | tf_op jit(solution)/shard_map/pallas_call | solution.py:412
  234.7 3.5 multiply_reduce_fusion.8
  238.4 2.5 concatenate.47.refs_0_
  240.9 49.1 %shard_map.532 = f32[256,1408]{1,0:T(8,128)} custom-call(f32[256,1408]{1,0:T(8,128)} %concatenate.47.refs_0_), custom_call_target="tpu_custom_call" | custom-call | tf_op jit(solution)/shard_map/pallas_call | solution.py:825
  297.3 2.3 multiply_add_fusion.2
  306.8 3.7 fusion.16
  311.2 2.4 constant_dynamic-update-slice_fusion.6
  324.5 4.1 pad_maximum_fusion.parts_ref
  328.7 10.4 %multiply_add_fusion = (f32[1024,1024]{1,0:T(8,128)}, f32[1024,1024]{1,0:T(8,128)S(1)}) fusion(f32[1024,1024]{1,0:T(8,128)} %get-tuple-element.220, f32[1024,1024]{1,0:T(8,128)} %param.61, f32[1024,1024]{1,0:T(8,128)} %get-tuple-element.219, f32[1024,1024]{1,0:T(8,128)} %param.60), kind=kLoop, calls=%fused_computation.4 | loop fusion | flops 4194304 | bytes 25165824 | tf_op jit(solution)/shard_map/add | solution.py:1468
  339.1 5.7 shard_map.533.line_ref
  344.8 50.4 %shard_map.534 = (f32[720,256]{1,0:T(8,128)S(1)}, f32[256,1024]{1,0:T(8,128)S(1)}) custom-call(f32[4,2,720,256]{3,2,1,0:T(8,128)} %pad_maximum_fusion.parts_ref, f32[256,1024]{1,0:T(8,128)S(1)} %shard_map.533.line_ref), custom_call_target="tpu_custom_call" | custom-call | tf_op jit(solution)/shard_map/pallas_call | solution.py:903
  395.4 52.2 %shard_map.535 = (f32[4,2,208,256]{3,2,1,0:T(8,128)S(1)}, f32[4,2,512,256]{3,2,1,0:T(8,128)}, f32[4,256,1024]{2,1,0:T(8,128)}) custom-call(f32[512,256]{1,0:T(8,128)S(1)} %fusion.28.square_ref, f32[208,256]{1,0:T(8,128)S(1)} %slice.324.small_ref, f32[256,1024]{1,0:T(8,128)S(1)} %get-tuple-element.104.gram_ref), custom_call_target="tpu_custom_call" | custom-call | tf_op jit(solution)/shard_map/pallas_call | solution.py:1073
  451.6 2.1 copy.111
  458.4 7.2 %shard_map.536 = f32[1024,1024]{1,0:T(8,128)} custom-call(s32[1]{0:T(128)} %bitcast.66.active_ref, f32[1024,1024]{1,0:T(8,128)} %bitcast.303, f32[1024,1024]{1,0:T(8,128)} %copy-done.2, f32[1024,1024]{1,0:T(8,128)} %get-tuple-element.304.value_ref), custom_call_target="tpu_custom_call" | custom-call | flops 64424509440 | bytes 8388608 | tf_op jit(solution)/shard_map/pallas_call | solution.py:617
  470.1 4.6 all-to-all-start.1
  475.4 78.6 %shard_map.537 = f32[1024,1024]{1,0:T(8,128)} custom-call(s32[1]{0:T(128)} %bitcast.65.active_ref, f32[4,2,512,256]{3,2,1,0:T(8,128)} %get-tuple-element.110.x_ref), custom_call_target="tpu_custom_call" | custom-call | flops 64424509440 | bytes 8388608 | tf_op jit(solution)/shard_map/pallas_call | solution.py:617
  566.6 2.1 fusion.94
  570.0 14.0 %collective-permute-start.19 = (f32[4,512,256]{1,2,0:T(8,128)}, f32[4,512,256]{1,2,0:T(8,128)}, u32[]{:S(2)}, u32[]{:S(2)}) collective-permute-start(f32[4,512,256]{1,2,0:T(8,128)} %all-to-all-done.1), channel_id=1, source_target_pairs={{0,4},{4,0},{8,12},{12,8},{16,20},{20,16},{24,28},{28,24},{1,5},{5... | collective-permute-start | bytes 6291464 | tf_op jit(solution)/shard_map/ppermute | solution.py:1129
  584.1 47.4 %all-reduce.10.cloned.1.call-done = f32[256,1024]{1,0:T(8,128)} async-done(((f32[256,1024]{1,0:T(8,128)}), f32[256,1024]{1,0:T(8,128)}) %all-reduce.10.cloned.1.call-update) | async-done | bytes 1048592 | tf_op jit(solution)/shard_map/psum | solution.py:1543
  631.4 12.0 %shard_map.538 = f32[1,384,384]{2,1,0:T(8,128)S(1)} custom-call(s32[1]{0:T(128)} %bitcast.68.active_ref, f32[1,384,384]{2,1,0:T(8,128)S(1)} %select_bitcast_fusion.3.gram_ref, f32[384,384]{1,0:T(8,128)S(1)} %pad_convert_fusion.member_ref), custom_call_target="tpu_custom_call" | custom-call | flops 11324620800 | tf_op jit(solution)/shard_map/pallas_call | solution.py:694
  650.6 2.3 constant_dynamic-slice_fusion.2
  652.9 10.3 %all-to-all-start = ((f32[8,128,256]{2,1,0:T(8,128)}), f32[8,128,256]{2,1,0:T(8,128)}, u32[]{:S(2)}, u32[]{:S(2)}) async-start(f32[8,128,256]{2,1,0:T(8,128)} %bitcast.235), calls=%async_computation | async-start | bytes 2097152 | tf_op jit(solution)/shard_map/all_to_all | solution.py:1559
  663.3 3.4 add_add_fusion.2
  666.7 1.9 collective-permute-start.14
  672.3 1.9 bitcast_subtract_fusion.1
  674.2 2.0 bitcast_subtract_fusion
  685.6 3.0 select_bitcast_fusion
  690.1 2.2 copy.99
  692.3 3.8 maximum_bitcast_fusion
  696.1 3.0 slice.393
  699.1 5.8 copy.100
  (603 shorter events, 145.3 us)
Async XLA Ops:
  7.2 321.4 %all-reduce.12.cloned.1.call-start = ((), (), s32[]{:S(2)}) async-start(), calls=%async_computation.4 | async-start | bytes 16777216 | tf_op jit(solution)/shard_map/psum | solution.py:1301
  8.1 106.1 %copy-start.117 = (f32[1,1024]{1,0:T(1,128)}, f32[1,1024]{1,0:T(1,128)S(1)}, u32[]{:S(2)}) copy-start(f32[1,1024]{1,0:T(1,128)S(1)} %get-tuple-element.294) | copy-start | bytes 12292
  8.9 23.1 %copy-start.105 = (f32[1,1024]{1,0:T(1,128)}, f32[1,1024]{1,0:T(1,128)S(1)}, u32[]{:S(2)}) copy-start(f32[1,1024]{1,0:T(1,128)S(1)} %get-tuple-element.293) | copy-start | bytes 12292
  8.9 105.3 %copy-start.111 = (f32[1,1024]{1,0:T(1,128)}, f32[1,1024]{1,0:T(1,128)S(1)}, u32[]{:S(2)}) copy-start(f32[1,1024]{1,0:T(1,128)S(1)} %get-tuple-element.292) | copy-start | bytes 12292
  10.1 21.9 %copy-start.113 = (f32[256]{0:T(256)}, f32[256]{0:T(256)S(1)}, u32[]{:S(2)}) copy-start(f32[256]{0:T(256)S(1)} %broadcast_multiply_fusion.3) | copy-start | bytes 3076
  11.4 20.6 %copy-start.120 = (f32[256]{0:T(256)}, f32[256]{0:T(256)S(1)}, u32[]{:S(2)}) copy-start(f32[256]{0:T(256)S(1)} %fusion.90) | copy-start | bytes 3076
  12.8 18.7 %collective-permute-start = (f32[1,1024]{1,0:T(1,128)S(1)}, f32[1,1024]{1,0:T(1,128)S(1)}, u32[]{:S(2)}, u32[]{:S(2)}) collective-permute-start(f32[1,1024]{1,0:T(1,128)S(1)} %slice.349), channel_id=1, source_target_pairs={{0,8},{4,12},{8,16},{12,20},{16,24},{20,28},{1,9},{5,13},{9,17},{1... | collective-permute-start | bytes 12296 | tf_op jit(solution)/shard_map/ppermute | solution.py:34
  32.0 28.3 %copy-start.90 = (bf16[256,1024]{1,0:T(8,128)(2,1)}, bf16[256,1024]{1,0:T(8,128)(2,1)S(1)}, u32[]{:S(2)}) copy-start(bf16[256,1024]{1,0:T(8,128)(2,1)S(1)} %get-tuple-element.242) | copy-start | bytes 1572868
  35.3 14.7 %copy-start.108 = (bf16[256,32]{0,1:T(8,128)(2,1)}, bf16[256,32]{0,1:T(8,128)(2,1)S(1)}, u32[]{:S(2)}) copy-start(bf16[256,32]{0,1:T(8,128)(2,1)S(1)} %convolution_convert_fusion.1) | copy-start | bytes 49156
  35.9 24.3 %copy-start.103 = (bf16[256,64]{0,1:T(8,128)(2,1)}, bf16[256,64]{0,1:T(8,128)(2,1)S(1)}, u32[]{:S(2)}) copy-start(bf16[256,64]{0,1:T(8,128)(2,1)S(1)} %convolution_convert_fusion) | copy-start | bytes 98308
  50.8 141.9 %copy-start.3 = (f32[4,128,256]{2,1,0:T(8,128)}, f32[4,128,256]{2,1,0:T(8,128)S(1)}, u32[]{:S(2)}) copy-start(f32[4,128,256]{2,1,0:T(8,128)S(1)} %get-tuple-element.74.blocks_ref) | copy-start | bytes 1572868
  50.8 9.9 %collective-permute-start.3 = (f32[128,256]{1,0:T(8,128)S(1)}, f32[128,256]{1,0:T(8,128)S(1)}, u32[]{:S(2)}, u32[]{:S(2)}) collective-permute-start(f32[128,256]{1,0:T(8,128)S(1)} %get-tuple-element.73), channel_id=1, source_target_pairs={{0,8},{4,12},{8,16},{12,20},{16,24},{20,28},{1,9},{5,13},{9,17},{1... | collective-permute-start | bytes 393224 | tf_op jit(solution)/shard_map/ppermute | solution.py:34
  54.4 8.1 %collective-permute-start.2 = (f32[128,256]{1,0:T(8,128)S(1)}, f32[128,256]{1,0:T(8,128)S(1)}, u32[]{:S(2)}, u32[]{:S(2)}) collective-permute-start(f32[128,256]{1,0:T(8,128)S(1)} %get-tuple-element.73), channel_id=1, source_target_pairs={{0,16},{4,20},{8,24},{12,28},{1,17},{5,21},{9,25},{13,29},{2,18},{... | collective-permute-start | bytes 393224 | tf_op jit(solution)/shard_map/ppermute | solution.py:34
  56.4 6.1 collective-permute-start.1
  57.7 61.7 %collective-permute-start.7 = (f32[64,256]{1,0:T(8,128)S(1)}, f32[64,256]{1,0:T(8,128)}, u32[]{:S(2)}, u32[]{:S(2)}) collective-permute-start(f32[64,256]{1,0:T(8,128)S(1)} %slice.301), channel_id=1, source_target_pairs={{24,0},{28,4},{25,1},{29,5},{26,2},{30,6},{27,3},{31,7}} | collective-permute-start | bytes 196616 | tf_op jit(solution)/shard_map/ppermute | solution.py:34
  59.0 60.4 %collective-permute-start.6 = (f32[64,256]{1,0:T(8,128)S(1)}, f32[64,256]{1,0:T(8,128)}, u32[]{:S(2)}, u32[]{:S(2)}) collective-permute-start(f32[64,256]{1,0:T(8,128)S(1)} %slice.301), channel_id=1, source_target_pairs={{16,0},{20,4},{24,8},{28,12},{17,1},{21,5},{25,9},{29,13},{18,2},{... | collective-permute-start | bytes 196616 | tf_op jit(solution)/shard_map/ppermute | solution.py:34
  60.8 58.6 %collective-permute-start.5 = (f32[64,256]{1,0:T(8,128)S(1)}, f32[64,256]{1,0:T(8,128)}, u32[]{:S(2)}, u32[]{:S(2)}) collective-permute-start(f32[64,256]{1,0:T(8,128)S(1)} %slice.301), channel_id=1, source_target_pairs={{8,0},{12,4},{16,8},{20,12},{24,16},{28,20},{9,1},{13,5},{17,9},{2... | collective-permute-start | bytes 196616 | tf_op jit(solution)/shard_map/ppermute | solution.py:34
  114.5 6.2 collective-permute-start.4
  178.7 7.7 %collective-permute-start.8 = (f32[1,1024]{1,0:T(1,128)}, f32[1,1024]{1,0:T(1,128)}, u32[]{:S(2)}, u32[]{:S(2)}) collective-permute-start(f32[1,1024]{1,0:T(1,128)} %broadcast_select_fusion.3), channel_id=1, source_target_pairs={{8,0},{12,4},{16,8},{20,12},{24,16},{28,20},{9,1},{13,5},{17,9},{2... | collective-permute-start | bytes 12296 | tf_op jit(solution)/shard_map/ppermute | solution.py:34
  186.3 379.1 %all-reduce.8.cloned.1.call-start = ((), (), s32[]{:S(2)}) async-start(), calls=%async_computation.2 | async-start | bytes 1179648 | tf_op jit(solution)/shard_map/psum | solution.py:1542
  194.9 12.5 %collective-permute-start.11 = (f32[64,256]{1,0:T(8,128)S(1)}, f32[64,256]{1,0:T(8,128)S(1)}, u32[]{:S(2)}, u32[]{:S(2)}) collective-permute-start(f32[64,256]{1,0:T(8,128)S(1)} %get-tuple-element.80), channel_id=1, source_target_pairs={{24,0},{28,4},{25,1},{29,5},{26,2},{30,6},{27,3},{31,7}} | collective-permute-start | bytes 196616 | tf_op jit(solution)/shard_map/ppermute | solution.py:34
  196.5 11.0 %collective-permute-start.10 = (f32[64,256]{1,0:T(8,128)S(1)}, f32[64,256]{1,0:T(8,128)S(1)}, u32[]{:S(2)}, u32[]{:S(2)}) collective-permute-start(f32[64,256]{1,0:T(8,128)S(1)} %get-tuple-element.80), channel_id=1, source_target_pairs={{16,0},{20,4},{24,8},{28,12},{17,1},{21,5},{25,9},{29,13},{18,2},{... | collective-permute-start | bytes 196616 | tf_op jit(solution)/shard_map/ppermute | solution.py:34
  198.0 9.5 %collective-permute-start.9 = (f32[64,256]{1,0:T(8,128)S(1)}, f32[64,256]{1,0:T(8,128)S(1)}, u32[]{:S(2)}, u32[]{:S(2)}) collective-permute-start(f32[64,256]{1,0:T(8,128)S(1)} %get-tuple-element.80), channel_id=1, source_target_pairs={{8,0},{12,4},{16,8},{20,12},{24,16},{28,20},{9,1},{13,5},{17,9},{2... | collective-permute-start | bytes 196616 | tf_op jit(solution)/shard_map/ppermute | solution.py:34
  228.4 6.2 collective-permute-start.12
  299.7 6.8 collective-permute-start.13
  344.7 50.5 %copy-start.80 = (f32[256,1024]{0,1:T(8,128)S(1)}, f32[256,1024]{0,1:T(8,128)}, u32[]{:S(2)}) copy-start(f32[256,1024]{0,1:T(8,128)} %copy.95) | copy-start | bytes 3145732
  344.8 50.5 %copy-start.86 = (f32[3,1024,256]{2,1,0:T(8,128)S(1)}, f32[3,1024,256]{2,1,0:T(8,128)}, u32[]{:S(2)}) copy-start(f32[3,1024,256]{2,1,0:T(8,128)} %param.58) | copy-start | bytes 9437188
  457.3 17.4 %copy-start.140 = (f32[2,1024]{1,0:T(2,128)}, f32[2,1024]{1,0:T(2,128)S(1)}, u32[]{:S(2)}) copy-start(f32[2,1024]{1,0:T(2,128)S(1)} %get-tuple-element.260) | copy-start | bytes 24580
  465.6 88.3 %copy-start.150 = (f32[3,256]{1,0:T(4,128)}, f32[3,256]{1,0:T(4,128)S(1)}, u32[]{:S(2)}) copy-start(f32[3,256]{1,0:T(4,128)S(1)} %get-tuple-element.258) | copy-start | bytes 9220
  465.7 88.9 %copy-start.149 = (f32[3,256]{1,0:T(4,128)}, f32[3,256]{1,0:T(4,128)S(1)}, u32[]{:S(2)}) copy-start(f32[3,256]{1,0:T(4,128)S(1)} %get-tuple-element.226) | copy-start | bytes 9220
  467.7 87.4 %copy-start.170 = (f32[256]{0:T(256)}, f32[256]{0:T(256)S(1)}, u32[]{:S(2)}) copy-start(f32[256]{0:T(256)S(1)} %get-tuple-element.256) | copy-start | bytes 3076
  470.1 100.0 %all-to-all-start.1 = ((f32[4,512,256]{1,2,0:T(8,128)}), f32[4,512,256]{1,2,0:T(8,128)}, u32[]{:S(2)}, u32[]{:S(2)}) async-start(f32[4,512,256]{1,2,0:T(8,128)} %broadcast_in_dim.41), calls=%async_computation.1 | async-start | bytes 4194304 | tf_op jit(solution)/shard_map/all_to_all | solution.py:1147
  474.7 156.7 %all-reduce.10.cloned.1.call-start = ((), (), s32[]{:S(2)}) async-start(), calls=%async_computation.3 | async-start | bytes 2097152 | tf_op jit(solution)/shard_map/psum | solution.py:1543
  475.4 87.3 %copy-start.138 = (f32[2,1024]{1,0:T(2,128)S(1)}, f32[2,1024]{1,0:T(2,128)}, u32[]{:S(2)}) copy-start(f32[2,1024]{1,0:T(2,128)} %param.38) | copy-start | bytes 24580
  475.4 91.3 %copy-start.72 = (f32[1024,288]{0,1:T(8,128)S(1)}, f32[1024,288]{0,1:T(8,128)}, u32[]{:S(2)}) copy-start(f32[1024,288]{0,1:T(8,128)} %param.52) | copy-start | bytes 3538948
  570.0 115.6 %collective-permute-start.19 = (f32[4,512,256]{1,2,0:T(8,128)}, f32[4,512,256]{1,2,0:T(8,128)}, u32[]{:S(2)}, u32[]{:S(2)}) collective-permute-start(f32[4,512,256]{1,2,0:T(8,128)} %all-to-all-done.1), channel_id=1, source_target_pairs={{0,4},{4,0},{8,12},{12,8},{16,20},{20,16},{24,28},{28,24},{1,5},{5... | collective-permute-start | bytes 6291464 | tf_op jit(solution)/shard_map/ppermute | solution.py:1129
  644.8 21.9 %collective-permute-start.18 = (f32[128,1024]{1,0:T(8,128)}, f32[128,1024]{1,0:T(8,128)}, u32[]{:S(2)}, u32[]{:S(2)}) collective-permute-start(f32[128,1024]{1,0:T(8,128)} %get-tuple-element.247), channel_id=1, source_target_pairs={{4,12},{12,4},{20,28},{28,20},{5,13},{13,5},{21,29},{29,21},{6,14}... | collective-permute-start | bytes 1572872 | tf_op jit(solution)/shard_map/ppermute | solution.py:1575
  646.3 22.3 %collective-permute-start.17 = (f32[128,1024]{1,0:T(8,128)}, f32[128,1024]{1,0:T(8,128)}, u32[]{:S(2)}, u32[]{:S(2)}) collective-permute-start(f32[128,1024]{1,0:T(8,128)} %get-tuple-element.248), channel_id=1, source_target_pairs={{4,8},{12,0},{20,24},{28,16},{5,9},{13,1},{21,25},{29,17},{6,10},{... | collective-permute-start | bytes 1572872 | tf_op jit(solution)/shard_map/ppermute | solution.py:1575
  647.6 21.0 %collective-permute-start.16 = (f32[128,1024]{1,0:T(8,128)}, f32[128,1024]{1,0:T(8,128)}, u32[]{:S(2)}, u32[]{:S(2)}) collective-permute-start(f32[128,1024]{1,0:T(8,128)} %get-tuple-element.249), channel_id=1, source_target_pairs={{4,4},{12,12},{20,20},{28,28},{5,5},{13,13},{21,21},{29,29},{6,6},... | collective-permute-start | bytes 1572872 | tf_op jit(solution)/shard_map/ppermute | solution.py:1575
  649.1 14.1 %copy-start.115 = (f32[256]{0:T(256)S(1)}, f32[256]{0:T(256)}, u32[]{:S(2)}) copy-start(f32[256]{0:T(256)} %copy-done.113) | copy-start | bytes 3076
  649.1 14.1 %copy-start.122 = (f32[256]{0:T(256)S(1)}, f32[256]{0:T(256)}, u32[]{:S(2)}) copy-start(f32[256]{0:T(256)} %copy-done.120) | copy-start | bytes 3076
  649.1 14.1 %copy-start.143 = (f32[256]{0:T(256)S(1)}, f32[256]{0:T(256)}, u32[]{:S(2)}) copy-start(f32[256]{0:T(256)} %compare_convert_fusion) | copy-start | bytes 3076
  649.1 14.1 %copy-start.157 = (f32[256]{0:T(256)S(1)}, f32[256]{0:T(256)}, u32[]{:S(2)}) copy-start(f32[256]{0:T(256)} %copy-done.156) | copy-start | bytes 3076
  649.2 14.1 %copy-start.159 = (f32[256]{0:T(256)S(1)}, f32[256]{0:T(256)}, u32[]{:S(2)}) copy-start(f32[256]{0:T(256)} %copy-done.158) | copy-start | bytes 3076
  649.2 14.1 %copy-start.166 = (f32[256]{0:T(256)S(1)}, f32[256]{0:T(256)}, u32[]{:S(2)}) copy-start(f32[256]{0:T(256)} %negate_multiply_fusion) | copy-start | bytes 3076
  649.2 19.4 %collective-permute-start.15 = (f32[128,1024]{1,0:T(8,128)}, f32[128,1024]{1,0:T(8,128)}, u32[]{:S(2)}, u32[]{:S(2)}) collective-permute-start(f32[128,1024]{1,0:T(8,128)} %get-tuple-element.246), channel_id=1, source_target_pairs={{4,0},{12,8},{20,16},{28,24},{5,1},{13,9},{21,17},{29,25},{6,2},{1... | collective-permute-start | bytes 1572872 | tf_op jit(solution)/shard_map/ppermute | solution.py:1575
  652.9 29.1 %all-to-all-start = ((f32[8,128,256]{2,1,0:T(8,128)}), f32[8,128,256]{2,1,0:T(8,128)}, u32[]{:S(2)}, u32[]{:S(2)}) async-start(f32[8,128,256]{2,1,0:T(8,128)} %bitcast.235), calls=%async_computation | async-start | bytes 2097152 | tf_op jit(solution)/shard_map/all_to_all | solution.py:1559
  666.7 9.6 %collective-permute-start.14 = (f32[384,384]{1,0:T(8,128)S(1)}, f32[384,384]{1,0:T(8,128)}, u32[]{:S(2)}, u32[]{:S(2)}) collective-permute-start(f32[384,384]{1,0:T(8,128)S(1)} %bitcast.221), channel_id=1, source_target_pairs={{0,4},{4,0},{8,12},{12,8},{16,20},{20,16},{24,28},{28,24},{1,5},{5... | collective-permute-start | bytes 1769480 | tf_op jit(solution)/shard_map/ppermute | solution.py:1129
  (156 other events, 856.8 us)
Sparse Core Ops, SparseCore 0:
  186.4 132.3 all-reduce.11
  451.7 38.1 all-reduce.7
  565.5 65.8 all-reduce.9
